TPU v7x, 32 devices: a whole 2x2x4 slice. The times are simulated.
32 devices in a mesh: dp: 8 (over y, x, core), tp: 4 (over z).
Axes of the slice: x: 2, y: 2, z: 4, core: 2. Of those that a mesh axis runs over, the one named last changes fastest.
Arguments:
- tokens: bfloat16 [16384, 768], P('dp'), may hold values from -6 to 6
- segment_ids: int32 [32, 512], P('dp'), may hold values from 0 to 7, never falling along the last dimension, each value on 1 to 256 neighbouring positions
- pair_order: int32 [256], replicated, may hold values from 0 to 255, each once
- w_query: bfloat16 [768, 768], P(None, 'tp'), may hold values from -0.0546875 to 0.0546875
- w_key: bfloat16 [768, 768], P(None, 'tp'), may hold values from -0.21875 to 0.21875
- w_value: bfloat16 [768, 768], P(None, 'tp'), may hold values from -0.21875 to 0.21875
- w_out: bfloat16 [768, 768], P('tp'), may hold values from -0.625 to 0.625
- rel_bias: float32 [32, 12], P(None, 'tp'), may hold values from -4 to 4
- gain_attn: float32 [768], replicated, may hold values from 0.5 to 1.5
- w_hidden: bfloat16 [768, 3072], P(None, 'tp'), may hold values from -0.21875 to 0.21875
- w_down: bfloat16 [3072, 768], P('tp'), may hold values from -0.109375 to 0.109375
- gain_ffn: float32 [768], replicated, may hold values from 0.5 to 1.5
- gain_final: float32 [768], replicated, may hold values from 0.5 to 1.5
- w_project: bfloat16 [768, 768], replicated, may hold values from -0.21875 to 0.21875
Outputs:
- layer_out: bfloat16 [16384, 768], P('dp')
- d_tokens: float32 [16384, 768], P('dp')
- grad_query: float32 [768, 768], P('dp', 'tp')
- grad_key: float32 [768, 768], P('dp', 'tp')
- grad_value: float32 [768, 768], P('dp', 'tp')
- grad_out: float32 [768, 768], P('tp', 'dp')
- grad_rel_bias: float32 [32, 12], P(None, 'tp')
- grad_gain_attn: float32 [768], P('dp')
- grad_hidden: float32 [768, 3072], P('dp', 'tp')
- grad_down: float32 [3072, 768], P('tp', 'dp')
- grad_gain_ffn: float32 [768], P('dp')
- grad_gain_final: float32 [768], P('dp')
- grad_project: float32 [768, 768], P('dp')
Inputs may be any that keep to these rules, and one draw needn't show every extreme that they name: `segment_ids`: within each row the segment numbers never fall, and every number from 0 to 7 appears. `pair_order`: every number appears once.
All inputs are finite; a program needn't handle non-finite values.
Results may differ from a plain program's by a relative error of at most 0.034.
Values may be sent and summed in bfloat16 or wider, within the bound.
No kernel may reach another device: no remote copies, remote signals or barrier semaphores. Data moves between devices by JAX's collectives and lax.ppermute only.
A program may use at most 192 MiB of HBM per device.

v0:
```python
import functools
import math

import jax
import jax.numpy as jnp
import numpy as np
from jax import lax
from jax.experimental import pallas as pl
from jax.experimental.pallas import tpu as pltpu
from jax.sharding import PartitionSpec as P

MAX_DIST = 128
SEG_ROW = 8
TILE = 128
VMEM = 52 * 2**20

epsilon = 1e-06
logit_scale = 50.0
loss_scale = 128.0
masked_value = -1e30
highest = lax.Precision.HIGHEST
f32 = jnp.float32
bf16 = jnp.bfloat16

NN = (((1,), (0,)), ((), ()))
NT = (((1,), (1,)), ((), ()))
TN = (((0,), (0,)), ((), ()))


def dg(a, b, dims):
    return lax.dot_general(a, b, dims, preferred_element_type=f32)


def bucket_of(offsets, bucket_count, distance):
    half_count = bucket_count // 2
    exact_count = half_count // 2
    far_side = np.where(offsets > 0, half_count, 0)
    magnitude = np.abs(offsets)
    logged = (
        np.log(np.maximum(magnitude, exact_count) / exact_count)
        / math.log(distance / exact_count)
        * (half_count - exact_count)
    )
    far_bucket = np.minimum(exact_count + logged.astype(np.int64), half_count - 1)
    return (far_side + np.where(magnitude < exact_count, magnitude, far_bucket)).astype(np.int32)


def cost(flops, moved):
    return pl.CostEstimate(flops=int(flops), bytes_accessed=int(moved), transcendentals=0)


def bias_lanes(bucket_count):
    lanes = np.arange(4 * TILE)
    lanes = np.where(lanes >= 2 * TILE, lanes - 4 * TILE, lanes)
    return np.eye(bucket_count, dtype=np.float32)[bucket_of(-lanes, bucket_count, MAX_DIST)].T


def grad_lanes(bucket_count):
    sub = np.arange(8)[:, None]
    lane = np.arange(4 * TILE)[None, :]
    y = (lane - sub) % (4 * TILE)
    y = np.where(y >= 2 * TILE, y - 4 * TILE, y)
    near = bucket_of(-y, bucket_count, MAX_DIST)
    up = np.full((8, TILE), bucket_of(np.array(MAX_DIST), bucket_count, MAX_DIST))
    down = np.full((8, TILE), bucket_of(np.array(-MAX_DIST), bucket_count, MAX_DIST))
    ids = np.concatenate([near, up, down], 1).reshape(-1)
    return np.eye(bucket_count, dtype=np.float32)[ids]


def bring(place_ref, piece_refs, into, sems):
    slices = piece_refs[0].shape[-2]
    copies = []
    for m, piece in enumerate(piece_refs):
        start = pl.multiple_of(place_ref[m], 16) if slices % 16 == 0 else place_ref[m]
        copy = pltpu.make_async_copy(piece, into.at[:, pl.ds(start, slices), :], sems.at[m])
        copy.start()
        copies.append(copy)
    return copies


def spread_bias(vec_ref, bias_s, heads):
    for h in range(heads):
        wide = jnp.broadcast_to(vec_ref[0, h : h + 1, :], (TILE, 4 * TILE))
        bias_s[h] = pltpu.roll(wide, 0, 1, stride=1, stride_axis=0)


def with_bias(tile, offset, h, bias_s, vec_ref):
    if offset == 0:
        return tile + bias_s[h, :, 0:TILE]
    if offset == 1:
        return tile + bias_s[h, :, 3 * TILE : 4 * TILE]
    if offset == -1:
        return tile + bias_s[h, :, TILE : 2 * TILE]
    lane = 2 * TILE + 1 if offset > 1 else 2 * TILE - 1
    return tile + vec_ref[0, h : h + 1, lane : lane + 1]


def masks(seg):
    hot = lax.broadcasted_iota(jnp.int32, (16, seg.shape[-1]), 0) == seg
    return (
        jnp.where(hot, 0.0, masked_value).astype(bf16),
        jnp.where(hot, 1.0, 0.0).astype(bf16),
    )


def inv_rms(values):
    return lax.rsqrt(jnp.mean(values * values, -1, keepdims=True) + epsilon)


def rounded(value):
    return lax.reduce_precision(value, 8, 7)


def tree(parts):
    while len(parts) > 1:
        parts = [parts[i] + parts[i + 1] for i in range(0, len(parts), 2)]
    return parts[0]


def exact_parts(value):
    parts = []
    for _ in range(3):
        part = value.astype(bf16)
        parts.append(part)
        value = value - part.astype(f32)
    return parts


PAD = 16


def pack_kernel(at_ref, q_ref, k_ref, v_ref, o_ref, rel_ref, out_ref, mine_ref, pack_s):
    cols = q_ref.shape[1]
    for at, ref in enumerate((q_ref, k_ref, v_ref)):
        pack_s[at * cols : (at + 1) * cols] = ref[...].astype(f32).T
    pack_s[3 * cols :] = o_ref[...].astype(f32)
    out_ref[...] = pack_s[...].astype(bf16)
    slices = mine_ref.shape[0] - PAD
    start = at_ref[0] * slices
    if slices % 8 == 0:
        start = pl.multiple_of(start, 8)
    mine_ref[:slices] = pack_s[pl.ds(start, slices), :].astype(bf16)
    mine_ref[slices:] = jnp.zeros_like(mine_ref[slices:])
    buckets, heads = rel_ref.shape
    lane = 0
    for at in range(0, buckets, PAD):
        for part in exact_parts(rel_ref[at : at + PAD]):
            mine_ref[slices:, lane : lane + heads] = part
            lane += TILE


def pack_weights(at, w_query, w_key, w_value, w_out, rel_bias, share):
    width, cols = w_query.shape
    slices = width // share
    full = lambda shape: pl.BlockSpec(shape, lambda i, at: (0, 0))
    return pl.pallas_call(
        pack_kernel,
        grid_spec=pltpu.PrefetchScalarGridSpec(
            num_scalar_prefetch=1,
            grid=(1,),
            in_specs=[full((width, cols))] * 3 + [full((cols, width)), full(rel_bias.shape)],
            out_specs=[full((width, width)), full((slices + PAD, width))],
            scratch_shapes=[pltpu.VMEM((width, width), f32)],
        ),
        out_shape=[
            jax.ShapeDtypeStruct((width, width), bf16),
            jax.ShapeDtypeStruct((slices + PAD, width), bf16),
        ],
        compiler_params=pltpu.CompilerParams(vmem_limit_bytes=VMEM),
        cost_estimate=cost(10**9, 2**20),
        name="pack_weights",
    )(at, w_query, w_key, w_value, w_out, rel_bias)


def unpack_table(pads, buckets, heads):
    rows = []
    lane = 0
    for _ in range(0, buckets, PAD):
        parts = [
            pads[:, :, lane + p * TILE : lane + p * TILE + heads].astype(f32) for p in range(3)
        ]
        rows.append(parts[0] + parts[1] + parts[2])
        lane += 3 * TILE
    return jnp.concatenate(rows, 1)


def stack_kernel(*refs):
    ins, outs = refs[:3], refs[3:]
    slices = outs[0].shape[1]
    for at, ref in enumerate(ins):
        outs[0][at] = ref[:slices]
        if len(outs) == 2:
            outs[1][at] = ref[slices:]


def stack(arrays, slices):
    rows, width = arrays[0].shape
    shapes = [(3, slices, width)] + ([(3, rows - slices, width)] if rows > slices else [])
    return pl.pallas_call(
        stack_kernel,
        out_shape=[jax.ShapeDtypeStruct(shape, bf16) for shape in shapes],
        cost_estimate=cost(0, 12 * arrays[0].size),
        name="stack",
    )(*arrays)


def others_kernel(order_ref, all_ref, *outs):
    slices = outs[0].shape[1]
    for k in range(1, all_ref.shape[0]):
        for at, out in enumerate(outs):
            out[k - 1] = all_ref[order_ref[k], at * slices : (at + 1) * slices]


def others_of(order, everything, count):
    n, total, width = everything.shape
    slices = total // count
    shape = (n - 1, slices, width)
    return pl.pallas_call(
        others_kernel,
        grid_spec=pltpu.PrefetchScalarGridSpec(
            num_scalar_prefetch=1,
            grid=(1,),
            in_specs=[pl.BlockSpec((n, total, width), lambda i, p: (0, 0, 0))],
            out_specs=[pl.BlockSpec(shape, lambda i, p: (0, 0, 0))] * count,
        ),
        out_shape=[jax.ShapeDtypeStruct(shape, bf16)] * count,
        cost_estimate=cost(0, 4 * everything.size),
        name="others_of",
    )(order, everything)


def attend_row(heads, hd, weights, a1_ref, vec_ref, seg_ref, qkv_ref, lse_ref, ctx_ref, bias_s):
    length = a1_ref.shape[0]
    blocks = length // TILE

    @pl.when(pl.program_id(1) == 0)
    def _():
        spread_bias(vec_ref, bias_s, heads)

    qkv_ref[0, 0] = dg(weights, a1_ref[...], NT).astype(bf16)
    q_mask, k_mask = masks(seg_ref[0])
    ones = jnp.ones((16, length), bf16)
    for h in range(heads):
        q_t = jnp.concatenate([qkv_ref[0, 0, h * hd : (h + 1) * hd], q_mask], 0)
        k_t = jnp.concatenate([qkv_ref[0, 0, (heads + h) * hd : (heads + h + 1) * hd], k_mask], 0)
        v_t = jnp.concatenate(
            [qkv_ref[0, 0, (2 * heads + h) * hd : (2 * heads + h + 1) * hd], ones], 0
        )
        scores = dg(k_t.T, q_t, NN)
        columns = []
        tops = []
        for i in range(blocks):
            tiles = [
                with_bias(
                    scores[j * TILE : (j + 1) * TILE, i * TILE : (i + 1) * TILE],
                    j - i,
                    h,
                    bias_s,
                    vec_ref,
                )
                for j in range(blocks)
            ]
            top = jnp.max(functools.reduce(jnp.maximum, tiles), 0, keepdims=True)
            tops.append(top)
            columns.append(jnp.concatenate([jnp.exp(t - top).astype(bf16) for t in tiles], 0))
        mixed = dg(v_t, jnp.concatenate(columns, 1), NN)
        total = mixed[hd : hd + 1]
        lse_ref[0, 0, h : h + 1, :] = jnp.concatenate(tops, 1) + jnp.log(total)
        ctx_ref[0, 0, h * hd : (h + 1) * hd, :] = (mixed[:hd] / total).astype(bf16)


def attn_own_kernel(heads, hd, a1_ref, vec_ref, seg_ref, w_ref, *rest):
    attend_row(heads, hd, w_ref[: 3 * heads * hd], a1_ref, vec_ref, seg_ref, *rest)


def attn_far_kernel(heads, hd, count, place_ref, a1_ref, vec_ref, seg_ref, own_ref, *rest):
    pieces = rest[:count]
    qkv_ref, lse_ref, ctx_ref, sorted_ref, bias_s, w_s, sems, out_sems = rest[count + 3 :]
    s, r = pl.program_id(0), pl.program_id(1)
    keep = [
        pltpu.make_async_copy(own_ref, sorted_ref.at[0], out_sems.at[0]),
        pltpu.make_async_copy(w_s, sorted_ref.at[pl.ds(1, w_s.shape[0])], out_sems.at[1]),
    ]

    @pl.when((s == 0) & (r == 0))
    def _():
        for copy in bring(place_ref, pieces, w_s, sems):
            copy.wait()
        for copy in keep:
            copy.start()

    attend_row(
        heads,
        hd,
        w_s[s, : 3 * heads * hd],
        a1_ref,
        vec_ref,
        seg_ref,
        qkv_ref,
        lse_ref,
        ctx_ref,
        bias_s,
    )

    @pl.when((s == pl.num_programs(0) - 1) & (r == pl.num_programs(1) - 1))
    def _():
        for copy in keep:
            copy.wait()


def attention(a1, own_a, vecs, segs, slots, place=None, pieces=None, earlier=None):
    rows, _, length = segs.shape
    width = a1.shape[1]
    heads = vecs.shape[1]
    hd = width // (4 * heads)
    cols = heads * hd
    first = slots - vecs.shape[0] if pieces else 0
    count = slots - 1 if pieces else 1
    anywhere = pl.BlockSpec(memory_space=pl.ANY)
    in_specs = [
        pl.BlockSpec((length, width), lambda s, r, *_: (r, 0)),
        pl.BlockSpec((1, heads, 4 * TILE), lambda s, r, *_: (s + (1 if pieces else 0), 0, 0)),
        pl.BlockSpec((1, 1, length), lambda s, r, *_: (r, 0, 0)),
    ]
    at = 1 if pieces else 0
    out_specs = [
        pl.BlockSpec((1, 1, 3 * cols, length), lambda s, r, *_: (s + at, r, 0, 0)),
        pl.BlockSpec((1, 1, heads, length), lambda s, r, *_: (s + at, r, 0, 0)),
        pl.BlockSpec((1, 1, cols, length), lambda s, r, *_: (s + at, r, 0, 0)),
    ]
    out_shape = [
        jax.ShapeDtypeStruct((slots, rows, 3 * cols, length), bf16),
        jax.ShapeDtypeStruct((slots, rows, heads, length), f32),
        jax.ShapeDtypeStruct((slots, rows, cols, length), bf16),
    ]
    scratch = [pltpu.VMEM((heads, TILE, 4 * TILE), f32)]
    steps = count * rows
    common = dict(
        compiler_params=pltpu.CompilerParams(vmem_limit_bytes=VMEM),
        cost_estimate=cost(steps * 2.5 * 10**9, 2**20),
    )
    if not pieces:
        return pl.pallas_call(
            functools.partial(attn_own_kernel, heads, hd),
            grid=(count, rows),
            in_specs=in_specs + [pl.BlockSpec((width, width), lambda s, r: (0, 0))],
            out_specs=out_specs,
            out_shape=out_shape,
            scratch_shapes=scratch,
            name="attn_own",
            **common,
        )(a1, vecs, segs, own_a)
    n = len(pieces)
    return pl.pallas_call(
        functools.partial(attn_far_kernel, heads, hd, n),
        grid_spec=pltpu.PrefetchScalarGridSpec(
            num_scalar_prefetch=1,
            grid=(count, rows),
            in_specs=in_specs
            + [pl.BlockSpec((width, width), lambda s, r, p: (0, 0))]
            + [anywhere] * (n + 3),
            out_specs=out_specs + [anywhere],
            scratch_shapes=scratch
            + [
                pltpu.VMEM((count, width, width), bf16),
                pltpu.SemaphoreType.DMA((n,)),
                pltpu.SemaphoreType.DMA((2,)),
            ],
        ),
        out_shape=out_shape + [jax.ShapeDtypeStruct((slots, width, width), bf16)],
        input_output_aliases={5 + n: 0, 6 + n: 1, 7 + n: 2},
        name="attn_far",
        **common,
    )(place, a1, vecs, segs, own_a, *pieces, *earlier)


GELU_A = math.sqrt(2.0 / math.pi)
GELU_B = 0.044715


def gelu(v):
    t = jnp.tanh(v * (GELU_A + (GELU_A * GELU_B) * (v * v)))
    half = 0.5 * v
    return half + half * t


def gelu_pair(v):
    square = v * v
    t = jnp.tanh(v * (GELU_A + (GELU_A * GELU_B) * square))
    half = 0.5 * v
    inner = GELU_A + (3.0 * GELU_A * GELU_B) * square
    return half + half * t, 0.5 + 0.5 * t + half * (1.0 - t * t) * inner


def ffn_own_kernel(x_ref, ctx_ref, wo_ref, gain_ref, b_ref, c_ref, mid_ref, a2_ref, part_ref):
    slots, _, cols, length = ctx_ref.shape
    attn = dg(
        ctx_ref[...].reshape(slots * cols, length),
        wo_ref[...].reshape(slots * cols, wo_ref.shape[-1]),
        TN,
    )
    mid = (x_ref[...].astype(f32) + attn).astype(bf16)
    mid_ref[...] = mid
    mid = mid.astype(f32)
    a2 = (mid * inv_rms(mid) * gain_ref[...]).astype(bf16)
    a2_ref[...] = a2
    hidden = gelu(dg(a2, b_ref[...], NN)).astype(bf16)
    part_ref[...] = dg(hidden, c_ref[...], NN).astype(bf16)


def ffn_own(x, ctx, sorted_a, gain, own_b, own_c):
    slots, rows, cols, length = ctx.shape
    tokens, width = x.shape
    units = own_b.shape[1]
    by_row = pl.BlockSpec((length, width), lambda r: (r, 0))
    return pl.pallas_call(
        ffn_own_kernel,
        grid=(rows,),
        in_specs=[
            by_row,
            pl.BlockSpec((slots, 1, cols, length), lambda r: (0, r, 0, 0)),
            pl.BlockSpec((slots, cols, width), lambda r: (0, 3, 0)),
            pl.BlockSpec((1, width), lambda r: (0, 0)),
            pl.BlockSpec((width, units), lambda r: (0, 0)),
            pl.BlockSpec((units, width), lambda r: (0, 0)),
        ],
        out_specs=[by_row] * 3,
        out_shape=[jax.ShapeDtypeStruct((tokens, width), bf16)] * 3,
        compiler_params=pltpu.CompilerParams(vmem_limit_bytes=VMEM),
        cost_estimate=cost(tokens * width * 6 * units, 2**24),
        name="ffn_own",
    )(x, ctx, sorted_a, gain, own_b, own_c)


def ffn_row(a2, mid, part, up, down, gain_ref, seg_ref, out_ref, res_ref, pool_ref, wait=None):
    res = mid.astype(f32) + part.astype(f32)
    for k in range(len(up)):
        if wait is not None:
            wait(k)
        hidden = gelu(dg(a2, up[k][...], NN)).astype(bf16)
        res = res + dg(hidden, down[k][...], NN)
    res_ref[...] = res.astype(bf16)
    final = (res * inv_rms(res) * gain_ref[...]).astype(bf16)
    out_ref[...] = final
    if pool_ref is not None:
        seg = seg_ref[0]
        hot = lax.broadcasted_iota(jnp.int32, (SEG_ROW, seg.shape[-1]), 0) == seg
        member = jnp.where(hot, 1.0, 0.0)
        pool_ref[...] = dg(member.astype(bf16), final, NN) / jnp.sum(member, 1, keepdims=True)


def ffn_first_kernel(
    count, place_ref, order_ref, a2_ref, mid_ref, part_ref, gain_ref, seg_ref, *rest
):
    pieces, far_c = rest[:count], rest[count]
    out_ref, res_ref, pool_ref, sb_ref, sc_ref, b_s, c_s, sems, out_sems = rest[count + 1 :]
    others = b_s.shape[0]
    slices = far_c.shape[2]
    copies = []
    for k in range(others):
        here = []
        for m in range(count):
            start = pl.multiple_of(place_ref[m], 16) if slices % 16 == 0 else place_ref[m]
            into = b_s.at[k, pl.ds(start, slices), :]
            here.append(pltpu.make_async_copy(pieces[m].at[k], into, sems.at[0, k, m]))
            into = c_s.at[k, pl.ds(m * slices, slices), :]
            here.append(pltpu.make_async_copy(far_c.at[m, k], into, sems.at[1, k, m]))
        copies.append(here)
    keep = []
    for k in range(others):
        keep.append(pltpu.make_async_copy(b_s.at[k], sb_ref.at[k], out_sems.at[0, k]))
        keep.append(pltpu.make_async_copy(c_s.at[k], sc_ref.at[k], out_sems.at[1, k]))
    for here in copies:
        for copy in here:
            copy.start()

    def wait(k):
        for copy in copies[k]:
            copy.wait()
        keep[2 * k].start()
        keep[2 * k + 1].start()

    ffn_row(
        a2_ref[...],
        mid_ref[...],
        part_ref[...],
        [b_s.at[k] for k in range(others)],
        [c_s.at[k] for k in range(others)],
        gain_ref,
        seg_ref,
        out_ref,
        res_ref,
        pool_ref,
        wait,
    )
    for copy in keep:
        copy.wait()


def ffn_first(place, order, a2, mid, part, gain, segs, pieces, far_c):
    rows, _, length = segs.shape
    tokens, width = a2.shape
    units = pieces[0].shape[-1]
    others = pieces[0].shape[0]
    n = len(pieces)
    first = pl.BlockSpec((length, width), lambda r, p, o: (o[0], 0))
    anywhere = pl.BlockSpec(memory_space=pl.ANY)
    return pl.pallas_call(
        functools.partial(ffn_first_kernel, n),
        grid_spec=pltpu.PrefetchScalarGridSpec(
            num_scalar_prefetch=2,
            grid=(1,),
            in_specs=[
                first,
                first,
                first,
                pl.BlockSpec((1, width), lambda r, p, o: (0, 0)),
                pl.BlockSpec((1, 1, length), lambda r, p, o: (o[0], 0, 0)),
            ]
            + [anywhere] * (n + 1),
            out_specs=[
                first,
                first,
                pl.BlockSpec((SEG_ROW, width), lambda r, p, o: (0, 0)),
                anywhere,
                anywhere,
            ],
            scratch_shapes=[
                pltpu.VMEM((others, width, units), bf16),
                pltpu.VMEM((others, units, width), bf16),
                pltpu.SemaphoreType.DMA((2, others, n)),
                pltpu.SemaphoreType.DMA((2, others)),
            ],
        ),
        out_shape=[
            jax.ShapeDtypeStruct((tokens, width), bf16),
            jax.ShapeDtypeStruct((tokens, width), bf16),
            jax.ShapeDtypeStruct((SEG_ROW, width), f32),
            jax.ShapeDtypeStruct((others, width, units), bf16),
            jax.ShapeDtypeStruct((others, units, width), bf16),
        ],
        compiler_params=pltpu.CompilerParams(vmem_limit_bytes=VMEM),
        cost_estimate=cost(length * width * 4 * units * others, 2**24),
        name="ffn_first",
    )(place, order, a2, mid, part, gain, segs, *pieces, far_c)


def ffn_rest_kernel(
    order_ref, a2_ref, mid_ref, part_ref, gain_ref, b_ref, c_ref, _out, _res, out_ref, res_ref
):
    others = b_ref.shape[0]
    ffn_row(
        a2_ref[...],
        mid_ref[...],
        part_ref[...],
        [b_ref.at[k] for k in range(others)],
        [c_ref.at[k] for k in range(others)],
        gain_ref,
        None,
        out_ref,
        res_ref,
        None,
    )


def ffn_rest(order, a2, mid, part, gain, sorted_b, sorted_c, out, res, rows):
    tokens, width = a2.shape
    length = tokens // rows
    slots, _, units = sorted_b.shape
    row = pl.BlockSpec((length, width), lambda r, o: (o[r + 1], 0))
    whole = pl.BlockSpec(sorted_b.shape, lambda r, o: (0, 0, 0))
    anywhere = pl.BlockSpec(memory_space=pl.ANY)
    return pl.pallas_call(
        ffn_rest_kernel,
        grid_spec=pltpu.PrefetchScalarGridSpec(
            num_scalar_prefetch=1,
            grid=(rows - 1,),
            in_specs=[row, row, row, pl.BlockSpec((1, width), lambda r, o: (0, 0)), whole, whole]
            + [anywhere] * 2,
            out_specs=[row, row],
        ),
        out_shape=[jax.ShapeDtypeStruct((tokens, width), bf16)] * 2,
        input_output_aliases={7: 0, 8: 1},
        compiler_params=pltpu.CompilerParams(vmem_limit_bytes=VMEM),
        cost_estimate=cost(tokens * width * 3 * units * slots, 2**24),
        name="ffn_rest",
    )(order, a2, mid, part, gain, sorted_b, sorted_c, out, res)


def loss_math(pooled, project, pair_col, pair_row, gain):
    slots = pooled.shape[0]
    projected = dg(pooled, project, NN)
    inv_norm = lax.rsqrt(jnp.sum(projected * projected, -1, keepdims=True) + epsilon)
    unit = projected * inv_norm
    embedded = unit.astype(bf16)
    similar = logit_scale * dg(embedded, embedded, NT)
    rows = lax.broadcasted_iota(jnp.int32, (slots, slots), 0)
    columns = lax.broadcasted_iota(jnp.int32, (slots, slots), 1)
    same = rows == columns
    similar = jnp.where(same, masked_value, similar)
    partner = jnp.where((pair_col == pair_row) & jnp.logical_not(same), 2.0, 0.0)

    def total(axis):
        top = jnp.max(similar, axis, keepdims=True)
        return top + jnp.log(jnp.sum(jnp.exp(similar - top), axis, keepdims=True))

    both = jnp.exp(similar - total(1)) + jnp.exp(similar - total(0)) - partner
    high = both.astype(bf16)
    low = (both - high.astype(f32)).astype(bf16)
    d_unit = (loss_scale * logit_scale) * (dg(high, embedded, NN) + dg(low, embedded, NN))
    d_proj = inv_norm * (d_unit - unit * jnp.sum(d_unit * unit, -1, keepdims=True))
    d_proj = d_proj.astype(bf16)
    d_pooled = dg(d_proj, project, NT)
    d_gain = jnp.sum(d_pooled * pooled.astype(f32), 0, keepdims=True) / gain
    return d_proj, d_pooled, d_gain


def loss_kernel(count, at_ref, *refs):
    pieces, rest = refs[:count], refs[count:]
    project_ref, pc_ref, pr_ref, gain_ref, dpool_ref, dproj_ref, dgain_ref, a_s, b_s = rest
    each = SEG_ROW
    parts = pieces[0].shape[0] // each
    for m, piece in enumerate(pieces):
        value = piece[...].astype(f32)
        for part in range(parts):
            start = pl.multiple_of(at_ref[1 + m * parts + part] * each, each)
            a_s[pl.ds(start, each), :] = value[part * each : (part + 1) * each]
    pooled = a_s[...].astype(bf16)
    d_proj, d_pooled, d_gain = loss_math(
        pooled, project_ref[...], pc_ref[...], pr_ref[...], gain_ref[...]
    )
    a_s[...] = d_pooled
    b_s[...] = dg(pooled, d_proj, TN)
    here = dpool_ref.shape[0]
    block = dproj_ref.shape[0]
    dpool_ref[...] = a_s[pl.ds(pl.multiple_of(at_ref[0] * here, here), here), :]
    dproj_ref[...] = b_s[pl.ds(pl.multiple_of(at_ref[0] * block, block), block), :]
    dgain_ref[...] = d_gain


def loss_head(at, pieces, project, pairs, gain, here, block):
    slots = sum(piece.shape[0] for piece in pieces)
    width = project.shape[0]
    pair_col = pairs[:, None]
    pair_row = pairs[None, :]
    if len(pieces) == 1:
        pooled = pieces[0]
        d_proj, d_pooled, d_gain = loss_math(pooled, project, pair_col, pair_row, gain)
        own_cols = lax.dynamic_slice_in_dim(pooled, at[0] * block, block, 1)
        d_pooled = lax.dynamic_slice_in_dim(d_pooled, at[0] * here, here, 0)
        return d_pooled, dg(own_cols, d_proj, TN), d_gain
    full = lambda shape: pl.BlockSpec(shape, lambda i, at: (0, 0))
    return pl.pallas_call(
        functools.partial(loss_kernel, len(pieces)),
        grid_spec=pltpu.PrefetchScalarGridSpec(
            num_scalar_prefetch=1,
            grid=(1,),
            in_specs=[full(piece.shape) for piece in pieces]
            + [
                full(project.shape),
                full((slots, 1)),
                full((1, slots)),
                full((1, width)),
            ],
            out_specs=[full((here, width)), full((block, width)), full((1, width))],
            scratch_shapes=[pltpu.VMEM((slots, width), f32), pltpu.VMEM((width, width), f32)],
        ),
        out_shape=[
            jax.ShapeDtypeStruct((here, width), f32),
            jax.ShapeDtypeStruct((block, width), f32),
            jax.ShapeDtypeStruct((1, width), f32),
        ],
        compiler_params=pltpu.CompilerParams(vmem_limit_bytes=VMEM),
        cost_estimate=cost(3 * 10**9, 2**20),
        name="loss_head",
    )(at, *pieces, project, pair_col, pair_row, gain)


def d_result_of(res, seg, d_pool, gain):
    hot = lax.broadcasted_iota(jnp.int32, (SEG_ROW, seg.shape[-1]), 0) == seg
    member = jnp.where(hot, 1.0, 0.0)
    per_token = d_pool / jnp.sum(member, 1, keepdims=True)
    high = per_token.astype(bf16)
    low = (per_token - high.astype(f32)).astype(bf16)
    twice = jnp.concatenate([member, member], 0).astype(bf16)
    d_final = dg(twice, jnp.concatenate([high, low], 0), TN)
    scale = inv_rms(res)
    unit = res * scale
    weighted = d_final * gain
    return scale * (weighted - unit * jnp.mean(weighted * unit, -1, keepdims=True))


def ffn_back_kernel(
    row_ref,
    res_ref,
    mid_ref,
    a2_ref,
    seg_ref,
    dpool_ref,
    gain_end_ref,
    gain_ref,
    own_b_ref,
    own_c_ref,
    b_ref,
    c_ref,
    wo_ref,
    dmid_ref,
    dattn_ref,
    dctx_ref,
    dgain_ref,
    dres_s,
    low_s,
    sum_s,
):
    k = pl.program_id(0)

    @pl.when(k == 0)
    def _():
        d_res = d_result_of(
            res_ref[...].astype(f32), seg_ref[0], dpool_ref[...], gain_end_ref[...]
        )
        dres_s[...] = d_res
        low_s[...] = d_res.astype(bf16)
        sum_s[...] = jnp.zeros_like(sum_s)

    def add(up, down):
        slope = gelu_pair(dg(a2_ref[...], up, NN))[1]
        d_pre = (dg(low_s[...], down, NT) * slope).astype(bf16)
        sum_s[...] += dg(d_pre, up, NT)

    @pl.when(k == 0)
    def _():
        add(own_b_ref[...], own_c_ref[...])

    @pl.when(k > 0)
    def _():
        add(b_ref[0], c_ref[0])

    @pl.when(k == pl.num_programs(0) - 1)
    def _():
        mid = mid_ref[...].astype(f32)
        scale = inv_rms(mid)
        unit = mid * scale
        grad = sum_s[...]
        weighted = grad * gain_ref[...]
        d_mid = dres_s[...] + scale * (weighted - unit * jnp.mean(weighted * unit, -1, keepdims=True))
        dgain_ref[...] = jnp.sum(grad * unit, 0, keepdims=True)
        dmid_ref[...] = d_mid
        low = d_mid.astype(bf16)
        dattn_ref[...] = low
        for s in range(wo_ref.shape[0]):
            dctx_ref[s] = dg(wo_ref[s], low, NT).astype(bf16)


def ffn_back(
    row, res, mid, a2, segs, d_pool, gain_end, gain, sorted_a, own_b, own_c, sorted_b, sorted_c
):
    rows, _, length = segs.shape
    tokens, width = res.shape
    slots = sorted_a.shape[0]
    units = sorted_b.shape[-1]
    cols = width // 4
    own = pl.BlockSpec((length, width), lambda k, row: (row[0], 0))
    fixed = lambda k, row: (0, 0)
    return pl.pallas_call(
        ffn_back_kernel,
        grid_spec=pltpu.PrefetchScalarGridSpec(
            num_scalar_prefetch=1,
            grid=(slots,),
            in_specs=[
                own,
                own,
                own,
                pl.BlockSpec((1, 1, length), lambda k, row: (row[0], 0, 0)),
                pl.BlockSpec((SEG_ROW, width), lambda k, row: (row[0], 0)),
                pl.BlockSpec((1, width), fixed),
                pl.BlockSpec((1, width), fixed),
                pl.BlockSpec((width, units), fixed),
                pl.BlockSpec((units, width), fixed),
                pl.BlockSpec((1, width, units), lambda k, row: (jnp.maximum(k - 1, 0), 0, 0)),
                pl.BlockSpec((1, units, width), lambda k, row: (jnp.maximum(k - 1, 0), 0, 0)),
                pl.BlockSpec((slots, cols, width), lambda k, row: (0, 3, 0)),
            ],
            out_specs=[
                pl.BlockSpec((length, width), fixed),
                pl.BlockSpec((length, width), fixed),
                pl.BlockSpec((slots, cols, length), lambda k, row: (0, 0, 0)),
                pl.BlockSpec((1, width), fixed),
            ],
            scratch_shapes=[
                pltpu.VMEM((length, width), f32),
                pltpu.VMEM((length, width), bf16),
                pltpu.VMEM((length, width), f32),
            ],
        ),
        out_shape=[
            jax.ShapeDtypeStruct((length, width), f32),
            jax.ShapeDtypeStruct((length, width), bf16),
            jax.ShapeDtypeStruct((slots, cols, length), bf16),
            jax.ShapeDtypeStruct((1, width), f32),
        ],
        compiler_params=pltpu.CompilerParams(vmem_limit_bytes=VMEM),
        cost_estimate=cost(1.2 * 10**10, 2**24),
        name="ffn_back",
    )(row, res, mid, a2, segs, d_pool, gain_end, gain, own_b, own_c, sorted_b, sorted_c, sorted_a)


def fold(tile):
    lanes = tile.shape[1]
    total = tile[0:8]
    for b in range(1, TILE // 8):
        total = total + pltpu.roll(tile[8 * b : 8 * b + 8], lanes - 8 * b, 1)
    return total


def attn_back_kernel(
    heads,
    hd,
    row_ref,
    qkv_ref,
    lse_ref,
    ctx_ref,
    dctx_ref,
    vec_ref,
    seg_ref,
    w_ref,
    x_ref,
    dmid_ref,
    gain_ref,
    dqkv_ref,
    fold_ref,
    dtok_ref,
    dgain_ref,
    bias_s,
    sum_s,
):
    slot = pl.program_id(0)
    length = qkv_ref.shape[-1]
    blocks = length // TILE
    spread_bias(vec_ref, bias_s, heads)
    q_mask, k_mask = masks(seg_ref[0])
    for h in range(heads):
        q_low = qkv_ref[0, 0, h * hd : (h + 1) * hd]
        k_low = qkv_ref[0, 0, (heads + h) * hd : (heads + h + 1) * hd]
        v_low = qkv_ref[0, 0, (2 * heads + h) * hd : (2 * heads + h + 1) * hd]
        dc = dctx_ref[0, h * hd : (h + 1) * hd]
        c = ctx_ref[0, 0, h * hd : (h + 1) * hd]
        delta = jnp.sum(dc.astype(f32) * c.astype(f32), 0, keepdims=True)
        lse = lse_ref[0, 0, h : h + 1]
        scores = dg(
            jnp.concatenate([k_low, k_mask], 0).T, jnp.concatenate([q_low, q_mask], 0), NN
        )
        d_probs = dg(v_low.T, dc, NN)
        probs_cols = []
        score_cols = []
        near = [None, None, None]
        far = [None, None]
        for i in range(blocks):
            at = slice(i * TILE, (i + 1) * TILE)
            probs = []
            grads = []
            for j in range(blocks):
                to = slice(j * TILE, (j + 1) * TILE)
                tile = with_bias(scores[to, at], j - i, h, bias_s, vec_ref)
                prob = jnp.exp(tile - lse[:, at])
                grad = prob * (d_probs[to, at] - delta[:, at])
                probs.append(prob.astype(bf16))
                grads.append(grad.astype(bf16))
                if abs(j - i) <= 1:
                    old = near[j - i + 1]
                    near[j - i + 1] = grad if old is None else old + grad
                else:
                    old = far[int(j < i)]
                    far[int(j < i)] = grad if old is None else old + grad
            probs_cols.append(jnp.concatenate(probs, 0))
            score_cols.append(jnp.concatenate(grads, 0))
        probs = jnp.concatenate(probs_cols, 1)
        grads = jnp.concatenate(score_cols, 1)
        dqkv_ref[0, h * hd : (h + 1) * hd] = dg(k_low, grads, NN).astype(bf16)
        dqkv_ref[0, (heads + h) * hd : (heads + h + 1) * hd] = dg(q_low, grads, NT).astype(bf16)
        dqkv_ref[0, (2 * heads + h) * hd : (2 * heads + h + 1) * hd] = dg(dc, probs, NT).astype(
            bf16
        )
        band = jnp.concatenate([near[1], near[0], jnp.zeros_like(near[0]), near[2]], 1)
        fold_ref[0, h, :, : 4 * TILE] = fold(band)
        for side in range(2):
            total = far[side][0:8]
            for b in range(1, TILE // 8):
                total = total + far[side][8 * b : 8 * b + 8]
            fold_ref[0, h, :, (4 + side) * TILE : (5 + side) * TILE] = total
    part = dg(dqkv_ref[0], w_ref[0], TN)

    @pl.when(slot == 0)
    def _():
        sum_s[...] = part

    @pl.when(slot > 0)
    def _():
        sum_s[...] += part

    @pl.when(slot == pl.num_programs(0) - 1)
    def _():
        x = x_ref[...].astype(f32)
        scale = inv_rms(x)
        unit = x * scale
        grad = sum_s[...]
        weighted = grad * gain_ref[...]
        d_tok = dmid_ref[...] + scale * (weighted - unit * jnp.mean(weighted * unit, -1, keepdims=True))
        dtok_ref[...] = d_tok.astype(bf16)
        dgain_ref[...] = jnp.sum(grad * unit, 0, keepdims=True)


def attn_back(row, qkv, lse, ctx, d_ctx, vecs, segs, all_a, x, d_mid, gain):
    slots, rows, cols3, length = qkv.shape
    heads = lse.shape[2]
    cols = cols3 // 3
    width = x.shape[1]
    own4 = lambda k, row: (k, row[0], 0, 0)
    slot = lambda k, row: (k, 0, 0)
    fixed = lambda k, row: (0, 0)
    return pl.pallas_call(
        functools.partial(attn_back_kernel, heads, cols // heads),
        grid_spec=pltpu.PrefetchScalarGridSpec(
            num_scalar_prefetch=1,
            grid=(slots,),
            in_specs=[
                pl.BlockSpec((1, 1, cols3, length), own4),
                pl.BlockSpec((1, 1, heads, length), own4),
                pl.BlockSpec((1, 1, cols, length), own4),
                pl.BlockSpec((1, cols, length), slot),
                pl.BlockSpec((1, heads, 4 * TILE), slot),
                pl.BlockSpec((1, 1, length), lambda k, row: (row[0], 0, 0)),
                pl.BlockSpec((1, cols3, width), slot),
                pl.BlockSpec((length, width), lambda k, row: (row[0], 0)),
                pl.BlockSpec((length, width), fixed),
                pl.BlockSpec((1, width), fixed),
            ],
            out_specs=[
                pl.BlockSpec((1, cols3, length), slot),
                pl.BlockSpec((1, heads, 8, 6 * TILE), lambda k, row: (k, 0, 0, 0)),
                pl.BlockSpec((length, width), fixed),
                pl.BlockSpec((1, width), fixed),
            ],
            scratch_shapes=[
                pltpu.VMEM((heads, TILE, 4 * TILE), f32),
                pltpu.VMEM((length, width), f32),
            ],
        ),
        out_shape=[
            jax.ShapeDtypeStruct((slots, cols3, length), bf16),
            jax.ShapeDtypeStruct((slots, heads, 8, 6 * TILE), f32),
            jax.ShapeDtypeStruct((length, width), bf16),
            jax.ShapeDtypeStruct((1, width), f32),
        ],
        compiler_params=pltpu.CompilerParams(vmem_limit_bytes=VMEM),
        cost_estimate=cost(1.5 * 10**10, 2**24),
        name="attn_back",
    )(row, qkv, lse, ctx, d_ctx, vecs, segs, all_a, x, d_mid, gain)


def split_blocks(core, rel_ref, block, pad, extra, values, keep_ref, give_ref, lead):
    for c in range(2):

        @pl.when(core == c)
        def _():
            for chip in range(4):
                for ref, j in ((keep_ref, 2 * chip + c), (give_ref, 2 * chip + 1 - c)):
                    rows = values(j * block, (j + 1) * block)
                    for at, value in enumerate(rows):
                        ref[rel_ref[chip], lead + at, :block] = value
                    if pad:
                        ref[rel_ref[chip], lead, block:] = extra(j)


def attn_weights_kernel(
    block, place_ref, a1_ref, dattn_ref, dqkv_ref, ctx_ref, extra_ref, *rest
):
    outs, (a1_s, dattn_s, sum_s) = rest[:-3], rest[-3:]

    @pl.when(pl.program_id(0) == 0)
    def _():
        a1_s[...] = a1_ref[...].T
        dattn_s[...] = dattn_ref[...].T

    cols3 = dqkv_ref.shape[1]
    sum_s[:, :cols3] = dg(a1_s[...], dqkv_ref[0], NT).astype(bf16)
    sum_s[:, cols3:] = dg(dattn_s[...], ctx_ref[0, 0], NT).astype(bf16)
    if len(outs) == 1:
        outs[0][0] = sum_s[...]
    else:
        split_blocks(
            place_ref[1],
            place_ref.at[pl.ds(2, 4)],
            block,
            True,
            lambda j: extra_ref[0, j],
            lambda a, b: [sum_s[a:b]],
            outs[0],
            outs[1],
            0,
        )


def attn_weights(place, a1, d_attn, d_qkv, ctx, extra, split):
    slots, cols3, length = d_qkv.shape
    cols = ctx.shape[2]
    width = a1.shape[1]
    _, blocks, pad, _ = extra.shape
    block = width // blocks
    if split:
        shape = (4, slots, block + pad, width)
        out_specs = [pl.BlockSpec((4, 1, block + pad, width), lambda k, p: (0, k, 0, 0))] * 2
        out_shape = [jax.ShapeDtypeStruct(shape, bf16)] * 2
    else:
        out_specs = [pl.BlockSpec((1, width, width), lambda k, p: (k, 0, 0))]
        out_shape = [jax.ShapeDtypeStruct((slots, width, width), bf16)]
    return pl.pallas_call(
        functools.partial(attn_weights_kernel, block),
        grid_spec=pltpu.PrefetchScalarGridSpec(
            num_scalar_prefetch=1,
            grid=(slots,),
            in_specs=[
                pl.BlockSpec((length, width), lambda k, p: (p[0], 0)),
                pl.BlockSpec((length, width), lambda k, p: (0, 0)),
                pl.BlockSpec((1, cols3, length), lambda k, p: (k, 0, 0)),
                pl.BlockSpec((1, 1, cols, length), lambda k, p: (k, p[0], 0, 0)),
                pl.BlockSpec((1, blocks, pad, width), lambda k, p: (k, 0, 0, 0)),
            ],
            out_specs=out_specs,
            scratch_shapes=[
                pltpu.VMEM((width, length), bf16),
                pltpu.VMEM((width, length), bf16),
                pltpu.VMEM((width, width), bf16),
            ],
        ),
        out_shape=out_shape,
        compiler_params=pltpu.CompilerParams(vmem_limit_bytes=VMEM),
        cost_estimate=cost(10**6, 10**6),
        name="attn_weights",
    )(place, a1, d_attn, d_qkv, ctx, extra)


def ffn_grads_kernel(
    res_ref, seg_ref, dpool_ref, gain_ref, a2_ref, b_ref, c_ref, low_ref, hid_ref, dpre_ref
):
    d_res = d_result_of(res_ref[...].astype(f32), seg_ref[0], dpool_ref[...], gain_ref[...])
    low = d_res.astype(bf16)
    low_ref[...] = low
    hidden, slope = gelu_pair(dg(a2_ref[...], b_ref[...], NN))
    hid_ref[...] = hidden.astype(bf16)
    dpre_ref[...] = (dg(low, c_ref[...], NT) * slope).astype(bf16)


def ffn_grads(res, segs, d_pool, gain, a2, own_b, own_c):
    rows, _, length = segs.shape
    tokens, width = res.shape
    units = own_b.shape[1]
    by_row = pl.BlockSpec((length, width), lambda r: (r, 0))
    by_unit = pl.BlockSpec((length, units), lambda r: (r, 0))
    return pl.pallas_call(
        ffn_grads_kernel,
        grid=(rows,),
        in_specs=[
            by_row,
            pl.BlockSpec((1, 1, length), lambda r: (r, 0, 0)),
            pl.BlockSpec((SEG_ROW, width), lambda r: (r, 0)),
            pl.BlockSpec((1, width), lambda r: (0, 0)),
            by_row,
            pl.BlockSpec((width, units), lambda r: (0, 0)),
            pl.BlockSpec((units, width), lambda r: (0, 0)),
        ],
        out_specs=[by_row, by_unit, by_unit],
        out_shape=[
            jax.ShapeDtypeStruct((tokens, width), bf16),
            jax.ShapeDtypeStruct((tokens, units), bf16),
            jax.ShapeDtypeStruct((tokens, units), bf16),
        ],
        compiler_params=pltpu.CompilerParams(vmem_limit_bytes=VMEM),
        cost_estimate=cost(8 * 10**9, 2**24),
        name="ffn_grads",
    )(res, segs, d_pool, gain, a2, own_b, own_c)


def ffn_weights_kernel(block, place_ref, low_ref, hid_ref, a2_ref, dpre_ref, *rest):
    outs, (up_s, down_s) = rest[:-2], rest[-2:]
    r = pl.program_id(0)

    @pl.when(r == 0)
    def _():
        up_s[...] = jnp.zeros_like(up_s)
        down_s[...] = jnp.zeros_like(down_s)

    up_s[...] += dg(a2_ref[...], dpre_ref[...], TN)
    down_s[...] += dg(low_ref[...], hid_ref[...], TN)

    @pl.when(r == pl.num_programs(0) - 1)
    def _():
        if len(outs) == 1:
            outs[0][0] = up_s[...].astype(bf16)
            outs[0][1] = down_s[...].astype(bf16)
        else:
            split_blocks(
                place_ref[1],
                place_ref.at[pl.ds(2, 4)],
                block,
                False,
                None,
                lambda a, b: [up_s[a:b].astype(bf16), down_s[a:b].astype(bf16)],
                outs[0],
                outs[1],
                0,
            )


def ffn_weights(place, low, hidden, a2, d_pre, rows, blocks, split):
    tokens, width = low.shape
    length = tokens // rows
    units = hidden.shape[1]
    block = width // blocks
    by_row = pl.BlockSpec((length, width), lambda r, p: (r, 0))
    by_unit = pl.BlockSpec((length, units), lambda r, p: (r, 0))
    shape = (4, 2, block, units) if split else (2, width, units)
    zeros = (0,) * len(shape)
    return pl.pallas_call(
        functools.partial(ffn_weights_kernel, block),
        grid_spec=pltpu.PrefetchScalarGridSpec(
            num_scalar_prefetch=1,
            grid=(rows,),
            in_specs=[by_row, by_unit, by_row, by_unit],
            out_specs=[pl.BlockSpec(shape, lambda r, p: zeros)] * (2 if split else 1),
            scratch_shapes=[pltpu.VMEM((width, units), f32)] * 2,
        ),
        out_shape=[jax.ShapeDtypeStruct(shape, bf16)] * (2 if split else 1),
        compiler_params=pltpu.CompilerParams(vmem_limit_bytes=VMEM),
        cost_estimate=cost(8 * 10**9, 2**24),
        name="ffn_weights",
    )(place, low, hidden, a2, d_pre)


def shards(
    n_dp,
    n_tp,
    tokens,
    segment_ids,
    pair_order,
    w_query,
    w_key,
    w_value,
    w_out,
    rel_bias,
    gain_attn,
    w_hidden,
    w_down,
    gain_ffn,
    gain_final,
    w_project,
):
    rows, length = segment_ids.shape
    bucket_count, heads = rel_bias.shape
    width = tokens.shape[1]
    units = w_hidden.shape[1]
    dp = lax.axis_index("dp")
    tp = lax.axis_index("tp")
    share = math.gcd(n_dp, 8)
    split = n_dp == 8
    mates = [[(i, i ^ m) for i in range(n_dp)] for m in range(share)]
    levels = [[(i, i ^ k) for i in range(n_tp)] for k in range(n_tp)]

    def over_dp(value, m):
        return lax.ppermute(value, "dp", mates[m])

    def over_tp(value, k):
        return lax.ppermute(value, "tp", levels[k])

    slices = width // share
    low_bits = dp % share
    place = (low_bits ^ jnp.arange(share, dtype=jnp.int32)) * slices

    def from_levels(mine):
        return stack([over_tp(mine, k) for k in range(1, n_tp)], slices)

    def from_chips(far):
        return [far] + [over_dp(far, m) for m in range(2, share, 2)]

    def from_cores(pieces):
        both = [(piece, over_dp(piece, 1)) for piece in pieces]
        return [piece for pair in both for piece in pair]

    def after(values, others):
        return lax.optimization_barrier((values, others))[0]

    order = tp ^ jnp.arange(n_tp, dtype=jnp.int32)
    pack_a, mine_a = pack_weights(
        low_bits[None].astype(jnp.int32), w_query, w_key, w_value, w_out, rel_bias, share
    )
    far_a, pads = from_levels(mine_a)
    mine_bc = jnp.concatenate(
        [
            lax.dynamic_slice_in_dim(w, low_bits * slices, slices, 0)
            for w in (w_hidden, w_down)
        ]
    )
    all_bc = lax.all_gather(mine_bc, "tp", axis=0)
    tables = jnp.concatenate([rel_bias[None], unpack_table(pads, bucket_count, heads)])
    vec_own = jnp.einsum("kbh,bn->khn", tables[:1], bias_lanes(bucket_count), precision=highest)
    vecs = jnp.einsum("kbh,bn->khn", tables, bias_lanes(bucket_count), precision=highest)
    segs = segment_ids[:, None, :]
    row = tp[None].astype(jnp.int32)
    one = gain_attn[None]
    two = gain_ffn[None]
    end = gain_final[None]

    x = tokens.astype(f32)
    a1 = (x * inv_rms(x) * one).astype(bf16)
    state = attention(after(a1, far_a), pack_a, vec_own, segs, n_tp)
    far_a = from_chips(far_a)
    far_b, far_c = others_of(after(order, (state, far_a)), all_bc, 2)
    groups = np.arange(n_dp).reshape(-1, share).tolist()
    far_c = lax.all_gather(far_c, "dp", axis=0, axis_index_groups=groups)
    far_a = from_cores(after(far_a, far_b))
    far_b = from_chips(after(far_b, far_a))
    qkv, lse, ctx, sorted_a = attention(a1, pack_a, vecs, segs, n_tp, place, far_a, state)
    far_b = from_cores(after(far_b, lse))
    mid, a2, part = ffn_own(tokens, ctx, sorted_a, two, w_hidden, w_down)
    layer_out, res, pooled, sorted_b, sorted_c = ffn_first(
        place, order, a2, mid, part, end, segs, far_b, far_c
    )
    block = width // n_dp
    here = rows * SEG_ROW
    pooled = pooled.astype(bf16)
    if split:
        pooled = jnp.concatenate([pooled] + [over_tp(pooled, k) for k in range(1, n_tp)])
        pooled = jnp.concatenate([pooled, over_dp(pooled, 1)])
        pooled_all = from_chips(pooled)
        spots = (dp ^ jnp.arange(n_dp))[:, None] * rows + order[None]
        at = jnp.concatenate([dp[None], spots.reshape(-1)]).astype(jnp.int32)
    else:
        pooled = lax.all_gather(pooled, "tp", axis=0, tiled=True)
        pooled_all = [lax.all_gather(pooled, "dp", axis=0, tiled=True)]
        at = dp[None].astype(jnp.int32)
    d_pool, grad_project, d_gain_end = loss_head(
        at, pooled_all, w_project, pair_order // 2, end, here, block
    )
    grad_gain_final = lax.dynamic_slice_in_dim(d_gain_end[0], dp * block, block, 0)
    d_mid, d_attn, d_ctx, d_gain_two = ffn_back(
        row,
        res,
        mid,
        a2,
        segs,
        d_pool,
        end,
        two,
        sorted_a,
        w_hidden,
        w_down,
        sorted_b,
        sorted_c,
    )
    d_qkv, folded, d_tok, d_gain_one = attn_back(
        row, qkv, lse, ctx, d_ctx, vecs, segs, sorted_a, tokens, d_mid, one
    )
    d_tokens = lax.all_gather(d_tok, "tp", axis=0, tiled=True).astype(f32)

    d_rel = jnp.einsum(
        "khn,nb->kbh",
        folded.reshape(n_tp, heads, -1),
        grad_lanes(bucket_count),
        precision=highest,
    )
    gains = jnp.concatenate([d_gain_one, d_gain_two])
    pad = 16
    extra = jnp.zeros((n_tp, n_dp, pad, width), bf16)
    if split:
        small = d_rel.reshape(n_tp, 1, 1, bucket_count * heads).astype(bf16)
        gain_rows = jnp.swapaxes(gains.reshape(2, n_dp, block), 0, 1).astype(bf16)
        extra = jnp.concatenate(
            [
                jnp.broadcast_to(gain_rows[None], (n_tp, n_dp, 2, block)),
                jnp.broadcast_to(small, (n_tp, n_dp, 1, block)),
                jnp.zeros((n_tp, n_dp, pad - 3, block), bf16),
            ],
            2,
        )
        extra = jnp.pad(extra, ((0, 0), (0, 0), (0, 0), (0, width - block)))
    chips = (dp // 2) ^ jnp.arange(4, dtype=jnp.int32)
    spots = jnp.concatenate([row, (dp % 2)[None].astype(jnp.int32), chips])
    parts_a = attn_weights(spots, a1, d_attn, d_qkv, ctx, extra, split)

    def to_core(parts):
        keep, give = parts
        took = over_dp(give, 1)
        return [rounded(keep[c].astype(f32) + took[c].astype(f32)) for c in range(4)]

    def to_chip(pair):
        return [pair[0]] + [over_dp(pair[c].astype(bf16), 2 * c) for c in range(1, 4)]

    def total(parts):
        return tree([part.astype(f32) for part in parts])

    def scatter(parts):
        return lax.psum_scatter(parts[0].astype(f32), "dp", scatter_dimension=1, tiled=True)

    if split:
        pair_a = to_core(parts_a)
        got_a = to_chip(pair_a)
        first = after(order, pair_a)
    else:
        first = after(order, parts_a)
    layer_out, res = ffn_rest(
        first, a2, mid, part, end, sorted_b, sorted_c, layer_out, res, rows
    )
    low, hidden, d_pre = ffn_grads(res, segs, d_pool, end, a2, w_hidden, w_down)
    parts_f = ffn_weights(spots, low, hidden, a2, d_pre, rows, n_dp, split)
    if split:
        got_f = to_chip(to_core(after(parts_f, got_a)))
        own_a, own_f = rounded(total(after(got_a, got_f))), total(got_f)
    else:
        own_a, own_f = rounded(scatter(parts_a)), scatter(parts_f)

    def reduce_tp(value):
        return tree([value[0]] + [over_tp(value[k], k) for k in range(1, n_tp)])

    grad_a = tree(
        [own_a[0].astype(f32)]
        + [over_tp(own_a[k].astype(bf16), k).astype(f32) for k in range(1, n_tp)]
    )
    cols = width // 4
    if split:
        gain_one, gain_two = grad_a[block, :block], grad_a[block + 1, :block]
        d_rel_here = grad_a[block + 2, : bucket_count * heads].reshape(bucket_count, heads)
    else:
        gains = tree([gains] + [over_tp(gains, k) for k in range(1, n_tp)])
        d_rel_here, gains = lax.psum((reduce_tp(d_rel), gains), "dp")
        gain_one, gain_two = lax.dynamic_slice_in_dim(gains, dp * block, block, 1)
    return (
        layer_out,
        d_tokens,
        grad_a[:block, :cols],
        grad_a[:block, cols : 2 * cols],
        grad_a[:block, 2 * cols : 3 * cols],
        grad_a[:block, 3 * cols :].T,
        d_rel_here,
        gain_one,
        own_f[0],
        own_f[1].T,
        gain_two,
        grad_gain_final,
        grad_project,
    )


def solution(mesh):
    placed = (
        P("dp", None),
        P("dp", None),
        P(),
        P(None, "tp"),
        P(None, "tp"),
        P(None, "tp"),
        P("tp", None),
        P(None, "tp"),
        P(),
        P(None, "tp"),
        P("tp", None),
        P(),
        P(),
        P(),
    )
    return jax.shard_map(
        functools.partial(shards, mesh.shape["dp"], mesh.shape["tp"]),
        mesh=mesh,
        in_specs=placed,
        out_specs=(
            P("dp", None),
            P("dp", None),
            P("dp", "tp"),
            P("dp", "tp"),
            P("dp", "tp"),
            P("tp", "dp"),
            P(None, "tp"),
            P("dp"),
            P("dp", "tp"),
            P("tp", "dp"),
            P("dp"),
            P("dp"),
            P("dp", None),
        ),
        check_vma=False,
    )
```

profile of v0, /device:TPU:0, one launch (start us, length us, event | category | flops | bytes accessed | tf_op | source)
XLA Modules:
  0.0 297.5 jit_solution(18441654383295451713)
XLA Ops:
  11.3 3.0 %collective-permute-start = (bf16[112,768]{1,0:T(8,128)(2,1)S(1)}, bf16[112,768]{1,0:T(8,128)(2,1)S(1)}, u32[]{:S(2)}, u32[]{:S(2)}) collective-permute-start(bf16[112,768]{1,0:T(8,128)(2,1)S(1)} %get-tuple-element.72), channel_id=1, source_target_pairs={{0,1},{1,0},{2,3},{3,2},{4,5},{5,4},{6,7},{7,6},{8,9},{9,8},{10,11... | collective-permute-start | bytes 516104 | tf_op jit(solution)/shard_map/ppermute | solution.py:1173
  14.3 2.6 collective-permute-start.1
  18.7 2.7 fusion
  21.5 2.4 fusion.2.a1_ref
  24.6 5.3 %collective-permute-done.1.refs_1_ = bf16[112,768]{1,0:T(8,128)(2,1)S(1)} collective-permute-done((bf16[112,768]{1,0:T(8,128)(2,1)S(1)}, bf16[112,768]{1,0:T(8,128)(2,1)S(1)}, u32[]{:S(2)}, u32[]{:S(2)}) %collective-permute-start.1) | collective-permute-done | bytes 172064 | tf_op jit(solution)/shard_map/ppermute | solution.py:1173
  31.2 1.9 stack.1
  34.6 1.5 collective-permute-start.4
  36.6 11.0 %attn_own.1 = (bf16[4,4,576,512]{3,2,1,0:T(8,128)(2,1)}, f32[4,4,3,512]{3,2,1,0:T(4,128)S(1)}, bf16[4,4,192,512]{3,2,1,0:T(8,128)(2,1)}) custom-call(bf16[2048,768]{1,0:T(8,128)(2,1)} %fusion.2.a1_ref, f32[1,3,512]{2,1,0:T(4,128)S(1)} %convolution_bitcast_fusion.vec_ref, s32[4,1,512]{2,1,0:T(1,128)S(1)} %broadcast_in_dim.54.seg_ref, ...), custom_call_target="tpu_custom_call" | custom-call | flops 10000000000 | bytes 1048576 | tf_op jit(solution)/shard_map/attn_own/pallas_call | solution.py:343
  47.7 5.3 %collective-permute-done.4.rest_4_ = bf16[3,96,768]{2,1,0:T(8,128)(2,1)} collective-permute-done((bf16[3,96,768]{2,1,0:T(8,128)(2,1)}, bf16[3,96,768]{2,1,0:T(8,128)(2,1)}, u32[]{:S(2)}, u32[]{:S(2)}) %collective-permute-start.4) | collective-permute-done | bytes 442400 | tf_op jit(solution)/shard_map/ppermute | solution.py:1170
  52.9 2.9 others_of.1
  63.8 32.4 %attn_far.1 = (bf16[4,4,576,512]{3,2,1,0:T(8,128)(2,1)}, f32[4,4,3,512]{3,2,1,0:T(4,128)S(1)}, bf16[4,4,192,512]{3,2,1,0:T(8,128)(2,1)}, bf16[4,768,768]{2,1,0:T(8,128)(2,1)}) custom-call(s32[8]{0:T(128)S(1)} %xor_multiply_fusion.1.place_ref, bf16[2048,768]{1,0:T(8,128)(2,1)} %fusion.2.a1_ref, ...), custom_call_target="tpu_custom_call", output_to_operand_aliasing={{0}: (13, {}), {1}: (14, {}), {2}: (15, {})} | custom-call | flops 30000001024 | bytes 1048576 | tf_op jit(solution)/shard_map/attn_far/pallas_call | solution.py:354
  97.4 13.6 %ffn_own.1 = (bf16[2048,768]{1,0:T(8,128)(2,1)}, bf16[2048,768]{1,0:T(8,128)(2,1)}, bf16[2048,768]{1,0:T(8,128)(2,1)}) custom-call(bf16[2048,768]{1,0:T(8,128)(2,1)} %x_ref.3, bf16[4,4,192,512]{3,2,1,0:T(8,128)(2,1)} %get-tuple-element.86.ctx_ref, bf16[4,768,768]{2,1,0:T(8,128)(2,1)} %get-tuple-element.87.wo_ref.w_ref, ...), custom_call_target="tpu_custom_call" | custom-call | flops 7247757312 | bytes 16777216 | tf_op jit(solution)/shard_map/ffn_own/pallas_call | solution.py:416
  111.8 11.5 %ffn_first.1 = (bf16[2048,768]{1,0:T(8,128)(2,1)}, bf16[2048,768]{1,0:T(8,128)(2,1)}, f32[8,768]{1,0:T(8,128)S(1)}, bf16[3,768,768]{2,1,0:T(8,128)(2,1)}, bf16[3,768,768]{2,1,0:T(8,128)(2,1)}) custom-call(s32[8]{0:T(128)S(1)} %xor_multiply_fusion.1.place_ref, s32[4]{0:T(128)S(1)} %copy-done.3, bf16[2048,768]{1,0:T(8,128)(2,1)} %get-tuple-element.88.a2_ref, ...), custom_call_target="tpu_custom_call" | custom-call | flops 3623878656 | bytes 16777216 | tf_op jit(solution)/shard_map/ffn_first/pallas_call | solution.py:508
  123.4 4.2 %collective-permute-start.17 = (bf16[8,768]{1,0:T(8,128)(2,1)S(1)}, bf16[8,768]{1,0:T(8,128)(2,1)S(1)}, u32[]{:S(2)}, u32[]{:S(2)}) collective-permute-start(bf16[8,768]{1,0:T(8,128)(2,1)S(1)} %get-tuple-element.186), channel_id=1, source_target_pairs={{0,1},{1,0},{2,3},{3,2},{4,5},{5,4},{6,7},{7,6},{8,9},{9,8},{10,11... | collective-permute-start | bytes 36872 | tf_op jit(solution)/shard_map/ppermute | solution.py:1173
  127.6 2.8 collective-permute-start.18
  132.1 3.7 %collective-permute-done.19 = bf16[8,768]{1,0:T(8,128)(2,1)S(1)} collective-permute-done((bf16[8,768]{1,0:T(8,128)(2,1)S(1)}, bf16[8,768]{1,0:T(8,128)(2,1)S(1)}, u32[]{:S(2)}, u32[]{:S(2)}) %collective-permute-start.19) | collective-permute-done | bytes 12320 | tf_op jit(solution)/shard_map/ppermute | solution.py:1173
  142.0 2.0 collective-permute-done.22.refs_2_
  145.2 3.7 %loss_head.1 = (f32[32,768]{1,0:T(8,128)S(1)}, f32[96,768]{1,0:T(8,128)}, f32[1,768]{1,0:T(1,128)S(1)}) custom-call(s32[33]{0:T(128)S(1)} %pad_add_fusion.1.at_ref, bf16[64,768]{1,0:T(8,128)(2,1)S(1)} %constant_dynamic-update-slice_fusion.refs_0_, bf16[64,768]{1,0:T(8,128)(2,1)S(1)} %collective-permute-done.21.refs_1_, ...), custom_call_target="tpu_custom_call" | custom-call | flops 3000000000 | bytes 1048576 | tf_op jit(solution)/shard_map/loss_head/pallas_call | solution.py:653
  148.9 16.0 %ffn_back.1 = (f32[512,768]{1,0:T(8,128)}, bf16[512,768]{1,0:T(8,128)(2,1)S(1)}, bf16[4,192,512]{2,1,0:T(8,128)(2,1)S(1)}, f32[1,768]{1,0:T(1,128)S(1)}) custom-call(s32[1]{0:T(128)} %bitcast.row_ref, bf16[2048,768]{1,0:T(8,128)(2,1)} %get-tuple-element.98.res_ref._res, bf16[2048,768]{1,0:T(8,128)(2,1)} %get-tuple-element.89.mid_ref, ...), custom_call_target="tpu_custom_call" | custom-call | flops 12000000000 | bytes 16777216 | tf_op jit(solution)/shard_map/ffn_back/pallas_call | solution.py:765
  165.8 17.7 %attn_back.1 = (bf16[4,576,512]{2,1,0:T(8,128)(2,1)}, f32[4,3,8,768]{3,2,1,0:T(8,128)S(1)}, bf16[512,768]{1,0:T(8,128)(2,1)}, f32[1,768]{1,0:T(1,128)S(1)}) custom-call(s32[1]{0:T(128)} %bitcast.row_ref, bf16[4,4,576,512]{3,2,1,0:T(8,128)(2,1)} %get-tuple-element.104.qkv_ref, f32[4,4,3,512]{3,2,1,0:T(4,128)S(1)} %get-tuple-element.92.lse_ref, ...), custom_call_target="tpu_custom_call" | custom-call | flops 15000000512 | bytes 16777216 | tf_op jit(solution)/shard_map/attn_back/pallas_call | solution.py:921
  186.5 8.9 %attn_weights.1 = (bf16[4,4,112,768]{3,2,1,0:T(8,128)(2,1)}, bf16[4,4,112,768]{3,2,1,0:T(8,128)(2,1)}) custom-call(s32[6]{0:T(128)S(1)} %pad_add_fusion.place_ref, bf16[2048,768]{1,0:T(8,128)(2,1)} %fusion.2.a1_ref, bf16[512,768]{1,0:T(8,128)(2,1)S(1)} %get-tuple-element.103.dattn_ref, bf16[4,576,512]{2,1,0:T(8,128)(2,1)} %get-tuple-element.107.dqkv_ref, ...), custom_call_target="tpu_custom_call" | custom-call | flops 1000000 | bytes 1000000 | tf_op jit(solution)/shard_map/attn_weights/pallas_call | solution.py:1017
  195.4 5.4 %collective-permute-done.24 = bf16[4,4,112,768]{3,2,1,0:T(8,128)(2,1)} collective-permute-done((bf16[4,4,112,768]{3,2,1,0:T(8,128)(2,1)}, bf16[4,4,112,768]{3,2,1,0:T(8,128)(2,1)}, u32[]{:S(2)}, u32[]{:S(2)}) %collective-permute-start.24) | collective-permute-done | bytes 2752544 | tf_op jit(solution)/shard_map/ppermute | solution.py:1170
  200.8 4.7 %fusion.19 = (bf16[4,112,768]{2,1,0:T(8,128)(2,1)S(1)}, bf16[4,112,768]{2,1,0:T(8,128)(2,1)S(1)}, bf16[4,112,768]{2,1,0:T(8,128)(2,1)S(1)}, f32[4,112,768]{2,1,0:T(8,128)}) fusion(bf16[4,4,112,768]{3,2,1,0:T(8,128)(2,1)} %collective-permute-done.24, bf16[4,4,112,768]{3,2,1,0:T(8,128)(2,1)} %get-tuple-element.111), kind=kLoop, calls=%fused_computation.70 | loop fusion | flops 6537216 | bytes 8945664 | tf_op jit(solution)/shard_map/convert_element_type | solution.py:1296
  209.0 18.3 %ffn_rest.1 = (bf16[2048,768]{1,0:T(8,128)(2,1)}, bf16[2048,768]{1,0:T(8,128)(2,1)}) custom-call(s32[4]{0:T(128)S(1)} %copy-done.3, bf16[2048,768]{1,0:T(8,128)(2,1)} %get-tuple-element.88.a2_ref, bf16[2048,768]{1,0:T(8,128)(2,1)} %get-tuple-element.89.mid_ref, ...), custom_call_target="tpu_custom_call", output_to_operand_aliasing={{0}: (7, {}), {1}: (8, {})} | custom-call | flops 10871635968 | bytes 16777216 | tf_op jit(solution)/shard_map/ffn_rest/pallas_call | solution.py:573
  227.3 11.8 %ffn_grads.1 = (bf16[2048,768]{1,0:T(8,128)(2,1)}, bf16[2048,768]{1,0:T(8,128)(2,1)}, bf16[2048,768]{1,0:T(8,128)(2,1)}) custom-call(bf16[2048,768]{1,0:T(8,128)(2,1)} %get-tuple-element.117.res_ref, s32[4,1,512]{2,1,0:T(1,128)S(1)} %broadcast_in_dim.54.seg_ref, f32[32,768]{1,0:T(8,128)S(1)} %get-tuple-element.100.dpool_ref, ...), custom_call_target="tpu_custom_call" | custom-call | flops 8000000000 | bytes 16777216 | tf_op jit(solution)/shard_map/ffn_grads/pallas_call | solution.py:1060
  239.1 10.2 %ffn_weights.1 = (bf16[4,2,96,768]{3,2,1,0:T(8,128)(2,1)S(1)}, bf16[4,2,96,768]{3,2,1,0:T(8,128)(2,1)}) custom-call(s32[6]{0:T(128)S(1)} %pad_add_fusion.place_ref, bf16[2048,768]{1,0:T(8,128)(2,1)} %get-tuple-element.118.low_ref, bf16[2048,768]{1,0:T(8,128)(2,1)} %get-tuple-element.119.hid_ref, bf16[2048,768]{1,0:T(8,128)(2,1)} %get-tuple-element.88.a2_ref, ...), custom_call_target="tpu_custom_call" | custom-call | flops 8000000000 | bytes 16777216 | tf_op jit(solution)/shard_map/ffn_weights/pallas_call | solution.py:1124
  249.4 3.0 %collective-permute-done.28 = bf16[4,2,96,768]{3,2,1,0:T(8,128)(2,1)S(1)} collective-permute-done((bf16[4,2,96,768]{3,2,1,0:T(8,128)(2,1)}, bf16[4,2,96,768]{3,2,1,0:T(8,128)(2,1)S(1)}, u32[]{:S(2)}, u32[]{:S(2)}) %collective-permute-start.28) | collective-permute-done | bytes 1179680 | tf_op jit(solution)/shard_map/ppermute | solution.py:1170
  258.6 5.2 %convert_element_type.205 = f32[2048,768]{1,0:T(8,128)} convert(bf16[2048,768]{1,0:T(8,128)(2,1)} %all-gather.6.cloned.1.call-done) | non-fusion elementwise | flops 1572864 | bytes 9437184 | tf_op jit(solution)/shard_map/convert_element_type | solution.py:1263
  264.6 6.4 %collective-permute-done.30 = bf16[2,96,768]{2,1,0:T(8,128)(2,1)} collective-permute-done((bf16[2,96,768]{2,1,0:T(8,128)(2,1)}, bf16[2,96,768]{2,1,0:T(8,128)(2,1)}, u32[]{:S(2)}, u32[]{:S(2)}) %collective-permute-start.30) | collective-permute-done | bytes 294944 | tf_op jit(solution)/shard_map/ppermute | solution.py:1170
  273.0 2.8 collective-permute-start.32
  278.1 2.6 collective-permute-done.34
  280.7 6.9 %collective-permute-done.33 = bf16[112,768]{1,0:T(8,128)(2,1)S(1)} collective-permute-done((bf16[112,768]{1,0:T(8,128)(2,1)S(1)}, bf16[112,768]{1,0:T(8,128)(2,1)S(1)}, u32[]{:S(2)}, u32[]{:S(2)}) %collective-permute-start.33) | collective-permute-done | bytes 172064 | tf_op jit(solution)/shard_map/ppermute | solution.py:1173
  (198 shorter events, 49.9 us)
Async XLA Ops:
  7.2 45.7 %all-gather.8.cloned.1.call-start = ((), (), s32[]{:S(2)}) async-start(), calls=%async_computation.1 | async-start | bytes 1474560 | tf_op jit(solution)/shard_map/all_gather | solution.py:1203
  11.3 13.3 %collective-permute-start = (bf16[112,768]{1,0:T(8,128)(2,1)S(1)}, bf16[112,768]{1,0:T(8,128)(2,1)S(1)}, u32[]{:S(2)}, u32[]{:S(2)}) collective-permute-start(bf16[112,768]{1,0:T(8,128)(2,1)S(1)} %get-tuple-element.72), channel_id=1, source_target_pairs={{0,1},{1,0},{2,3},{3,2},{4,5},{5,4},{6,7},{7,6},{8,9},{9,8},{10,11... | collective-permute-start | bytes 516104 | tf_op jit(solution)/shard_map/ppermute | solution.py:1173
  14.3 15.6 %collective-permute-start.1 = (bf16[112,768]{1,0:T(8,128)(2,1)S(1)}, bf16[112,768]{1,0:T(8,128)(2,1)S(1)}, u32[]{:S(2)}, u32[]{:S(2)}) collective-permute-start(bf16[112,768]{1,0:T(8,128)(2,1)S(1)} %get-tuple-element.72), channel_id=1, source_target_pairs={{0,2},{1,3},{2,0},{3,1},{4,6},{5,7},{6,4},{7,5},{8,10},{9,11},{10,... | collective-permute-start | bytes 516104 | tf_op jit(solution)/shard_map/ppermute | solution.py:1173
  16.9 13.0 %collective-permute-start.2 = (bf16[112,768]{1,0:T(8,128)(2,1)S(1)}, bf16[112,768]{1,0:T(8,128)(2,1)S(1)}, u32[]{:S(2)}, u32[]{:S(2)}) collective-permute-start(bf16[112,768]{1,0:T(8,128)(2,1)S(1)} %get-tuple-element.72), channel_id=1, source_target_pairs={{0,3},{1,2},{2,1},{3,0},{4,7},{5,6},{6,5},{7,4},{8,11},{9,10},{10,... | collective-permute-start | bytes 516104 | tf_op jit(solution)/shard_map/ppermute | solution.py:1173
  18.6 93.2 %all-gather.10.cloned.1.call-start = ((), (), s32[]{:S(2)}) async-start(), calls=%async_computation.2 | async-start | bytes 3981312 | tf_op jit(solution)/shard_map/all_gather | solution.py:1219
  33.1 14.5 %collective-permute-start.3 = (bf16[3,96,768]{2,1,0:T(8,128)(2,1)}, bf16[3,96,768]{2,1,0:T(8,128)(2,1)S(1)}, u32[]{:S(2)}, u32[]{:S(2)}) collective-permute-start(bf16[3,96,768]{2,1,0:T(8,128)(2,1)} %get-tuple-element.82.rest_0_), channel_id=1, source_target_pairs={{0,8},{4,12},{8,0},{12,4},{16,24},{20,28},{24,16},{28,20},{1,9},{5... | collective-permute-start | bytes 1327112 | tf_op jit(solution)/shard_map/ppermute | solution.py:1170
  34.6 18.3 %collective-permute-start.4 = (bf16[3,96,768]{2,1,0:T(8,128)(2,1)}, bf16[3,96,768]{2,1,0:T(8,128)(2,1)}, u32[]{:S(2)}, u32[]{:S(2)}) collective-permute-start(bf16[3,96,768]{2,1,0:T(8,128)(2,1)} %get-tuple-element.82.rest_0_), channel_id=1, source_target_pairs={{0,16},{4,20},{8,24},{12,28},{16,0},{20,4},{24,8},{28,12},{1,17},{... | collective-permute-start | bytes 1327112 | tf_op jit(solution)/shard_map/ppermute | solution.py:1170
  36.1 16.8 %collective-permute-start.5 = (bf16[3,96,768]{2,1,0:T(8,128)(2,1)}, bf16[3,96,768]{2,1,0:T(8,128)(2,1)}, u32[]{:S(2)}, u32[]{:S(2)}) collective-permute-start(bf16[3,96,768]{2,1,0:T(8,128)(2,1)} %get-tuple-element.82.rest_0_), channel_id=1, source_target_pairs={{0,24},{4,28},{8,16},{12,20},{16,8},{20,12},{24,0},{28,4},{1,25},{... | collective-permute-start | bytes 1327112 | tf_op jit(solution)/shard_map/ppermute | solution.py:1170
  55.9 202.7 %all-gather.6.cloned.1.call-start = ((), (), s32[]{:S(2)}) async-start(), calls=%async_computation | async-start | bytes 3932160 | tf_op jit(solution)/shard_map/all_gather | solution.py:1263
  60.3 36.0 %collective-permute-start.10 = (bf16[3,96,768]{2,1,0:T(8,128)(2,1)}, bf16[3,96,768]{2,1,0:T(8,128)(2,1)S(1)}, u32[]{:S(2)}, u32[]{:S(2)}) collective-permute-start(bf16[3,96,768]{2,1,0:T(8,128)(2,1)} %get-tuple-element.93.rest_0_), channel_id=1, source_target_pairs={{0,8},{4,12},{8,0},{12,4},{16,24},{20,28},{24,16},{28,20},{1,9},{5... | collective-permute-start | bytes 1327112 | tf_op jit(solution)/shard_map/ppermute | solution.py:1170
  61.5 34.7 %collective-permute-start.11 = (bf16[3,96,768]{2,1,0:T(8,128)(2,1)}, bf16[3,96,768]{2,1,0:T(8,128)(2,1)S(1)}, u32[]{:S(2)}, u32[]{:S(2)}) collective-permute-start(bf16[3,96,768]{2,1,0:T(8,128)(2,1)} %get-tuple-element.93.rest_0_), channel_id=1, source_target_pairs={{0,16},{4,20},{8,24},{12,28},{16,0},{20,4},{24,8},{28,12},{1,17},{... | collective-permute-start | bytes 1327112 | tf_op jit(solution)/shard_map/ppermute | solution.py:1170
  62.3 33.9 %collective-permute-start.12 = (bf16[3,96,768]{2,1,0:T(8,128)(2,1)}, bf16[3,96,768]{2,1,0:T(8,128)(2,1)S(1)}, u32[]{:S(2)}, u32[]{:S(2)}) collective-permute-start(bf16[3,96,768]{2,1,0:T(8,128)(2,1)} %get-tuple-element.93.rest_0_), channel_id=1, source_target_pairs={{0,24},{4,28},{8,16},{12,20},{16,8},{20,12},{24,0},{28,4},{1,25},{... | collective-permute-start | bytes 1327112 | tf_op jit(solution)/shard_map/ppermute | solution.py:1170
  96.3 14.7 %collective-permute-start.13 = (bf16[3,96,768]{2,1,0:T(8,128)(2,1)S(1)}, bf16[3,96,768]{2,1,0:T(8,128)(2,1)S(1)}, u32[]{:S(2)}, u32[]{:S(2)}) collective-permute-start(bf16[3,96,768]{2,1,0:T(8,128)(2,1)S(1)} %copy-done), channel_id=1, source_target_pairs={{0,4},{4,0},{8,12},{12,8},{16,20},{20,16},{24,28},{28,24},{1,5},{5... | collective-permute-start | bytes 1327112 | tf_op jit(solution)/shard_map/ppermute | solution.py:1170
  96.3 14.7 %collective-permute-start.14 = (bf16[3,96,768]{2,1,0:T(8,128)(2,1)S(1)}, bf16[3,96,768]{2,1,0:T(8,128)(2,1)S(1)}, u32[]{:S(2)}, u32[]{:S(2)}) collective-permute-start(bf16[3,96,768]{2,1,0:T(8,128)(2,1)S(1)} %collective-permute-done.10.rest_2_), channel_id=1, source_target_pairs={{0,4},{4,0},{8,12},{12,8},{16,20},{20,16},{24,28},{28,24},{1,5},{5... | collective-permute-start | bytes 1327112 | tf_op jit(solution)/shard_map/ppermute | solution.py:1170
  96.8 14.2 %collective-permute-start.15 = (bf16[3,96,768]{2,1,0:T(8,128)(2,1)S(1)}, bf16[3,96,768]{2,1,0:T(8,128)(2,1)S(1)}, u32[]{:S(2)}, u32[]{:S(2)}) collective-permute-start(bf16[3,96,768]{2,1,0:T(8,128)(2,1)S(1)} %collective-permute-done.11.rest_4_), channel_id=1, source_target_pairs={{0,4},{4,0},{8,12},{12,8},{16,20},{20,16},{24,28},{28,24},{1,5},{5... | collective-permute-start | bytes 1327112 | tf_op jit(solution)/shard_map/ppermute | solution.py:1170
  96.9 14.9 %collective-permute-start.16 = (bf16[3,96,768]{2,1,0:T(8,128)(2,1)S(1)}, bf16[3,96,768]{2,1,0:T(8,128)(2,1)}, u32[]{:S(2)}, u32[]{:S(2)}) collective-permute-start(bf16[3,96,768]{2,1,0:T(8,128)(2,1)S(1)} %collective-permute-done.12.rest_6_), channel_id=1, source_target_pairs={{0,4},{4,0},{8,12},{12,8},{16,20},{20,16},{24,28},{28,24},{1,5},{5... | collective-permute-start | bytes 1327112 | tf_op jit(solution)/shard_map/ppermute | solution.py:1170
  123.4 8.7 %collective-permute-start.17 = (bf16[8,768]{1,0:T(8,128)(2,1)S(1)}, bf16[8,768]{1,0:T(8,128)(2,1)S(1)}, u32[]{:S(2)}, u32[]{:S(2)}) collective-permute-start(bf16[8,768]{1,0:T(8,128)(2,1)S(1)} %get-tuple-element.186), channel_id=1, source_target_pairs={{0,1},{1,0},{2,3},{3,2},{4,5},{5,4},{6,7},{7,6},{8,9},{9,8},{10,11... | collective-permute-start | bytes 36872 | tf_op jit(solution)/shard_map/ppermute | solution.py:1173
  127.6 4.6 %collective-permute-start.18 = (bf16[8,768]{1,0:T(8,128)(2,1)S(1)}, bf16[8,768]{1,0:T(8,128)(2,1)S(1)}, u32[]{:S(2)}, u32[]{:S(2)}) collective-permute-start(bf16[8,768]{1,0:T(8,128)(2,1)S(1)} %get-tuple-element.186), channel_id=1, source_target_pairs={{0,2},{1,3},{2,0},{3,1},{4,6},{5,7},{6,4},{7,5},{8,10},{9,11},{10,... | collective-permute-start | bytes 36872 | tf_op jit(solution)/shard_map/ppermute | solution.py:1173
  130.4 5.5 %collective-permute-start.19 = (bf16[8,768]{1,0:T(8,128)(2,1)S(1)}, bf16[8,768]{1,0:T(8,128)(2,1)S(1)}, u32[]{:S(2)}, u32[]{:S(2)}) collective-permute-start(bf16[8,768]{1,0:T(8,128)(2,1)S(1)} %get-tuple-element.186), channel_id=1, source_target_pairs={{0,3},{1,2},{2,1},{3,0},{4,7},{5,6},{6,5},{7,4},{8,11},{9,10},{10,... | collective-permute-start | bytes 36872 | tf_op jit(solution)/shard_map/ppermute | solution.py:1173
  137.1 4.9 %collective-permute-start.21 = (bf16[64,768]{1,0:T(8,128)(2,1)S(1)}, bf16[64,768]{1,0:T(8,128)(2,1)S(1)}, u32[]{:S(2)}, u32[]{:S(2)}) collective-permute-start(bf16[64,768]{1,0:T(8,128)(2,1)S(1)} %constant_dynamic-update-slice_fusion.refs_0_), channel_id=1, source_target_pairs={{0,8},{4,12},{8,0},{12,4},{16,24},{20,28},{24,16},{28,20},{1,9},{5... | collective-permute-start | bytes 294920 | tf_op jit(solution)/shard_map/ppermute | solution.py:1170
  138.4 5.6 %collective-permute-start.22 = (bf16[64,768]{1,0:T(8,128)(2,1)S(1)}, bf16[64,768]{1,0:T(8,128)(2,1)S(1)}, u32[]{:S(2)}, u32[]{:S(2)}) collective-permute-start(bf16[64,768]{1,0:T(8,128)(2,1)S(1)} %constant_dynamic-update-slice_fusion.refs_0_), channel_id=1, source_target_pairs={{0,16},{4,20},{8,24},{12,28},{16,0},{20,4},{24,8},{28,12},{1,17},{... | collective-permute-start | bytes 294920 | tf_op jit(solution)/shard_map/ppermute | solution.py:1170
  139.7 5.5 %collective-permute-start.23 = (bf16[64,768]{1,0:T(8,128)(2,1)S(1)}, bf16[64,768]{1,0:T(8,128)(2,1)S(1)}, u32[]{:S(2)}, u32[]{:S(2)}) collective-permute-start(bf16[64,768]{1,0:T(8,128)(2,1)S(1)} %constant_dynamic-update-slice_fusion.refs_0_), channel_id=1, source_target_pairs={{0,24},{4,28},{8,16},{12,20},{16,8},{20,12},{24,0},{28,4},{1,25},{... | collective-permute-start | bytes 294920 | tf_op jit(solution)/shard_map/ppermute | solution.py:1170
  195.4 5.4 %collective-permute-start.24 = (bf16[4,4,112,768]{3,2,1,0:T(8,128)(2,1)}, bf16[4,4,112,768]{3,2,1,0:T(8,128)(2,1)}, u32[]{:S(2)}, u32[]{:S(2)}) collective-permute-start(bf16[4,4,112,768]{3,2,1,0:T(8,128)(2,1)} %get-tuple-element.112), channel_id=1, source_target_pairs={{0,4},{4,0},{8,12},{12,8},{16,20},{20,16},{24,28},{28,24},{1,5},{5... | collective-permute-start | bytes 8257544 | tf_op jit(solution)/shard_map/ppermute | solution.py:1170
  205.5 43.8 %collective-permute-start.25 = (bf16[4,112,768]{2,1,0:T(8,128)(2,1)S(1)}, bf16[4,112,768]{2,1,0:T(8,128)(2,1)S(1)}, u32[]{:S(2)}, u32[]{:S(2)}) collective-permute-start(bf16[4,112,768]{2,1,0:T(8,128)(2,1)S(1)} %get-tuple-element.188), channel_id=1, source_target_pairs={{0,8},{4,12},{8,0},{12,4},{16,24},{20,28},{24,16},{28,20},{1,9},{5... | collective-permute-start | bytes 2064392 | tf_op jit(solution)/shard_map/ppermute | solution.py:1170
  206.6 42.7 %collective-permute-start.26 = (bf16[4,112,768]{2,1,0:T(8,128)(2,1)S(1)}, bf16[4,112,768]{2,1,0:T(8,128)(2,1)S(1)}, u32[]{:S(2)}, u32[]{:S(2)}) collective-permute-start(bf16[4,112,768]{2,1,0:T(8,128)(2,1)S(1)} %get-tuple-element.189), channel_id=1, source_target_pairs={{0,16},{4,20},{8,24},{12,28},{16,0},{20,4},{24,8},{28,12},{1,17},{... | collective-permute-start | bytes 2064392 | tf_op jit(solution)/shard_map/ppermute | solution.py:1170
  207.8 41.6 %collective-permute-start.27 = (bf16[4,112,768]{2,1,0:T(8,128)(2,1)S(1)}, bf16[4,112,768]{2,1,0:T(8,128)(2,1)S(1)}, u32[]{:S(2)}, u32[]{:S(2)}) collective-permute-start(bf16[4,112,768]{2,1,0:T(8,128)(2,1)S(1)} %get-tuple-element.187), channel_id=1, source_target_pairs={{0,24},{4,28},{8,16},{12,20},{16,8},{20,12},{24,0},{28,4},{1,25},{... | collective-permute-start | bytes 2064392 | tf_op jit(solution)/shard_map/ppermute | solution.py:1170
  254.5 10.1 %collective-permute-start.29 = (bf16[2,96,768]{2,1,0:T(8,128)(2,1)}, bf16[2,96,768]{2,1,0:T(8,128)(2,1)S(1)}, u32[]{:S(2)}, u32[]{:S(2)}) collective-permute-start(bf16[2,96,768]{2,1,0:T(8,128)(2,1)} %get-tuple-element.193), channel_id=1, source_target_pairs={{0,8},{4,12},{8,0},{12,4},{16,24},{20,28},{24,16},{28,20},{1,9},{5... | collective-permute-start | bytes 884744 | tf_op jit(solution)/shard_map/ppermute | solution.py:1170
  255.6 15.4 %collective-permute-start.30 = (bf16[2,96,768]{2,1,0:T(8,128)(2,1)}, bf16[2,96,768]{2,1,0:T(8,128)(2,1)}, u32[]{:S(2)}, u32[]{:S(2)}) collective-permute-start(bf16[2,96,768]{2,1,0:T(8,128)(2,1)} %get-tuple-element.192), channel_id=1, source_target_pairs={{0,16},{4,20},{8,24},{12,28},{16,0},{20,4},{24,8},{28,12},{1,17},{... | collective-permute-start | bytes 884744 | tf_op jit(solution)/shard_map/ppermute | solution.py:1170
  256.8 14.2 %collective-permute-start.31 = (bf16[2,96,768]{2,1,0:T(8,128)(2,1)}, bf16[2,96,768]{2,1,0:T(8,128)(2,1)}, u32[]{:S(2)}, u32[]{:S(2)}) collective-permute-start(bf16[2,96,768]{2,1,0:T(8,128)(2,1)} %get-tuple-element.191), channel_id=1, source_target_pairs={{0,24},{4,28},{8,16},{12,20},{16,8},{20,12},{24,0},{28,4},{1,25},{... | collective-permute-start | bytes 884744 | tf_op jit(solution)/shard_map/ppermute | solution.py:1170
  271.4 9.3 %collective-permute-start.34 = (bf16[112,768]{1,0:T(8,128)(2,1)S(1)}, bf16[112,768]{1,0:T(8,128)(2,1)S(1)}, u32[]{:S(2)}, u32[]{:S(2)}) collective-permute-start(bf16[112,768]{1,0:T(8,128)(2,1)S(1)} %get-tuple-element.195), channel_id=1, source_target_pairs={{0,3},{1,2},{2,1},{3,0},{4,7},{5,6},{6,5},{7,4},{8,11},{9,10},{10,... | collective-permute-start | bytes 516104 | tf_op jit(solution)/shard_map/ppermute | solution.py:1173
  272.6 15.0 %collective-permute-start.33 = (bf16[112,768]{1,0:T(8,128)(2,1)S(1)}, bf16[112,768]{1,0:T(8,128)(2,1)S(1)}, u32[]{:S(2)}, u32[]{:S(2)}) collective-permute-start(bf16[112,768]{1,0:T(8,128)(2,1)S(1)} %get-tuple-element.196), channel_id=1, source_target_pairs={{0,2},{1,3},{2,0},{3,1},{4,6},{5,7},{6,4},{7,5},{8,10},{9,11},{10,... | collective-permute-start | bytes 516104 | tf_op jit(solution)/shard_map/ppermute | solution.py:1173
  273.0 14.6 %collective-permute-start.32 = (bf16[112,768]{1,0:T(8,128)(2,1)S(1)}, bf16[112,768]{1,0:T(8,128)(2,1)S(1)}, u32[]{:S(2)}, u32[]{:S(2)}) collective-permute-start(bf16[112,768]{1,0:T(8,128)(2,1)S(1)} %get-tuple-element.194), channel_id=1, source_target_pairs={{0,1},{1,0},{2,3},{3,2},{4,5},{5,4},{6,7},{7,6},{8,9},{9,8},{10,11... | collective-permute-start | bytes 516104 | tf_op jit(solution)/shard_map/ppermute | solution.py:1173
  (43 other events, 325.2 us)
Sparse Core Ops, SparseCore 0:
  18.7 32.7 all-gather.7
  56.0 48.9 all-gather.9
  195.5 61.9 all-gather.5
where the time goes:
time: 303 us; the launch traced here: 297 us
  Pallas kernels  161 us (53%)
  waiting for transfers between devices  47.8 us (16%)
  starting transfers between devices  38.3 us (13%)
  other arithmetic  19.4 us (6%)
  between operations  14.9 us (5%)
  local copies, waits for them, and re-layouts  13.9 us (5%)
    pallas_call x1, Pallas kernels, attention(): pl.pallas_call(functools.partial(attn_far_kernel, heads, hd, n), grid_spe...  32.4 us
    ppermute x26, waiting for transfers between devices, over_dp(): return lax.ppermute(value, 'dp', mates[m])  29.2 us
    ppermute x26, starting transfers between devices, over_dp(): return lax.ppermute(value, 'dp', mates[m])  19.7 us
    ppermute x9, waiting for transfers between devices, over_tp(): return lax.ppermute(value, 'tp', levels[k])  18.6 us
    ppermute x9, starting transfers between devices, over_tp(): return lax.ppermute(value, 'tp', levels[k])  18.5 us
    pallas_call x1, Pallas kernels, ffn_rest(): pl.pallas_call(ffn_rest_kernel, grid_spec=pltpu.PrefetchScalarGridSpec(nu...  18.3 us
    pallas_call x1, Pallas kernels, attn_back(): pl.pallas_call(functools.partial(attn_back_kernel, heads, cols // heads),...  17.7 us
    pallas_call x1, Pallas kernels, ffn_back(): pl.pallas_call(ffn_back_kernel, grid_spec=pltpu.PrefetchScalarGridSpec(nu...  16 us
  transfers between devices with their start and end apart: 38, of which 18 were waited for; matrix products, arithmetic and copies ran while one was open for 7% of the time, Pallas kernels for 33%

commit v1 on v0

--- a/solution.py
+++ b/solution.py
@@ -520,7 +520,7 @@
             + [anywhere] * (n + 1),
             out_specs=[
                 first,
-                first,
+                pl.BlockSpec((length, width), lambda r, p, o: (0, 0)),
                 pl.BlockSpec((SEG_ROW, width), lambda r, p, o: (0, 0)),
                 anywhere,
                 anywhere,
@@ -534,7 +534,7 @@
         ),
         out_shape=[
             jax.ShapeDtypeStruct((tokens, width), bf16),
-            jax.ShapeDtypeStruct((tokens, width), bf16),
+            jax.ShapeDtypeStruct((length, width), bf16),
             jax.ShapeDtypeStruct((SEG_ROW, width), f32),
             jax.ShapeDtypeStruct((others, width, units), bf16),
             jax.ShapeDtypeStruct((others, units, width), bf16),
@@ -543,48 +543,6 @@
         cost_estimate=cost(length * width * 4 * units * others, 2**24),
         name="ffn_first",
     )(place, order, a2, mid, part, gain, segs, *pieces, far_c)
-
-
-def ffn_rest_kernel(
-    order_ref, a2_ref, mid_ref, part_ref, gain_ref, b_ref, c_ref, _out, _res, out_ref, res_ref
-):
-    others = b_ref.shape[0]
-    ffn_row(
-        a2_ref[...],
-        mid_ref[...],
-        part_ref[...],
-        [b_ref.at[k] for k in range(others)],
-        [c_ref.at[k] for k in range(others)],
-        gain_ref,
-        None,
-        out_ref,
-        res_ref,
-        None,
-    )
-
-
-def ffn_rest(order, a2, mid, part, gain, sorted_b, sorted_c, out, res, rows):
-    tokens, width = a2.shape
-    length = tokens // rows
-    slots, _, units = sorted_b.shape
-    row = pl.BlockSpec((length, width), lambda r, o: (o[r + 1], 0))
-    whole = pl.BlockSpec(sorted_b.shape, lambda r, o: (0, 0, 0))
-    anywhere = pl.BlockSpec(memory_space=pl.ANY)
-    return pl.pallas_call(
-        ffn_rest_kernel,
-        grid_spec=pltpu.PrefetchScalarGridSpec(
-            num_scalar_prefetch=1,
-            grid=(rows - 1,),
-            in_specs=[row, row, row, pl.BlockSpec((1, width), lambda r, o: (0, 0)), whole, whole]
-            + [anywhere] * 2,
-            out_specs=[row, row],
-        ),
-        out_shape=[jax.ShapeDtypeStruct((tokens, width), bf16)] * 2,
-        input_output_aliases={7: 0, 8: 1},
-        compiler_params=pltpu.CompilerParams(vmem_limit_bytes=VMEM),
-        cost_estimate=cost(tokens * width * 3 * units * slots, 2**24),
-        name="ffn_rest",
-    )(order, a2, mid, part, gain, sorted_b, sorted_c, out, res)
 
 
 def loss_math(pooled, project, pair_col, pair_row, gain):
@@ -756,7 +714,7 @@
     row, res, mid, a2, segs, d_pool, gain_end, gain, sorted_a, own_b, own_c, sorted_b, sorted_c
 ):
     rows, _, length = segs.shape
-    tokens, width = res.shape
+    tokens, width = mid.shape
     slots = sorted_a.shape[0]
     units = sorted_b.shape[-1]
     cols = width // 4
@@ -768,7 +726,7 @@
             num_scalar_prefetch=1,
             grid=(slots,),
             in_specs=[
-                own,
+                pl.BlockSpec((length, width), fixed),
                 own,
                 own,
                 pl.BlockSpec((1, 1, length), lambda k, row: (row[0], 0, 0)),
@@ -966,10 +924,11 @@
             for chip in range(4):
                 for ref, j in ((keep_ref, 2 * chip + c), (give_ref, 2 * chip + 1 - c)):
                     rows = values(j * block, (j + 1) * block)
+                    to = chip if rel_ref is None else rel_ref[chip]
                     for at, value in enumerate(rows):
-                        ref[rel_ref[chip], lead + at, :block] = value
+                        ref[to, lead + at, :block] = value
                     if pad:
-                        ref[rel_ref[chip], lead, block:] = extra(j)
+                        ref[to, lead, block:] = extra(j)
 
 
 def attn_weights_kernel(
@@ -1040,58 +999,57 @@
     )(place, a1, d_attn, d_qkv, ctx, extra)
 
 
-def ffn_grads_kernel(
-    res_ref, seg_ref, dpool_ref, gain_ref, a2_ref, b_ref, c_ref, low_ref, hid_ref, dpre_ref
+def ffn_tail_kernel(
+    block,
+    place_ref,
+    order_ref,
+    a2_ref,
+    mid_ref,
+    part_ref,
+    own_ref,
+    seg_ref,
+    dpool_ref,
+    gain_ref,
+    own_b_ref,
+    own_c_ref,
+    b_ref,
+    c_ref,
+    _out,
+    out_ref,
+    *rest,
 ):
-    d_res = d_result_of(res_ref[...].astype(f32), seg_ref[0], dpool_ref[...], gain_ref[...])
-    low = d_res.astype(bf16)
-    low_ref[...] = low
-    hidden, slope = gelu_pair(dg(a2_ref[...], b_ref[...], NN))
-    hid_ref[...] = hidden.astype(bf16)
-    dpre_ref[...] = (dg(low, c_ref[...], NT) * slope).astype(bf16)
-
-
-def ffn_grads(res, segs, d_pool, gain, a2, own_b, own_c):
-    rows, _, length = segs.shape
-    tokens, width = res.shape
-    units = own_b.shape[1]
-    by_row = pl.BlockSpec((length, width), lambda r: (r, 0))
-    by_unit = pl.BlockSpec((length, units), lambda r: (r, 0))
-    return pl.pallas_call(
-        ffn_grads_kernel,
-        grid=(rows,),
-        in_specs=[
-            by_row,
-            pl.BlockSpec((1, 1, length), lambda r: (r, 0, 0)),
-            pl.BlockSpec((SEG_ROW, width), lambda r: (r, 0)),
-            pl.BlockSpec((1, width), lambda r: (0, 0)),
-            by_row,
-            pl.BlockSpec((width, units), lambda r: (0, 0)),
-            pl.BlockSpec((units, width), lambda r: (0, 0)),
-        ],
-        out_specs=[by_row, by_unit, by_unit],
-        out_shape=[
-            jax.ShapeDtypeStruct((tokens, width), bf16),
-            jax.ShapeDtypeStruct((tokens, units), bf16),
-            jax.ShapeDtypeStruct((tokens, units), bf16),
-        ],
-        compiler_params=pltpu.CompilerParams(vmem_limit_bytes=VMEM),
-        cost_estimate=cost(8 * 10**9, 2**24),
-        name="ffn_grads",
-    )(res, segs, d_pool, gain, a2, own_b, own_c)
-
-
-def ffn_weights_kernel(block, place_ref, low_ref, hid_ref, a2_ref, dpre_ref, *rest):
-    outs, (up_s, down_s) = rest[:-2], rest[-2:]
+    outs, (res_s, up_s, down_s) = rest[:-3], rest[-3:]
     r = pl.program_id(0)
+    others = b_ref.shape[0]
 
     @pl.when(r == 0)
     def _():
+        res_s[...] = own_ref[...]
         up_s[...] = jnp.zeros_like(up_s)
         down_s[...] = jnp.zeros_like(down_s)
 
-    up_s[...] += dg(a2_ref[...], dpre_ref[...], TN)
-    down_s[...] += dg(low_ref[...], hid_ref[...], TN)
+    @pl.when(r > 0)
+    def _():
+        ffn_row(
+            a2_ref[...],
+            mid_ref[...],
+            part_ref[...],
+            [b_ref.at[k] for k in range(others)],
+            [c_ref.at[k] for k in range(others)],
+            gain_ref,
+            None,
+            out_ref,
+            res_s,
+            None,
+        )
+
+    d_res = d_result_of(res_s[...].astype(f32), seg_ref[0], dpool_ref[...], gain_ref[...])
+    low = d_res.astype(bf16)
+    a2 = a2_ref[...]
+    hidden, slope = gelu_pair(dg(a2, own_b_ref[...], NN))
+    down_s[...] += dg(low, hidden.astype(bf16), TN)
+    d_pre = (dg(low, own_c_ref[...], NT) * slope).astype(bf16)
+    up_s[...] += dg(a2, d_pre, TN)
 
     @pl.when(r == pl.num_programs(0) - 1)
     def _():
@@ -1101,7 +1059,7 @@
         else:
             split_blocks(
                 place_ref[1],
-                place_ref.at[pl.ds(2, 4)],
+                None,
                 block,
                 False,
                 None,
@@ -1112,29 +1070,57 @@
             )
 
 
-def ffn_weights(place, low, hidden, a2, d_pre, rows, blocks, split):
-    tokens, width = low.shape
-    length = tokens // rows
-    units = hidden.shape[1]
+def ffn_tail(
+    place, order, a2, mid, part, res, segs, d_pool, gain, own_b, own_c, far_b, far_c, out, blocks, split
+):
+    rows, _, length = segs.shape
+    tokens, width = a2.shape
+    units = own_b.shape[1]
+    others = far_b.shape[0]
     block = width // blocks
-    by_row = pl.BlockSpec((length, width), lambda r, p: (r, 0))
-    by_unit = pl.BlockSpec((length, units), lambda r, p: (r, 0))
+    row = pl.BlockSpec((length, width), lambda r, p, o: (o[r], 0))
+    later = pl.BlockSpec((length, width), lambda r, p, o: (o[jnp.maximum(r, 1)], 0))
+
+    def fixed(shape):
+        zeros = (0,) * len(shape)
+        return pl.BlockSpec(shape, lambda r, p, o: zeros, pipeline_mode=pl.Buffered(1))
+
     shape = (4, 2, block, units) if split else (2, width, units)
     zeros = (0,) * len(shape)
+    n = 2 if split else 1
     return pl.pallas_call(
-        functools.partial(ffn_weights_kernel, block),
+        functools.partial(ffn_tail_kernel, block),
         grid_spec=pltpu.PrefetchScalarGridSpec(
-            num_scalar_prefetch=1,
+            num_scalar_prefetch=2,
             grid=(rows,),
-            in_specs=[by_row, by_unit, by_row, by_unit],
-            out_specs=[pl.BlockSpec(shape, lambda r, p: zeros)] * (2 if split else 1),
-            scratch_shapes=[pltpu.VMEM((width, units), f32)] * 2,
+            in_specs=[
+                row,
+                later,
+                later,
+                fixed((length, width)),
+                pl.BlockSpec((1, 1, length), lambda r, p, o: (o[r], 0, 0)),
+                pl.BlockSpec((SEG_ROW, width), lambda r, p, o: (o[r], 0)),
+                fixed((1, width)),
+                fixed((width, units)),
+                fixed((units, width)),
+                fixed((others, width, units)),
+                fixed((others, units, width)),
+                pl.BlockSpec(memory_space=pl.ANY),
+            ],
+            out_specs=[later] + [pl.BlockSpec(shape, lambda r, p, o: zeros)] * n,
+            scratch_shapes=[
+                pltpu.VMEM((length, width), bf16),
+                pltpu.VMEM((width, units), f32),
+                pltpu.VMEM((width, units), f32),
+            ],
         ),
-        out_shape=[jax.ShapeDtypeStruct(shape, bf16)] * (2 if split else 1),
+        out_shape=[jax.ShapeDtypeStruct((tokens, width), bf16)]
+        + [jax.ShapeDtypeStruct(shape, bf16)] * n,
+        input_output_aliases={13: 0},
         compiler_params=pltpu.CompilerParams(vmem_limit_bytes=VMEM),
-        cost_estimate=cost(8 * 10**9, 2**24),
-        name="ffn_weights",
-    )(place, low, hidden, a2, d_pre)
+        cost_estimate=cost(2 * 10**10, 2**24),
+        name="ffn_tail",
+    )(place, order, a2, mid, part, res, segs, d_pool, gain, own_b, own_c, far_b, far_c, out)
 
 
 def shards(
@@ -1307,14 +1293,19 @@
         first = after(order, pair_a)
     else:
         first = after(order, parts_a)
-    layer_out, res = ffn_rest(
-        first, a2, mid, part, end, sorted_b, sorted_c, layer_out, res, rows
-    )
-    low, hidden, d_pre = ffn_grads(res, segs, d_pool, end, a2, w_hidden, w_down)
-    parts_f = ffn_weights(spots, low, hidden, a2, d_pre, rows, n_dp, split)
+    layer_out, *parts_f = ffn_tail(
+        spots, first, a2, mid, part, res, segs, d_pool, end,
+        w_hidden, w_down, sorted_b, sorted_c, layer_out, n_dp, split,
+    )
     if split:
-        got_f = to_chip(to_core(after(parts_f, got_a)))
-        own_a, own_f = rounded(total(after(got_a, got_f))), total(got_f)
+        chips = [[c + core for c in range(0, n_dp, 2)] for core in range(2)]
+        give_f = over_dp(after(parts_f[1], got_a), 1)
+        pair_f = parts_f[0].astype(f32) + give_f.astype(f32)
+        own_a = rounded(total(got_a))
+        swapped = lax.all_to_all(
+            pair_f.astype(bf16), "dp", 0, 0, axis_index_groups=chips, tiled=True
+        )
+        own_f = jnp.sum(swapped.astype(f32), 0)
     else:
         own_a, own_f = rounded(scatter(parts_a)), scatter(parts_f)
 

time: 303 us -> 293 us (0.967)
  Pallas kernels: 161 us -> 154 us
    ppermute x26 -> x23, waiting for transfers between devices: 29.2 us -> 18.9 us  [over_dp(): return lax.ppermute(value, 'dp', mates[m])]
    ppermute x9, waiting for transfers between devices: 18.6 us -> 27.6 us  [over_tp(): return lax.ppermute(value, 'tp', levels[k])]
    pallas_call x3 -> x1, Pallas kernels: 40.3 us -> 33.2 us  [ffn_tail(): pl.pallas_call(functools.partial(ffn_tail_kernel, block), grid_spec=pltpu...]
    all_to_all x0 -> x1, starting transfers between devices: none -> 3.53 us  [shards(): lax.all_to_all(pair_f.astype(bf16), 'dp', 0, 0, axis_index_groups=chips,...]
    ppermute x26 -> x23, starting transfers between devices: 19.7 us -> 16.2 us  [over_dp(): return lax.ppermute(value, 'dp', mates[m])]
    unnamed x83 -> x69, local copies, waits for them, and re-layouts: 9.15 us -> 8.13 us
  transfers between devices with their start and end apart: 38 -> 36, of which waited for: 18 -> 14; matrix products, arithmetic and copies ran while one was open for 7% -> 8% of each run, Pallas kernels for 33% -> 32%
where the time goes in v1:
time: 293 us; the launch traced here: 288 us
  Pallas kernels  154 us (53%)
  waiting for transfers between devices  46.6 us (16%)
  starting transfers between devices  38.4 us (13%)
  other arithmetic  18.3 us (6%)
  between operations  14.8 us (5%)
  local copies, waits for them, and re-layouts  13.6 us (5%)
    pallas_call x1, Pallas kernels, ffn_tail(): pl.pallas_call(functools.partial(ffn_tail_kernel, block), grid_spec=pltpu...  33.2 us
    pallas_call x1, Pallas kernels, attention(): pl.pallas_call(functools.partial(attn_far_kernel, heads, hd, n), grid_spe...  32.5 us
    ppermute x9, waiting for transfers between devices, over_tp(): return lax.ppermute(value, 'tp', levels[k])  27.6 us
    ppermute x23, waiting for transfers between devices, over_dp(): return lax.ppermute(value, 'dp', mates[m])  18.9 us
    ppermute x9, starting transfers between devices, over_tp(): return lax.ppermute(value, 'tp', levels[k])  18.5 us
    pallas_call x1, Pallas kernels, attn_back(): pl.pallas_call(functools.partial(attn_back_kernel, heads, cols // heads),...  17.7 us
    ppermute x23, starting transfers between devices, over_dp(): return lax.ppermute(value, 'dp', mates[m])  16.2 us
    pallas_call x1, Pallas kernels, ffn_back(): pl.pallas_call(ffn_back_kernel, grid_spec=pltpu.PrefetchScalarGridSpec(nu...  16 us
  transfers between devices with their start and end apart: 36, of which 14 were waited for; matrix products, arithmetic and copies ran while one was open for 8% of the time, Pallas kernels for 32%

profile of v1, /device:TPU:0, one launch (start us, length us, event | category | flops | bytes accessed | tf_op | source)
XLA Modules:
  0.0 287.9 jit_solution(14814375544965967549)
XLA Ops:
  11.3 3.0 %collective-permute-start = (bf16[112,768]{1,0:T(8,128)(2,1)S(1)}, bf16[112,768]{1,0:T(8,128)(2,1)S(1)}, u32[]{:S(2)}, u32[]{:S(2)}) collective-permute-start(bf16[112,768]{1,0:T(8,128)(2,1)S(1)} %get-tuple-element.63), channel_id=1, source_target_pairs={{0,1},{1,0},{2,3},{3,2},{4,5},{5,4},{6,7},{7,6},{8,9},{9,8},{10,11... | collective-permute-start | bytes 516104 | tf_op jit(solution)/shard_map/ppermute | solution.py:1159
  14.3 2.6 collective-permute-start.1
  18.7 2.7 fusion
  21.5 2.4 fusion.2.a1_ref
  24.7 5.2 %collective-permute-done.1.refs_1_ = bf16[112,768]{1,0:T(8,128)(2,1)S(1)} collective-permute-done((bf16[112,768]{1,0:T(8,128)(2,1)S(1)}, bf16[112,768]{1,0:T(8,128)(2,1)S(1)}, u32[]{:S(2)}, u32[]{:S(2)}) %collective-permute-start.1) | collective-permute-done | bytes 172064 | tf_op jit(solution)/shard_map/ppermute | solution.py:1159
  31.2 1.9 stack.1
  33.1 1.5 collective-permute-start.3
  34.6 1.5 collective-permute-start.4
  36.6 11.0 %attn_own.1 = (bf16[4,4,576,512]{3,2,1,0:T(8,128)(2,1)}, f32[4,4,3,512]{3,2,1,0:T(4,128)S(1)}, bf16[4,4,192,512]{3,2,1,0:T(8,128)(2,1)}) custom-call(bf16[2048,768]{1,0:T(8,128)(2,1)} %fusion.2.a1_ref, f32[1,3,512]{2,1,0:T(4,128)S(1)} %convolution_bitcast_fusion.vec_ref, s32[4,1,512]{2,1,0:T(1,128)S(1)} %broadcast_in_dim.54.seg_ref, ...), custom_call_target="tpu_custom_call" | custom-call | flops 10000000000 | bytes 1048576 | tf_op jit(solution)/shard_map/attn_own/pallas_call | solution.py:343
  47.7 5.3 %collective-permute-done.4.rest_4_ = bf16[3,96,768]{2,1,0:T(8,128)(2,1)} collective-permute-done((bf16[3,96,768]{2,1,0:T(8,128)(2,1)}, bf16[3,96,768]{2,1,0:T(8,128)(2,1)}, u32[]{:S(2)}, u32[]{:S(2)}) %collective-permute-start.4) | collective-permute-done | bytes 442400 | tf_op jit(solution)/shard_map/ppermute | solution.py:1156
  52.9 2.9 %others_of.1 = (bf16[3,96,768]{2,1,0:T(8,128)(2,1)}, bf16[3,96,768]{2,1,0:T(8,128)(2,1)}) custom-call(s32[4]{0:T(128)} %iota_xor_fusion.order_ref, bf16[4,192,768]{2,1,0:T(8,128)(2,1)} %bitcast.75), custom_call_target="tpu_custom_call" | custom-call | bytes 2359296 | tf_op jit(solution)/shard_map/others_of/pallas_call | solution.py:218
  63.7 32.5 %attn_far.1 = (bf16[4,4,576,512]{3,2,1,0:T(8,128)(2,1)}, f32[4,4,3,512]{3,2,1,0:T(4,128)S(1)}, bf16[4,4,192,512]{3,2,1,0:T(8,128)(2,1)}, bf16[4,768,768]{2,1,0:T(8,128)(2,1)}) custom-call(s32[8]{0:T(128)S(1)} %xor_multiply_fusion.1.place_ref, bf16[2048,768]{1,0:T(8,128)(2,1)} %fusion.2.a1_ref, ...), custom_call_target="tpu_custom_call", output_to_operand_aliasing={{0}: (13, {}), {1}: (14, {}), {2}: (15, {})} | custom-call | flops 30000001024 | bytes 1048576 | tf_op jit(solution)/shard_map/attn_far/pallas_call | solution.py:354
  97.4 13.6 %ffn_own.1 = (bf16[2048,768]{1,0:T(8,128)(2,1)}, bf16[2048,768]{1,0:T(8,128)(2,1)}, bf16[2048,768]{1,0:T(8,128)(2,1)}) custom-call(bf16[2048,768]{1,0:T(8,128)(2,1)} %x_ref.3, bf16[4,4,192,512]{3,2,1,0:T(8,128)(2,1)} %get-tuple-element.77.ctx_ref, bf16[4,768,768]{2,1,0:T(8,128)(2,1)} %get-tuple-element.78.wo_ref.w_ref, ...), custom_call_target="tpu_custom_call" | custom-call | flops 7247757312 | bytes 16777216 | tf_op jit(solution)/shard_map/ffn_own/pallas_call | solution.py:416
  111.8 11.5 %ffn_first.1 = (bf16[2048,768]{1,0:T(8,128)(2,1)}, bf16[512,768]{1,0:T(8,128)(2,1)}, f32[8,768]{1,0:T(8,128)S(1)}, bf16[3,768,768]{2,1,0:T(8,128)(2,1)}, bf16[3,768,768]{2,1,0:T(8,128)(2,1)}) custom-call(s32[8]{0:T(128)S(1)} %xor_multiply_fusion.1.place_ref, s32[4]{0:T(128)S(1)} %copy-done.2, bf16[2048,768]{1,0:T(8,128)(2,1)} %get-tuple-element.79.a2_ref, ...), custom_call_target="tpu_custom_call" | custom-call | flops 3623878656 | bytes 16777216 | tf_op jit(solution)/shard_map/ffn_first/pallas_call | solution.py:508
  123.3 4.2 %collective-permute-start.17 = (bf16[8,768]{1,0:T(8,128)(2,1)S(1)}, bf16[8,768]{1,0:T(8,128)(2,1)S(1)}, u32[]{:S(2)}, u32[]{:S(2)}) collective-permute-start(bf16[8,768]{1,0:T(8,128)(2,1)S(1)} %get-tuple-element.168), channel_id=1, source_target_pairs={{0,1},{1,0},{2,3},{3,2},{4,5},{5,4},{6,7},{7,6},{8,9},{9,8},{10,11... | collective-permute-start | bytes 36872 | tf_op jit(solution)/shard_map/ppermute | solution.py:1159
  127.5 2.9 collective-permute-start.18
  132.1 3.8 %collective-permute-done.19 = bf16[8,768]{1,0:T(8,128)(2,1)S(1)} collective-permute-done((bf16[8,768]{1,0:T(8,128)(2,1)S(1)}, bf16[8,768]{1,0:T(8,128)(2,1)S(1)}, u32[]{:S(2)}, u32[]{:S(2)}) %collective-permute-start.19) | collective-permute-done | bytes 12320 | tf_op jit(solution)/shard_map/ppermute | solution.py:1159
  142.0 2.0 collective-permute-done.22.refs_2_
  145.2 3.7 %loss_head.1 = (f32[32,768]{1,0:T(8,128)S(1)}, f32[96,768]{1,0:T(8,128)}, f32[1,768]{1,0:T(1,128)S(1)}) custom-call(s32[33]{0:T(128)S(1)} %pad_add_fusion.1.at_ref, bf16[64,768]{1,0:T(8,128)(2,1)S(1)} %constant_dynamic-update-slice_fusion.refs_0_, bf16[64,768]{1,0:T(8,128)(2,1)S(1)} %collective-permute-done.21.refs_1_, ...), custom_call_target="tpu_custom_call" | custom-call | flops 3000000000 | bytes 1048576 | tf_op jit(solution)/shard_map/loss_head/pallas_call | solution.py:611
  149.0 16.0 %ffn_back.1 = (f32[512,768]{1,0:T(8,128)}, bf16[512,768]{1,0:T(8,128)(2,1)S(1)}, bf16[4,192,512]{2,1,0:T(8,128)(2,1)S(1)}, f32[1,768]{1,0:T(1,128)S(1)}) custom-call(s32[1]{0:T(128)} %bitcast.row_ref, bf16[512,768]{1,0:T(8,128)(2,1)} %get-tuple-element.89.res_ref.own_ref, bf16[2048,768]{1,0:T(8,128)(2,1)} %get-tuple-element.80.mid_ref, ...), custom_call_target="tpu_custom_call" | custom-call | flops 12000000000 | bytes 16777216 | tf_op jit(solution)/shard_map/ffn_back/pallas_call | solution.py:723
  165.9 17.7 %attn_back.1 = (bf16[4,576,512]{2,1,0:T(8,128)(2,1)}, f32[4,3,8,768]{3,2,1,0:T(8,128)S(1)}, bf16[512,768]{1,0:T(8,128)(2,1)}, f32[1,768]{1,0:T(1,128)S(1)}) custom-call(s32[1]{0:T(128)} %bitcast.row_ref, bf16[4,4,576,512]{3,2,1,0:T(8,128)(2,1)} %get-tuple-element.95.qkv_ref, f32[4,4,3,512]{3,2,1,0:T(4,128)S(1)} %get-tuple-element.83.lse_ref, ...), custom_call_target="tpu_custom_call" | custom-call | flops 15000000512 | bytes 16777216 | tf_op jit(solution)/shard_map/attn_back/pallas_call | solution.py:879
  186.6 8.9 %attn_weights.1 = (bf16[4,4,112,768]{3,2,1,0:T(8,128)(2,1)}, bf16[4,4,112,768]{3,2,1,0:T(8,128)(2,1)}) custom-call(s32[6]{0:T(128)S(1)} %pad_add_fusion.place_ref, bf16[2048,768]{1,0:T(8,128)(2,1)} %fusion.2.a1_ref, bf16[512,768]{1,0:T(8,128)(2,1)S(1)} %get-tuple-element.94.dattn_ref, bf16[4,576,512]{2,1,0:T(8,128)(2,1)} %get-tuple-element.98.dqkv_ref, ...), custom_call_target="tpu_custom_call" | custom-call | flops 1000000 | bytes 1000000 | tf_op jit(solution)/shard_map/attn_weights/pallas_call | solution.py:976
  195.5 5.4 %collective-permute-done.24 = bf16[4,4,112,768]{3,2,1,0:T(8,128)(2,1)} collective-permute-done((bf16[4,4,112,768]{3,2,1,0:T(8,128)(2,1)}, bf16[4,4,112,768]{3,2,1,0:T(8,128)(2,1)}, u32[]{:S(2)}, u32[]{:S(2)}) %collective-permute-start.24) | collective-permute-done | bytes 2752544 | tf_op jit(solution)/shard_map/ppermute | solution.py:1156
  200.9 3.0 %fusion.14 = (bf16[4,112,768]{2,1,0:T(8,128)(2,1)S(1)}, bf16[4,112,768]{2,1,0:T(8,128)(2,1)S(1)}, bf16[4,112,768]{2,1,0:T(8,128)(2,1)S(1)}) fusion(bf16[4,4,112,768]{3,2,1,0:T(8,128)(2,1)} %collective-permute-done.24, bf16[4,4,112,768]{3,2,1,0:T(8,128)(2,1)} %get-tuple-element.102), kind=kLoop, calls=%fused_computation.62 | loop fusion | flops 5160960 | bytes 6193152 | tf_op jit(solution)/shard_map/convert_element_type | solution.py:1282
  203.9 1.8 collective-permute-start.27
  207.5 33.2 %ffn_tail.1 = (bf16[2048,768]{1,0:T(8,128)(2,1)}, bf16[4,2,96,768]{3,2,1,0:T(8,128)(2,1)}, bf16[4,2,96,768]{3,2,1,0:T(8,128)(2,1)}) custom-call(s32[6]{0:T(128)S(1)} %pad_add_fusion.place_ref, s32[4]{0:T(128)S(1)} %copy-done.2, bf16[2048,768]{1,0:T(8,128)(2,1)} %get-tuple-element.79.a2_ref, ...), custom_call_target="tpu_custom_call", output_to_operand_aliasing={{0}: (13, {})} | custom-call | flops 20000000000 | bytes 16777216 | tf_op jit(solution)/shard_map/ffn_tail/pallas_call | solution.py:1091
  240.8 1.9 fusion.17
  245.1 2.7 collective-permute-start.28
  249.2 3.5 %all-to-all-start = ((bf16[4,2,96,768]{3,2,1,0:T(8,128)(2,1)}), bf16[4,2,96,768]{3,2,1,0:T(8,128)(2,1)S(1)}, u32[]{:S(2)}, u32[]{:S(2)}) async-start(bf16[4,2,96,768]{3,2,1,0:T(8,128)(2,1)} %add_convert_fusion), calls=%async_computation | async-start | bytes 2359296 | tf_op jit(solution)/shard_map/all_to_all | solution.py:1305
  253.3 3.0 %collective-permute-done.30 = bf16[112,768]{1,0:T(8,128)(2,1)S(1)} collective-permute-done((bf16[112,768]{1,0:T(8,128)(2,1)}, bf16[112,768]{1,0:T(8,128)(2,1)S(1)}, u32[]{:S(2)}, u32[]{:S(2)}) %collective-permute-start.30) | collective-permute-done | bytes 172064 | tf_op jit(solution)/shard_map/ppermute | solution.py:1159
  256.4 15.6 %collective-permute-done.29 = bf16[112,768]{1,0:T(8,128)(2,1)S(1)} collective-permute-done((bf16[112,768]{1,0:T(8,128)(2,1)S(1)}, bf16[112,768]{1,0:T(8,128)(2,1)S(1)}, u32[]{:S(2)}, u32[]{:S(2)}) %collective-permute-start.29) | collective-permute-done | bytes 172064 | tf_op jit(solution)/shard_map/ppermute | solution.py:1159
  274.8 5.1 %convert_element_type.158 = f32[2048,768]{1,0:T(8,128)} convert(bf16[2048,768]{1,0:T(8,128)(2,1)} %all-gather.6.cloned.1.call-done) | non-fusion elementwise | flops 1572864 | bytes 9437184 | tf_op jit(solution)/shard_map/convert_element_type | solution.py:1249
  (178 shorter events, 40.9 us)
Async XLA Ops:
  7.2 45.7 %all-gather.8.cloned.1.call-start = ((), (), s32[]{:S(2)}) async-start(), calls=%async_computation.2 | async-start | bytes 1474560 | tf_op jit(solution)/shard_map/all_gather | solution.py:1189
  11.3 13.4 %collective-permute-start = (bf16[112,768]{1,0:T(8,128)(2,1)S(1)}, bf16[112,768]{1,0:T(8,128)(2,1)S(1)}, u32[]{:S(2)}, u32[]{:S(2)}) collective-permute-start(bf16[112,768]{1,0:T(8,128)(2,1)S(1)} %get-tuple-element.63), channel_id=1, source_target_pairs={{0,1},{1,0},{2,3},{3,2},{4,5},{5,4},{6,7},{7,6},{8,9},{9,8},{10,11... | collective-permute-start | bytes 516104 | tf_op jit(solution)/shard_map/ppermute | solution.py:1159
  14.3 15.6 %collective-permute-start.1 = (bf16[112,768]{1,0:T(8,128)(2,1)S(1)}, bf16[112,768]{1,0:T(8,128)(2,1)S(1)}, u32[]{:S(2)}, u32[]{:S(2)}) collective-permute-start(bf16[112,768]{1,0:T(8,128)(2,1)S(1)} %get-tuple-element.63), channel_id=1, source_target_pairs={{0,2},{1,3},{2,0},{3,1},{4,6},{5,7},{6,4},{7,5},{8,10},{9,11},{10,... | collective-permute-start | bytes 516104 | tf_op jit(solution)/shard_map/ppermute | solution.py:1159
  16.9 13.0 %collective-permute-start.2 = (bf16[112,768]{1,0:T(8,128)(2,1)S(1)}, bf16[112,768]{1,0:T(8,128)(2,1)S(1)}, u32[]{:S(2)}, u32[]{:S(2)}) collective-permute-start(bf16[112,768]{1,0:T(8,128)(2,1)S(1)} %get-tuple-element.63), channel_id=1, source_target_pairs={{0,3},{1,2},{2,1},{3,0},{4,7},{5,6},{6,5},{7,4},{8,11},{9,10},{10,... | collective-permute-start | bytes 516104 | tf_op jit(solution)/shard_map/ppermute | solution.py:1159
  18.6 93.2 %all-gather.10.cloned.1.call-start = ((), (), s32[]{:S(2)}) async-start(), calls=%async_computation.3 | async-start | bytes 3981312 | tf_op jit(solution)/shard_map/all_gather | solution.py:1205
  33.1 14.5 %collective-permute-start.3 = (bf16[3,96,768]{2,1,0:T(8,128)(2,1)}, bf16[3,96,768]{2,1,0:T(8,128)(2,1)S(1)}, u32[]{:S(2)}, u32[]{:S(2)}) collective-permute-start(bf16[3,96,768]{2,1,0:T(8,128)(2,1)} %get-tuple-element.73.rest_0_), channel_id=1, source_target_pairs={{0,8},{4,12},{8,0},{12,4},{16,24},{20,28},{24,16},{28,20},{1,9},{5... | collective-permute-start | bytes 1327112 | tf_op jit(solution)/shard_map/ppermute | solution.py:1156
  34.6 18.3 %collective-permute-start.4 = (bf16[3,96,768]{2,1,0:T(8,128)(2,1)}, bf16[3,96,768]{2,1,0:T(8,128)(2,1)}, u32[]{:S(2)}, u32[]{:S(2)}) collective-permute-start(bf16[3,96,768]{2,1,0:T(8,128)(2,1)} %get-tuple-element.73.rest_0_), channel_id=1, source_target_pairs={{0,16},{4,20},{8,24},{12,28},{16,0},{20,4},{24,8},{28,12},{1,17},{... | collective-permute-start | bytes 1327112 | tf_op jit(solution)/shard_map/ppermute | solution.py:1156
  36.1 16.8 %collective-permute-start.5 = (bf16[3,96,768]{2,1,0:T(8,128)(2,1)}, bf16[3,96,768]{2,1,0:T(8,128)(2,1)}, u32[]{:S(2)}, u32[]{:S(2)}) collective-permute-start(bf16[3,96,768]{2,1,0:T(8,128)(2,1)} %get-tuple-element.73.rest_0_), channel_id=1, source_target_pairs={{0,24},{4,28},{8,16},{12,20},{16,8},{20,12},{24,0},{28,4},{1,25},{... | collective-permute-start | bytes 1327112 | tf_op jit(solution)/shard_map/ppermute | solution.py:1156
  55.9 218.9 %all-gather.6.cloned.1.call-start = ((), (), s32[]{:S(2)}) async-start(), calls=%async_computation.1 | async-start | bytes 3932160 | tf_op jit(solution)/shard_map/all_gather | solution.py:1249
  56.9 3.3 %collective-permute-start.9 = (bf16[3,96,768]{2,1,0:T(8,128)(2,1)}, bf16[3,96,768]{2,1,0:T(8,128)(2,1)S(1)}, u32[]{:S(2)}, u32[]{:S(2)}) collective-permute-start(bf16[3,96,768]{2,1,0:T(8,128)(2,1)} %collective-permute-done.5.rest_6_), channel_id=1, source_target_pairs={{0,4},{4,0},{8,12},{12,8},{16,20},{20,16},{24,28},{28,24},{1,5},{5... | collective-permute-start | bytes 1327112 | tf_op jit(solution)/shard_map/ppermute | solution.py:1156
  60.2 36.0 %collective-permute-start.10 = (bf16[3,96,768]{2,1,0:T(8,128)(2,1)}, bf16[3,96,768]{2,1,0:T(8,128)(2,1)S(1)}, u32[]{:S(2)}, u32[]{:S(2)}) collective-permute-start(bf16[3,96,768]{2,1,0:T(8,128)(2,1)} %get-tuple-element.84.rest_0_), channel_id=1, source_target_pairs={{0,8},{4,12},{8,0},{12,4},{16,24},{20,28},{24,16},{28,20},{1,9},{5... | collective-permute-start | bytes 1327112 | tf_op jit(solution)/shard_map/ppermute | solution.py:1156
  61.5 34.8 %collective-permute-start.11 = (bf16[3,96,768]{2,1,0:T(8,128)(2,1)}, bf16[3,96,768]{2,1,0:T(8,128)(2,1)S(1)}, u32[]{:S(2)}, u32[]{:S(2)}) collective-permute-start(bf16[3,96,768]{2,1,0:T(8,128)(2,1)} %get-tuple-element.84.rest_0_), channel_id=1, source_target_pairs={{0,16},{4,20},{8,24},{12,28},{16,0},{20,4},{24,8},{28,12},{1,17},{... | collective-permute-start | bytes 1327112 | tf_op jit(solution)/shard_map/ppermute | solution.py:1156
  62.3 34.0 %collective-permute-start.12 = (bf16[3,96,768]{2,1,0:T(8,128)(2,1)}, bf16[3,96,768]{2,1,0:T(8,128)(2,1)S(1)}, u32[]{:S(2)}, u32[]{:S(2)}) collective-permute-start(bf16[3,96,768]{2,1,0:T(8,128)(2,1)} %get-tuple-element.84.rest_0_), channel_id=1, source_target_pairs={{0,24},{4,28},{8,16},{12,20},{16,8},{20,12},{24,0},{28,4},{1,25},{... | collective-permute-start | bytes 1327112 | tf_op jit(solution)/shard_map/ppermute | solution.py:1156
  96.3 14.7 %collective-permute-start.13 = (bf16[3,96,768]{2,1,0:T(8,128)(2,1)S(1)}, bf16[3,96,768]{2,1,0:T(8,128)(2,1)S(1)}, u32[]{:S(2)}, u32[]{:S(2)}) collective-permute-start(bf16[3,96,768]{2,1,0:T(8,128)(2,1)S(1)} %copy-done), channel_id=1, source_target_pairs={{0,4},{4,0},{8,12},{12,8},{16,20},{20,16},{24,28},{28,24},{1,5},{5... | collective-permute-start | bytes 1327112 | tf_op jit(solution)/shard_map/ppermute | solution.py:1156
  96.3 14.7 %collective-permute-start.14 = (bf16[3,96,768]{2,1,0:T(8,128)(2,1)S(1)}, bf16[3,96,768]{2,1,0:T(8,128)(2,1)S(1)}, u32[]{:S(2)}, u32[]{:S(2)}) collective-permute-start(bf16[3,96,768]{2,1,0:T(8,128)(2,1)S(1)} %collective-permute-done.10.rest_2_), channel_id=1, source_target_pairs={{0,4},{4,0},{8,12},{12,8},{16,20},{20,16},{24,28},{28,24},{1,5},{5... | collective-permute-start | bytes 1327112 | tf_op jit(solution)/shard_map/ppermute | solution.py:1156
  96.8 14.2 %collective-permute-start.15 = (bf16[3,96,768]{2,1,0:T(8,128)(2,1)S(1)}, bf16[3,96,768]{2,1,0:T(8,128)(2,1)S(1)}, u32[]{:S(2)}, u32[]{:S(2)}) collective-permute-start(bf16[3,96,768]{2,1,0:T(8,128)(2,1)S(1)} %collective-permute-done.11.rest_4_), channel_id=1, source_target_pairs={{0,4},{4,0},{8,12},{12,8},{16,20},{20,16},{24,28},{28,24},{1,5},{5... | collective-permute-start | bytes 1327112 | tf_op jit(solution)/shard_map/ppermute | solution.py:1156
  96.9 14.9 %collective-permute-start.16 = (bf16[3,96,768]{2,1,0:T(8,128)(2,1)S(1)}, bf16[3,96,768]{2,1,0:T(8,128)(2,1)}, u32[]{:S(2)}, u32[]{:S(2)}) collective-permute-start(bf16[3,96,768]{2,1,0:T(8,128)(2,1)S(1)} %collective-permute-done.12.rest_6_), channel_id=1, source_target_pairs={{0,4},{4,0},{8,12},{12,8},{16,20},{20,16},{24,28},{28,24},{1,5},{5... | collective-permute-start | bytes 1327112 | tf_op jit(solution)/shard_map/ppermute | solution.py:1156
  123.3 8.8 %collective-permute-start.17 = (bf16[8,768]{1,0:T(8,128)(2,1)S(1)}, bf16[8,768]{1,0:T(8,128)(2,1)S(1)}, u32[]{:S(2)}, u32[]{:S(2)}) collective-permute-start(bf16[8,768]{1,0:T(8,128)(2,1)S(1)} %get-tuple-element.168), channel_id=1, source_target_pairs={{0,1},{1,0},{2,3},{3,2},{4,5},{5,4},{6,7},{7,6},{8,9},{9,8},{10,11... | collective-permute-start | bytes 36872 | tf_op jit(solution)/shard_map/ppermute | solution.py:1159
  127.5 4.6 %collective-permute-start.18 = (bf16[8,768]{1,0:T(8,128)(2,1)S(1)}, bf16[8,768]{1,0:T(8,128)(2,1)S(1)}, u32[]{:S(2)}, u32[]{:S(2)}) collective-permute-start(bf16[8,768]{1,0:T(8,128)(2,1)S(1)} %get-tuple-element.168), channel_id=1, source_target_pairs={{0,2},{1,3},{2,0},{3,1},{4,6},{5,7},{6,4},{7,5},{8,10},{9,11},{10,... | collective-permute-start | bytes 36872 | tf_op jit(solution)/shard_map/ppermute | solution.py:1159
  130.4 5.5 %collective-permute-start.19 = (bf16[8,768]{1,0:T(8,128)(2,1)S(1)}, bf16[8,768]{1,0:T(8,128)(2,1)S(1)}, u32[]{:S(2)}, u32[]{:S(2)}) collective-permute-start(bf16[8,768]{1,0:T(8,128)(2,1)S(1)} %get-tuple-element.168), channel_id=1, source_target_pairs={{0,3},{1,2},{2,1},{3,0},{4,7},{5,6},{6,5},{7,4},{8,11},{9,10},{10,... | collective-permute-start | bytes 36872 | tf_op jit(solution)/shard_map/ppermute | solution.py:1159
  137.2 4.9 %collective-permute-start.21 = (bf16[64,768]{1,0:T(8,128)(2,1)S(1)}, bf16[64,768]{1,0:T(8,128)(2,1)S(1)}, u32[]{:S(2)}, u32[]{:S(2)}) collective-permute-start(bf16[64,768]{1,0:T(8,128)(2,1)S(1)} %constant_dynamic-update-slice_fusion.refs_0_), channel_id=1, source_target_pairs={{0,8},{4,12},{8,0},{12,4},{16,24},{20,28},{24,16},{28,20},{1,9},{5... | collective-permute-start | bytes 294920 | tf_op jit(solution)/shard_map/ppermute | solution.py:1156
  138.5 5.5 %collective-permute-start.22 = (bf16[64,768]{1,0:T(8,128)(2,1)S(1)}, bf16[64,768]{1,0:T(8,128)(2,1)S(1)}, u32[]{:S(2)}, u32[]{:S(2)}) collective-permute-start(bf16[64,768]{1,0:T(8,128)(2,1)S(1)} %constant_dynamic-update-slice_fusion.refs_0_), channel_id=1, source_target_pairs={{0,16},{4,20},{8,24},{12,28},{16,0},{20,4},{24,8},{28,12},{1,17},{... | collective-permute-start | bytes 294920 | tf_op jit(solution)/shard_map/ppermute | solution.py:1156
  139.7 5.5 %collective-permute-start.23 = (bf16[64,768]{1,0:T(8,128)(2,1)S(1)}, bf16[64,768]{1,0:T(8,128)(2,1)S(1)}, u32[]{:S(2)}, u32[]{:S(2)}) collective-permute-start(bf16[64,768]{1,0:T(8,128)(2,1)S(1)} %constant_dynamic-update-slice_fusion.refs_0_), channel_id=1, source_target_pairs={{0,24},{4,28},{8,16},{12,20},{16,8},{20,12},{24,0},{28,4},{1,25},{... | collective-permute-start | bytes 294920 | tf_op jit(solution)/shard_map/ppermute | solution.py:1156
  195.5 5.4 %collective-permute-start.24 = (bf16[4,4,112,768]{3,2,1,0:T(8,128)(2,1)}, bf16[4,4,112,768]{3,2,1,0:T(8,128)(2,1)}, u32[]{:S(2)}, u32[]{:S(2)}) collective-permute-start(bf16[4,4,112,768]{3,2,1,0:T(8,128)(2,1)} %get-tuple-element.103), channel_id=1, source_target_pairs={{0,4},{4,0},{8,12},{12,8},{16,20},{20,16},{24,28},{28,24},{1,5},{5... | collective-permute-start | bytes 8257544 | tf_op jit(solution)/shard_map/ppermute | solution.py:1156
  203.9 36.8 %collective-permute-start.27 = (bf16[4,112,768]{2,1,0:T(8,128)(2,1)S(1)}, bf16[4,112,768]{2,1,0:T(8,128)(2,1)S(1)}, u32[]{:S(2)}, u32[]{:S(2)}) collective-permute-start(bf16[4,112,768]{2,1,0:T(8,128)(2,1)S(1)} %get-tuple-element.171), channel_id=1, source_target_pairs={{0,24},{4,28},{8,16},{12,20},{16,8},{20,12},{24,0},{28,4},{1,25},{... | collective-permute-start | bytes 2064392 | tf_op jit(solution)/shard_map/ppermute | solution.py:1156
  205.7 35.0 %collective-permute-start.26 = (bf16[4,112,768]{2,1,0:T(8,128)(2,1)S(1)}, bf16[4,112,768]{2,1,0:T(8,128)(2,1)S(1)}, u32[]{:S(2)}, u32[]{:S(2)}) collective-permute-start(bf16[4,112,768]{2,1,0:T(8,128)(2,1)S(1)} %get-tuple-element.170), channel_id=1, source_target_pairs={{0,16},{4,20},{8,24},{12,28},{16,0},{20,4},{24,8},{28,12},{1,17},{... | collective-permute-start | bytes 2064392 | tf_op jit(solution)/shard_map/ppermute | solution.py:1156
  206.6 34.1 %collective-permute-start.25 = (bf16[4,112,768]{2,1,0:T(8,128)(2,1)S(1)}, bf16[4,112,768]{2,1,0:T(8,128)(2,1)S(1)}, u32[]{:S(2)}, u32[]{:S(2)}) collective-permute-start(bf16[4,112,768]{2,1,0:T(8,128)(2,1)S(1)} %get-tuple-element.169), channel_id=1, source_target_pairs={{0,8},{4,12},{8,0},{12,4},{16,24},{20,28},{24,16},{28,20},{1,9},{5... | collective-permute-start | bytes 2064392 | tf_op jit(solution)/shard_map/ppermute | solution.py:1156
  240.7 7.1 %collective-permute-start.31 = (bf16[4,2,96,768]{3,2,1,0:T(8,128)(2,1)}, bf16[4,2,96,768]{3,2,1,0:T(8,128)(2,1)S(1)}, u32[]{:S(2)}, u32[]{:S(2)}) collective-permute-start(bf16[4,2,96,768]{3,2,1,0:T(8,128)(2,1)} %get-tuple-element.110), channel_id=1, source_target_pairs={{0,4},{4,0},{8,12},{12,8},{16,20},{20,16},{24,28},{28,24},{1,5},{5... | collective-permute-start | bytes 3538952 | tf_op jit(solution)/shard_map/ppermute | solution.py:1156
  243.4 12.9 %collective-permute-start.30 = (bf16[112,768]{1,0:T(8,128)(2,1)}, bf16[112,768]{1,0:T(8,128)(2,1)S(1)}, u32[]{:S(2)}, u32[]{:S(2)}) collective-permute-start(bf16[112,768]{1,0:T(8,128)(2,1)} %get-tuple-element.173), channel_id=1, source_target_pairs={{0,3},{1,2},{2,1},{3,0},{4,7},{5,6},{6,5},{7,4},{8,11},{9,10},{10,... | collective-permute-start | bytes 516104 | tf_op jit(solution)/shard_map/ppermute | solution.py:1159
  244.7 27.2 %collective-permute-start.29 = (bf16[112,768]{1,0:T(8,128)(2,1)S(1)}, bf16[112,768]{1,0:T(8,128)(2,1)S(1)}, u32[]{:S(2)}, u32[]{:S(2)}) collective-permute-start(bf16[112,768]{1,0:T(8,128)(2,1)S(1)} %get-tuple-element.174), channel_id=1, source_target_pairs={{0,2},{1,3},{2,0},{3,1},{4,6},{5,7},{6,4},{7,5},{8,10},{9,11},{10,... | collective-permute-start | bytes 516104 | tf_op jit(solution)/shard_map/ppermute | solution.py:1159
  245.1 26.8 %collective-permute-start.28 = (bf16[112,768]{1,0:T(8,128)(2,1)S(1)}, bf16[112,768]{1,0:T(8,128)(2,1)S(1)}, u32[]{:S(2)}, u32[]{:S(2)}) collective-permute-start(bf16[112,768]{1,0:T(8,128)(2,1)S(1)} %get-tuple-element.172), channel_id=1, source_target_pairs={{0,1},{1,0},{2,3},{3,2},{4,5},{5,4},{6,7},{7,6},{8,9},{9,8},{10,11... | collective-permute-start | bytes 516104 | tf_op jit(solution)/shard_map/ppermute | solution.py:1159
  249.2 30.7 %all-to-all-start = ((bf16[4,2,96,768]{3,2,1,0:T(8,128)(2,1)}), bf16[4,2,96,768]{3,2,1,0:T(8,128)(2,1)S(1)}, u32[]{:S(2)}, u32[]{:S(2)}) async-start(bf16[4,2,96,768]{3,2,1,0:T(8,128)(2,1)} %add_convert_fusion), calls=%async_computation | async-start | bytes 2359296 | tf_op jit(solution)/shard_map/all_to_all | solution.py:1305
  (34 other events, 244.2 us)
Sparse Core Ops, SparseCore 0:
  18.7 32.7 all-gather.7
  56.0 48.9 all-gather.9
  195.6 75.2 all-gather.5

commit v2 on v1

--- a/solution.py
+++ b/solution.py
@@ -68,29 +68,34 @@
 
 
 def bring(place_ref, piece_refs, into, sems):
-    slices = piece_refs[0].shape[-2]
+    width = into.shape[1]
+    slices = width // len(piece_refs)
     copies = []
     for m, piece in enumerate(piece_refs):
         start = pl.multiple_of(place_ref[m], 16) if slices % 16 == 0 else place_ref[m]
-        copy = pltpu.make_async_copy(piece, into.at[:, pl.ds(start, slices), :], sems.at[m])
+        if len(piece.shape) == 2:
+            piece, to = piece.at[pl.ds(0, slices)], into.at[0, pl.ds(start, slices)]
+        else:
+            to = into.at[:, pl.ds(start, slices), :]
+        copy = pltpu.make_async_copy(piece, to, sems.at[m])
         copy.start()
         copies.append(copy)
     return copies
 
 
-def spread_bias(vec_ref, bias_s, heads):
+def spread_bias(vec_ref, bias_s, heads, at=0):
     for h in range(heads):
         wide = jnp.broadcast_to(vec_ref[0, h : h + 1, :], (TILE, 4 * TILE))
-        bias_s[h] = pltpu.roll(wide, 0, 1, stride=1, stride_axis=0)
-
-
-def with_bias(tile, offset, h, bias_s, vec_ref):
+        bias_s[at + h] = pltpu.roll(wide, 0, 1, stride=1, stride_axis=0)
+
+
+def with_bias(tile, offset, h, bias_s, vec_ref, first=0):
     if offset == 0:
-        return tile + bias_s[h, :, 0:TILE]
+        return tile + bias_s[first + h, :, 0:TILE]
     if offset == 1:
-        return tile + bias_s[h, :, 3 * TILE : 4 * TILE]
+        return tile + bias_s[first + h, :, 3 * TILE : 4 * TILE]
     if offset == -1:
-        return tile + bias_s[h, :, TILE : 2 * TILE]
+        return tile + bias_s[first + h, :, TILE : 2 * TILE]
     lane = 2 * TILE + 1 if offset > 1 else 2 * TILE - 1
     return tile + vec_ref[0, h : h + 1, lane : lane + 1]
 
@@ -229,23 +234,16 @@
     )(order, everything)
 
 
-def attend_row(heads, hd, weights, a1_ref, vec_ref, seg_ref, qkv_ref, lse_ref, ctx_ref, bias_s):
+def attend_row(heads, hd, weights, a1_ref, vec_ref, seg_ref, qkv_s, lse_s, ctx_ref, bias_s, first):
     length = a1_ref.shape[0]
     blocks = length // TILE
-
-    @pl.when(pl.program_id(1) == 0)
-    def _():
-        spread_bias(vec_ref, bias_s, heads)
-
-    qkv_ref[0, 0] = dg(weights, a1_ref[...], NT).astype(bf16)
+    qkv_s[...] = dg(weights, a1_ref[...], NT).astype(bf16)
     q_mask, k_mask = masks(seg_ref[0])
     ones = jnp.ones((16, length), bf16)
     for h in range(heads):
-        q_t = jnp.concatenate([qkv_ref[0, 0, h * hd : (h + 1) * hd], q_mask], 0)
-        k_t = jnp.concatenate([qkv_ref[0, 0, (heads + h) * hd : (heads + h + 1) * hd], k_mask], 0)
-        v_t = jnp.concatenate(
-            [qkv_ref[0, 0, (2 * heads + h) * hd : (2 * heads + h + 1) * hd], ones], 0
-        )
+        q_t = jnp.concatenate([qkv_s[h * hd : (h + 1) * hd], q_mask], 0)
+        k_t = jnp.concatenate([qkv_s[(heads + h) * hd : (heads + h + 1) * hd], k_mask], 0)
+        v_t = jnp.concatenate([qkv_s[(2 * heads + h) * hd : (2 * heads + h + 1) * hd], ones], 0)
         scores = dg(k_t.T, q_t, NN)
         columns = []
         tops = []
@@ -257,6 +255,7 @@
                     h,
                     bias_s,
                     vec_ref,
+                    first,
                 )
                 for j in range(blocks)
             ]
@@ -265,113 +264,121 @@
             columns.append(jnp.concatenate([jnp.exp(t - top).astype(bf16) for t in tiles], 0))
         mixed = dg(v_t, jnp.concatenate(columns, 1), NN)
         total = mixed[hd : hd + 1]
-        lse_ref[0, 0, h : h + 1, :] = jnp.concatenate(tops, 1) + jnp.log(total)
+        lse_s[h : h + 1, :] = jnp.concatenate(tops, 1) + jnp.log(total)
         ctx_ref[0, 0, h * hd : (h + 1) * hd, :] = (mixed[:hd] / total).astype(bf16)
 
 
-def attn_own_kernel(heads, hd, a1_ref, vec_ref, seg_ref, w_ref, *rest):
-    attend_row(heads, hd, w_ref[: 3 * heads * hd], a1_ref, vec_ref, seg_ref, *rest)
-
-
-def attn_far_kernel(heads, hd, count, place_ref, a1_ref, vec_ref, seg_ref, own_ref, *rest):
-    pieces = rest[:count]
-    qkv_ref, lse_ref, ctx_ref, sorted_ref, bias_s, w_s, sems, out_sems = rest[count + 3 :]
-    s, r = pl.program_id(0), pl.program_id(1)
-    keep = [
-        pltpu.make_async_copy(own_ref, sorted_ref.at[0], out_sems.at[0]),
-        pltpu.make_async_copy(w_s, sorted_ref.at[pl.ds(1, w_s.shape[0])], out_sems.at[1]),
-    ]
-
-    @pl.when((s == 0) & (r == 0))
+def attn_kernel(heads, hd, n, low, keeps, place_ref, order_ref, a1_ref, vec_ref, seg_ref, *rest):
+    sources = rest[: max(n, 1)]
+    rest = rest[max(n, 1) + (0 if low == 0 else 4 if keeps else 1) :]
+    if keeps:
+        qkv_ref, lse_ref, ctx_ref, sorted_ref, bias_s, qkv_s, lse_s, w_s, sems, out_sem = rest
+    else:
+        ctx_ref, bias_s, qkv_s, lse_s = rest
+    r, s = pl.program_id(0), pl.program_id(1)
+    first = s * heads
+
+    @pl.when(r == 0)
     def _():
-        for copy in bring(place_ref, pieces, w_s, sems):
-            copy.wait()
-        for copy in keep:
-            copy.start()
-
+        spread_bias(vec_ref, bias_s, heads, first)
+
+    if keeps:
+        count = w_s.shape[0]
+        source = w_s if n else sources[0]
+        into = sorted_ref.at[pl.ds(low, count)] if n else sorted_ref.at[low]
+        keep = pltpu.make_async_copy(source, into, out_sem)
+
+        @pl.when((s == 0) & (r == 0))
+        def _():
+            if n:
+                for copy in bring(place_ref, sources, w_s, sems):
+                    copy.wait()
+            keep.start()
+
+        weights = w_s[s, : 3 * heads * hd] if n else sources[0][: 3 * heads * hd]
+    else:
+        weights = sources[0][s, : 3 * heads * hd]
     attend_row(
-        heads,
-        hd,
-        w_s[s, : 3 * heads * hd],
-        a1_ref,
-        vec_ref,
-        seg_ref,
-        qkv_ref,
-        lse_ref,
-        ctx_ref,
-        bias_s,
-    )
-
-    @pl.when((s == pl.num_programs(0) - 1) & (r == pl.num_programs(1) - 1))
-    def _():
-        for copy in keep:
-            copy.wait()
-
-
-def attention(a1, own_a, vecs, segs, slots, place=None, pieces=None, earlier=None):
+        heads, hd, weights, a1_ref, vec_ref, seg_ref, qkv_s, lse_s, ctx_ref, bias_s, first
+    )
+    if keeps:
+
+        @pl.when(r == 0)
+        def _():
+            qkv_ref[0] = qkv_s[...]
+            lse_ref[0] = lse_s[...]
+
+        @pl.when((s == pl.num_programs(1) - 1) & (r == pl.num_programs(0) - 1))
+        def _():
+            keep.wait()
+
+
+def attention(name, a1, vecs, segs, place, order, low, first_row, n_rows, weights, chain):
     rows, _, length = segs.shape
     width = a1.shape[1]
-    heads = vecs.shape[1]
+    count, heads, _ = vecs.shape
+    slots = order.shape[0]
     hd = width // (4 * heads)
     cols = heads * hd
-    first = slots - vecs.shape[0] if pieces else 0
-    count = slots - 1 if pieces else 1
+    n = len(weights) if weights[0].shape[0] != slots and len(weights) > 1 else 0
+    keeps = first_row == 0
     anywhere = pl.BlockSpec(memory_space=pl.ANY)
-    in_specs = [
-        pl.BlockSpec((length, width), lambda s, r, *_: (r, 0)),
-        pl.BlockSpec((1, heads, 4 * TILE), lambda s, r, *_: (s + (1 if pieces else 0), 0, 0)),
-        pl.BlockSpec((1, 1, length), lambda s, r, *_: (r, 0, 0)),
-    ]
-    at = 1 if pieces else 0
+    at = lambda r, o: o[r + first_row]
+    slot = lambda r, s: low + jnp.where(r == 0, s, count - 1)
+    if n:
+        w_specs = [anywhere] * n
+    elif keeps:
+        w_specs = [pl.BlockSpec((width, width), lambda r, s, p, o: (0, 0))]
+    else:
+        w_specs = [pl.BlockSpec((count, width, width), lambda r, s, p, o: (low // count, 0, 0))]
     out_specs = [
-        pl.BlockSpec((1, 1, 3 * cols, length), lambda s, r, *_: (s + at, r, 0, 0)),
-        pl.BlockSpec((1, 1, heads, length), lambda s, r, *_: (s + at, r, 0, 0)),
-        pl.BlockSpec((1, 1, cols, length), lambda s, r, *_: (s + at, r, 0, 0)),
+        pl.BlockSpec((1, 3 * cols, length), lambda r, s, p, o: (slot(r, s), 0, 0)),
+        pl.BlockSpec((1, heads, length), lambda r, s, p, o: (slot(r, s), 0, 0)),
+        pl.BlockSpec((1, 1, cols, length), lambda r, s, p, o: (s + low, at(r, o), 0, 0)),
+        anywhere,
     ]
     out_shape = [
-        jax.ShapeDtypeStruct((slots, rows, 3 * cols, length), bf16),
-        jax.ShapeDtypeStruct((slots, rows, heads, length), f32),
+        jax.ShapeDtypeStruct((slots, 3 * cols, length), bf16),
+        jax.ShapeDtypeStruct((slots, heads, length), f32),
         jax.ShapeDtypeStruct((slots, rows, cols, length), bf16),
+        jax.ShapeDtypeStruct((slots, width, width), bf16),
     ]
-    scratch = [pltpu.VMEM((heads, TILE, 4 * TILE), f32)]
-    steps = count * rows
-    common = dict(
+    scratch = [
+        pltpu.VMEM((count * heads, TILE, 4 * TILE), f32),
+        pltpu.VMEM((3 * cols, length), bf16),
+        pltpu.VMEM((heads, length), f32),
+    ]
+    if keeps:
+        scratch += [
+            pltpu.VMEM((count, width, width) if n else (1, 16, TILE), bf16),
+            pltpu.SemaphoreType.DMA((max(n, 1),)),
+            pltpu.SemaphoreType.DMA(()),
+        ]
+        linked = [] if chain is None else list(chain)
+    else:
+        out_specs, out_shape, linked = out_specs[2:3], out_shape[2:3], [chain[2]]
+    base = 5 + len(w_specs)
+    return pl.pallas_call(
+        functools.partial(attn_kernel, heads, hd, n, low, keeps),
+        grid_spec=pltpu.PrefetchScalarGridSpec(
+            num_scalar_prefetch=2,
+            grid=(n_rows, count),
+            in_specs=[
+                pl.BlockSpec((length, width), lambda r, s, p, o: (at(r, o), 0)),
+                pl.BlockSpec((1, heads, 4 * TILE), lambda r, s, p, o: (s, 0, 0)),
+                pl.BlockSpec((1, 1, length), lambda r, s, p, o: (at(r, o), 0, 0)),
+            ]
+            + w_specs
+            + [anywhere] * len(linked),
+            out_specs=out_specs,
+            scratch_shapes=scratch,
+        ),
+        out_shape=out_shape,
+        input_output_aliases={base + i: i for i in range(len(linked))},
         compiler_params=pltpu.CompilerParams(vmem_limit_bytes=VMEM),
-        cost_estimate=cost(steps * 2.5 * 10**9, 2**20),
-    )
-    if not pieces:
-        return pl.pallas_call(
-            functools.partial(attn_own_kernel, heads, hd),
-            grid=(count, rows),
-            in_specs=in_specs + [pl.BlockSpec((width, width), lambda s, r: (0, 0))],
-            out_specs=out_specs,
-            out_shape=out_shape,
-            scratch_shapes=scratch,
-            name="attn_own",
-            **common,
-        )(a1, vecs, segs, own_a)
-    n = len(pieces)
-    return pl.pallas_call(
-        functools.partial(attn_far_kernel, heads, hd, n),
-        grid_spec=pltpu.PrefetchScalarGridSpec(
-            num_scalar_prefetch=1,
-            grid=(count, rows),
-            in_specs=in_specs
-            + [pl.BlockSpec((width, width), lambda s, r, p: (0, 0))]
-            + [anywhere] * (n + 3),
-            out_specs=out_specs + [anywhere],
-            scratch_shapes=scratch
-            + [
-                pltpu.VMEM((count, width, width), bf16),
-                pltpu.SemaphoreType.DMA((n,)),
-                pltpu.SemaphoreType.DMA((2,)),
-            ],
-        ),
-        out_shape=out_shape + [jax.ShapeDtypeStruct((slots, width, width), bf16)],
-        input_output_aliases={5 + n: 0, 6 + n: 1, 7 + n: 2},
-        name="attn_far",
-        **common,
-    )(place, a1, vecs, segs, own_a, *pieces, *earlier)
+        cost_estimate=cost(n_rows * count * 2.5 * 10**9, 2**20),
+        name=name,
+    )(place, order, a1, vecs, segs, *weights, *linked)
 
 
 GELU_A = math.sqrt(2.0 / math.pi)
@@ -573,67 +580,6 @@
     return d_proj, d_pooled, d_gain
 
 
-def loss_kernel(count, at_ref, *refs):
-    pieces, rest = refs[:count], refs[count:]
-    project_ref, pc_ref, pr_ref, gain_ref, dpool_ref, dproj_ref, dgain_ref, a_s, b_s = rest
-    each = SEG_ROW
-    parts = pieces[0].shape[0] // each
-    for m, piece in enumerate(pieces):
-        value = piece[...].astype(f32)
-        for part in range(parts):
-            start = pl.multiple_of(at_ref[1 + m * parts + part] * each, each)
-            a_s[pl.ds(start, each), :] = value[part * each : (part + 1) * each]
-    pooled = a_s[...].astype(bf16)
-    d_proj, d_pooled, d_gain = loss_math(
-        pooled, project_ref[...], pc_ref[...], pr_ref[...], gain_ref[...]
-    )
-    a_s[...] = d_pooled
-    b_s[...] = dg(pooled, d_proj, TN)
-    here = dpool_ref.shape[0]
-    block = dproj_ref.shape[0]
-    dpool_ref[...] = a_s[pl.ds(pl.multiple_of(at_ref[0] * here, here), here), :]
-    dproj_ref[...] = b_s[pl.ds(pl.multiple_of(at_ref[0] * block, block), block), :]
-    dgain_ref[...] = d_gain
-
-
-def loss_head(at, pieces, project, pairs, gain, here, block):
-    slots = sum(piece.shape[0] for piece in pieces)
-    width = project.shape[0]
-    pair_col = pairs[:, None]
-    pair_row = pairs[None, :]
-    if len(pieces) == 1:
-        pooled = pieces[0]
-        d_proj, d_pooled, d_gain = loss_math(pooled, project, pair_col, pair_row, gain)
-        own_cols = lax.dynamic_slice_in_dim(pooled, at[0] * block, block, 1)
-        d_pooled = lax.dynamic_slice_in_dim(d_pooled, at[0] * here, here, 0)
-        return d_pooled, dg(own_cols, d_proj, TN), d_gain
-    full = lambda shape: pl.BlockSpec(shape, lambda i, at: (0, 0))
-    return pl.pallas_call(
-        functools.partial(loss_kernel, len(pieces)),
-        grid_spec=pltpu.PrefetchScalarGridSpec(
-            num_scalar_prefetch=1,
-            grid=(1,),
-            in_specs=[full(piece.shape) for piece in pieces]
-            + [
-                full(project.shape),
-                full((slots, 1)),
-                full((1, slots)),
-                full((1, width)),
-            ],
-            out_specs=[full((here, width)), full((block, width)), full((1, width))],
-            scratch_shapes=[pltpu.VMEM((slots, width), f32), pltpu.VMEM((width, width), f32)],
-        ),
-        out_shape=[
-            jax.ShapeDtypeStruct((here, width), f32),
-            jax.ShapeDtypeStruct((block, width), f32),
-            jax.ShapeDtypeStruct((1, width), f32),
-        ],
-        compiler_params=pltpu.CompilerParams(vmem_limit_bytes=VMEM),
-        cost_estimate=cost(3 * 10**9, 2**20),
-        name="loss_head",
-    )(at, *pieces, project, pair_col, pair_row, gain)
-
-
 def d_result_of(res, seg, d_pool, gain):
     hot = lax.broadcasted_iota(jnp.int32, (SEG_ROW, seg.shape[-1]), 0) == seg
     member = jnp.where(hot, 1.0, 0.0)
@@ -648,121 +594,6 @@
     return scale * (weighted - unit * jnp.mean(weighted * unit, -1, keepdims=True))
 
 
-def ffn_back_kernel(
-    row_ref,
-    res_ref,
-    mid_ref,
-    a2_ref,
-    seg_ref,
-    dpool_ref,
-    gain_end_ref,
-    gain_ref,
-    own_b_ref,
-    own_c_ref,
-    b_ref,
-    c_ref,
-    wo_ref,
-    dmid_ref,
-    dattn_ref,
-    dctx_ref,
-    dgain_ref,
-    dres_s,
-    low_s,
-    sum_s,
-):
-    k = pl.program_id(0)
-
-    @pl.when(k == 0)
-    def _():
-        d_res = d_result_of(
-            res_ref[...].astype(f32), seg_ref[0], dpool_ref[...], gain_end_ref[...]
-        )
-        dres_s[...] = d_res
-        low_s[...] = d_res.astype(bf16)
-        sum_s[...] = jnp.zeros_like(sum_s)
-
-    def add(up, down):
-        slope = gelu_pair(dg(a2_ref[...], up, NN))[1]
-        d_pre = (dg(low_s[...], down, NT) * slope).astype(bf16)
-        sum_s[...] += dg(d_pre, up, NT)
-
-    @pl.when(k == 0)
-    def _():
-        add(own_b_ref[...], own_c_ref[...])
-
-    @pl.when(k > 0)
-    def _():
-        add(b_ref[0], c_ref[0])
-
-    @pl.when(k == pl.num_programs(0) - 1)
-    def _():
-        mid = mid_ref[...].astype(f32)
-        scale = inv_rms(mid)
-        unit = mid * scale
-        grad = sum_s[...]
-        weighted = grad * gain_ref[...]
-        d_mid = dres_s[...] + scale * (weighted - unit * jnp.mean(weighted * unit, -1, keepdims=True))
-        dgain_ref[...] = jnp.sum(grad * unit, 0, keepdims=True)
-        dmid_ref[...] = d_mid
-        low = d_mid.astype(bf16)
-        dattn_ref[...] = low
-        for s in range(wo_ref.shape[0]):
-            dctx_ref[s] = dg(wo_ref[s], low, NT).astype(bf16)
-
-
-def ffn_back(
-    row, res, mid, a2, segs, d_pool, gain_end, gain, sorted_a, own_b, own_c, sorted_b, sorted_c
-):
-    rows, _, length = segs.shape
-    tokens, width = mid.shape
-    slots = sorted_a.shape[0]
-    units = sorted_b.shape[-1]
-    cols = width // 4
-    own = pl.BlockSpec((length, width), lambda k, row: (row[0], 0))
-    fixed = lambda k, row: (0, 0)
-    return pl.pallas_call(
-        ffn_back_kernel,
-        grid_spec=pltpu.PrefetchScalarGridSpec(
-            num_scalar_prefetch=1,
-            grid=(slots,),
-            in_specs=[
-                pl.BlockSpec((length, width), fixed),
-                own,
-                own,
-                pl.BlockSpec((1, 1, length), lambda k, row: (row[0], 0, 0)),
-                pl.BlockSpec((SEG_ROW, width), lambda k, row: (row[0], 0)),
-                pl.BlockSpec((1, width), fixed),
-                pl.BlockSpec((1, width), fixed),
-                pl.BlockSpec((width, units), fixed),
-                pl.BlockSpec((units, width), fixed),
-                pl.BlockSpec((1, width, units), lambda k, row: (jnp.maximum(k - 1, 0), 0, 0)),
-                pl.BlockSpec((1, units, width), lambda k, row: (jnp.maximum(k - 1, 0), 0, 0)),
-                pl.BlockSpec((slots, cols, width), lambda k, row: (0, 3, 0)),
-            ],
-            out_specs=[
-                pl.BlockSpec((length, width), fixed),
-                pl.BlockSpec((length, width), fixed),
-                pl.BlockSpec((slots, cols, length), lambda k, row: (0, 0, 0)),
-                pl.BlockSpec((1, width), fixed),
-            ],
-            scratch_shapes=[
-                pltpu.VMEM((length, width), f32),
-                pltpu.VMEM((length, width), bf16),
-                pltpu.VMEM((length, width), f32),
-            ],
-        ),
-        out_shape=[
-            jax.ShapeDtypeStruct((length, width), f32),
-            jax.ShapeDtypeStruct((length, width), bf16),
-            jax.ShapeDtypeStruct((slots, cols, length), bf16),
-            jax.ShapeDtypeStruct((1, width), f32),
-        ],
-        compiler_params=pltpu.CompilerParams(vmem_limit_bytes=VMEM),
-        cost_estimate=cost(1.2 * 10**10, 2**24),
-        name="ffn_back",
-    )(row, res, mid, a2, segs, d_pool, gain_end, gain, own_b, own_c, sorted_b, sorted_c, sorted_a)
-
-
 def fold(tile):
     lanes = tile.shape[1]
     total = tile[0:8]
@@ -771,149 +602,322 @@
     return total
 
 
-def attn_back_kernel(
-    heads,
-    hd,
-    row_ref,
-    qkv_ref,
-    lse_ref,
-    ctx_ref,
-    dctx_ref,
-    vec_ref,
-    seg_ref,
-    w_ref,
-    x_ref,
-    dmid_ref,
-    gain_ref,
-    dqkv_ref,
-    fold_ref,
-    dtok_ref,
-    dgain_ref,
-    bias_s,
-    sum_s,
+def loss_step(pieces, at_ref, project_ref, pc_ref, pr_ref, gain_ref, dpool_ref, dproj_ref, dgain_ref, a_s, b_s):
+    each = SEG_ROW
+    parts = pieces[0].shape[0] // each
+    for m, piece in enumerate(pieces):
+        value = piece[...].astype(f32)
+        for part in range(parts):
+            start = pl.multiple_of(at_ref[1 + m * parts + part] * each, each)
+            a_s[pl.ds(start, each), :] = value[part * each : (part + 1) * each]
+    pooled = a_s[...].astype(bf16)
+    d_proj, d_pooled, d_gain = loss_math(
+        pooled, project_ref[...], pc_ref[...], pr_ref[...], gain_ref[...]
+    )
+    a_s[...] = d_pooled
+    b_s[...] = dg(pooled, d_proj, TN)
+    here = dpool_ref.shape[0]
+    block = dproj_ref.shape[0]
+    dpool_ref[...] = a_s[pl.ds(pl.multiple_of(at_ref[0] * here, here), here), :]
+    dproj_ref[...] = b_s[pl.ds(pl.multiple_of(at_ref[0] * block, block), block), :]
+    dgain_ref[...] = d_gain
+
+
+def norm_back(grad, values, gain):
+    scale = inv_rms(values)
+    unit = values * scale
+    weighted = grad * gain
+    d_values = scale * (weighted - unit * jnp.mean(weighted * unit, -1, keepdims=True))
+    return d_values, jnp.sum(grad * unit, 0, keepdims=True)
+
+
+def row_back_kernel(count, with_loss, heads, hd, at_ref, row_ref, *refs):
+    pieces, refs = refs[:count], refs[count:]
+    project_ref, pc_ref, pr_ref, gain_end_ref, gain_two_ref, gain_one_ref, seg_ref = refs[:7]
+    lse_ref, vec_ref, res_any, mid_any, a2_any, x_any, own_b, own_c, far_b, far_c = refs[7:17]
+    far_a, qkv_any, ctx_any = refs[17:20]
+    dpool_ref, dproj_ref, dend_ref, dtwo_ref, dattn_ref = refs[20:25]
+    dqkv_ref, fold_ref, dtok_ref, done_ref = refs[25:29]
+    a_s, p_s, b_s, c_s, wo_s, wa_s, res_s, mid_s, a2_s, x_s, qkv_s, ctx_s = refs[29:41]
+    dres_s, low_s, sum_s, dctx_s, bias_s, b_sems, c_sems, sems = refs[41:]
+    step = pl.program_id(0)
+    slots = b_s.shape[0]
+    length = res_s.shape[0]
+    cols = heads * hd
+    row = row_ref[0]
+    mine = pl.ds(pl.multiple_of(row * length, length), length)
+    res_copy = pltpu.make_async_copy(res_any, res_s, sems.at[0])
+    a2_copy = pltpu.make_async_copy(a2_any.at[mine], a2_s, sems.at[1])
+    mid_copy = pltpu.make_async_copy(mid_any.at[mine], mid_s, sems.at[2])
+    wo_copy = pltpu.make_async_copy(far_a.at[:, pl.ds(3 * cols, cols)], wo_s, sems.at[3])
+    qkv_copy = pltpu.make_async_copy(qkv_any, qkv_s, sems.at[4])
+    ctx_copy = pltpu.make_async_copy(ctx_any.at[:, row], ctx_s, sems.at[5])
+    wa_copy = pltpu.make_async_copy(far_a.at[:, pl.ds(0, 3 * cols)], wa_s, sems.at[6])
+    x_copy = pltpu.make_async_copy(x_any.at[mine], x_s, sems.at[7])
+
+    def weight_copies(k):
+        b_from, c_from = (own_b, own_c) if k == 0 else (far_b.at[k - 1], far_c.at[k - 1])
+        return [
+            pltpu.make_async_copy(b_from, b_s.at[k], b_sems.at[k]),
+            pltpu.make_async_copy(c_from, c_s.at[k], c_sems.at[k]),
+        ]
+
+    @pl.when(step == 0)
+    def _():
+        res_copy.start()
+        a2_copy.start()
+        for k in range(slots):
+            for copy in weight_copies(k):
+                copy.start()
+        for copy in (mid_copy, wo_copy, qkv_copy, ctx_copy, wa_copy, x_copy):
+            copy.start()
+        if with_loss:
+            loss_step(
+                pieces,
+                at_ref,
+                project_ref,
+                pc_ref,
+                pr_ref,
+                gain_end_ref,
+                dpool_ref,
+                dproj_ref,
+                dend_ref,
+                a_s,
+                p_s,
+            )
+        else:
+            dpool_ref[...] = pieces[0][...]
+            dproj_ref[...] = jnp.zeros_like(dproj_ref)
+            dend_ref[...] = jnp.zeros_like(dend_ref)
+        res_copy.wait()
+        a2_copy.wait()
+        d_pool = dpool_ref[pl.ds(pl.multiple_of(row * SEG_ROW, SEG_ROW), SEG_ROW), :]
+        d_res = d_result_of(res_s[...].astype(f32), seg_ref[0], d_pool, gain_end_ref[...])
+        dres_s[...] = d_res
+        low_s[...] = d_res.astype(bf16)
+        sum_s[...] = jnp.zeros_like(sum_s)
+
+    for k in range(slots):
+
+        @pl.when(step == k + 1)
+        def _():
+            for copy in weight_copies(k):
+                copy.wait()
+
+    @pl.when((step >= 1) & (step <= slots))
+    def _():
+        up, down = b_s.at[step - 1], c_s.at[step - 1]
+        slope = gelu_pair(dg(a2_s[...], up[...], NN))[1]
+        d_pre = (dg(low_s[...], down[...], NT) * slope).astype(bf16)
+        sum_s[...] += dg(d_pre, up[...], NT)
+
+    @pl.when(step == slots)
+    def _():
+        mid_copy.wait()
+        wo_copy.wait()
+        d_mid, dtwo_ref[...] = norm_back(
+            sum_s[...], mid_s[...].astype(f32), gain_two_ref[...]
+        )
+        d_mid = dres_s[...] + d_mid
+        dres_s[...] = d_mid
+        low = d_mid.astype(bf16)
+        dattn_ref[...] = low
+        sum_s[...] = jnp.zeros_like(sum_s)
+        for k in range(slots):
+            dctx_s[k] = dg(wo_s[k], low, NT).astype(bf16)
+        qkv_copy.wait()
+        ctx_copy.wait()
+        wa_copy.wait()
+        x_copy.wait()
+
+    @pl.when(step > slots)
+    def _():
+        slot = step - slots - 1
+        blocks = length // TILE
+        spread_bias(vec_ref.at[pl.ds(slot, 1)], bias_s, heads)
+        q_mask, k_mask = masks(seg_ref[0])
+        for h in range(heads):
+            q_low = qkv_s[slot, h * hd : (h + 1) * hd]
+            k_low = qkv_s[slot, (heads + h) * hd : (heads + h + 1) * hd]
+            v_low = qkv_s[slot, (2 * heads + h) * hd : (2 * heads + h + 1) * hd]
+            dc = dctx_s[slot, h * hd : (h + 1) * hd]
+            c = ctx_s[slot, h * hd : (h + 1) * hd]
+            delta = jnp.sum(dc.astype(f32) * c.astype(f32), 0, keepdims=True)
+            lse = lse_ref[slot, h : h + 1]
+            scores = dg(
+                jnp.concatenate([k_low, k_mask], 0).T, jnp.concatenate([q_low, q_mask], 0), NN
+            )
+            d_probs = dg(v_low.T, dc, NN)
+            probs_cols = []
+            score_cols = []
+            near = [None, None, None]
+            far = [None, None]
+            for i in range(blocks):
+                at = slice(i * TILE, (i + 1) * TILE)
+                probs = []
+                grads = []
+                for j in range(blocks):
+                    to = slice(j * TILE, (j + 1) * TILE)
+                    tile = with_bias(scores[to, at], j - i, h, bias_s, vec_ref.at[pl.ds(slot, 1)])
+                    prob = jnp.exp(tile - lse[:, at])
+                    grad = prob * (d_probs[to, at] - delta[:, at])
+                    probs.append(prob.astype(bf16))
+                    grads.append(grad.astype(bf16))
+                    if abs(j - i) <= 1:
+                        old = near[j - i + 1]
+                        near[j - i + 1] = grad if old is None else old + grad
+                    else:
+                        old = far[int(j < i)]
+                        far[int(j < i)] = grad if old is None else old + grad
+                probs_cols.append(jnp.concatenate(probs, 0))
+                score_cols.append(jnp.concatenate(grads, 0))
+            probs = jnp.concatenate(probs_cols, 1)
+            grads = jnp.concatenate(score_cols, 1)
+            dqkv_ref[0, h * hd : (h + 1) * hd] = dg(k_low, grads, NN).astype(bf16)
+            dqkv_ref[0, (heads + h) * hd : (heads + h + 1) * hd] = dg(q_low, grads, NT).astype(bf16)
+            dqkv_ref[0, (2 * heads + h) * hd : (2 * heads + h + 1) * hd] = dg(dc, probs, NT).astype(
+                bf16
+            )
+            band = jnp.concatenate([near[1], near[0], jnp.zeros_like(near[0]), near[2]], 1)
+            fold_ref[0, h, :, : 4 * TILE] = fold(band)
+            for side in range(2):
+                total = far[side][0:8]
+                for b in range(1, TILE // 8):
+                    total = total + far[side][8 * b : 8 * b + 8]
+                fold_ref[0, h, :, (4 + side) * TILE : (5 + side) * TILE] = total
+        sum_s[...] += dg(dqkv_ref[0], wa_s[slot], TN)
+
+    @pl.when(step == 2 * slots)
+    def _():
+        d_x, done_ref[...] = norm_back(sum_s[...], x_s[...].astype(f32), gain_one_ref[...])
+        dtok_ref[...] = (dres_s[...] + d_x).astype(bf16)
+
+
+def row_back(
+    at,
+    row,
+    pieces,
+    with_loss,
+    project,
+    pairs,
+    gains,
+    segs,
+    lse,
+    vecs,
+    res,
+    mid,
+    a2,
+    x,
+    own_b,
+    own_c,
+    far_b,
+    far_c,
+    sorted_a,
+    qkv,
+    ctx,
+    here,
+    block,
 ):
-    slot = pl.program_id(0)
-    length = qkv_ref.shape[-1]
-    blocks = length // TILE
-    spread_bias(vec_ref, bias_s, heads)
-    q_mask, k_mask = masks(seg_ref[0])
-    for h in range(heads):
-        q_low = qkv_ref[0, 0, h * hd : (h + 1) * hd]
-        k_low = qkv_ref[0, 0, (heads + h) * hd : (heads + h + 1) * hd]
-        v_low = qkv_ref[0, 0, (2 * heads + h) * hd : (2 * heads + h + 1) * hd]
-        dc = dctx_ref[0, h * hd : (h + 1) * hd]
-        c = ctx_ref[0, 0, h * hd : (h + 1) * hd]
-        delta = jnp.sum(dc.astype(f32) * c.astype(f32), 0, keepdims=True)
-        lse = lse_ref[0, 0, h : h + 1]
-        scores = dg(
-            jnp.concatenate([k_low, k_mask], 0).T, jnp.concatenate([q_low, q_mask], 0), NN
-        )
-        d_probs = dg(v_low.T, dc, NN)
-        probs_cols = []
-        score_cols = []
-        near = [None, None, None]
-        far = [None, None]
-        for i in range(blocks):
-            at = slice(i * TILE, (i + 1) * TILE)
-            probs = []
-            grads = []
-            for j in range(blocks):
-                to = slice(j * TILE, (j + 1) * TILE)
-                tile = with_bias(scores[to, at], j - i, h, bias_s, vec_ref)
-                prob = jnp.exp(tile - lse[:, at])
-                grad = prob * (d_probs[to, at] - delta[:, at])
-                probs.append(prob.astype(bf16))
-                grads.append(grad.astype(bf16))
-                if abs(j - i) <= 1:
-                    old = near[j - i + 1]
-                    near[j - i + 1] = grad if old is None else old + grad
-                else:
-                    old = far[int(j < i)]
-                    far[int(j < i)] = grad if old is None else old + grad
-            probs_cols.append(jnp.concatenate(probs, 0))
-            score_cols.append(jnp.concatenate(grads, 0))
-        probs = jnp.concatenate(probs_cols, 1)
-        grads = jnp.concatenate(score_cols, 1)
-        dqkv_ref[0, h * hd : (h + 1) * hd] = dg(k_low, grads, NN).astype(bf16)
-        dqkv_ref[0, (heads + h) * hd : (heads + h + 1) * hd] = dg(q_low, grads, NT).astype(bf16)
-        dqkv_ref[0, (2 * heads + h) * hd : (2 * heads + h + 1) * hd] = dg(dc, probs, NT).astype(
-            bf16
-        )
-        band = jnp.concatenate([near[1], near[0], jnp.zeros_like(near[0]), near[2]], 1)
-        fold_ref[0, h, :, : 4 * TILE] = fold(band)
-        for side in range(2):
-            total = far[side][0:8]
-            for b in range(1, TILE // 8):
-                total = total + far[side][8 * b : 8 * b + 8]
-            fold_ref[0, h, :, (4 + side) * TILE : (5 + side) * TILE] = total
-    part = dg(dqkv_ref[0], w_ref[0], TN)
-
-    @pl.when(slot == 0)
-    def _():
-        sum_s[...] = part
-
-    @pl.when(slot > 0)
-    def _():
-        sum_s[...] += part
-
-    @pl.when(slot == pl.num_programs(0) - 1)
-    def _():
-        x = x_ref[...].astype(f32)
-        scale = inv_rms(x)
-        unit = x * scale
-        grad = sum_s[...]
-        weighted = grad * gain_ref[...]
-        d_tok = dmid_ref[...] + scale * (weighted - unit * jnp.mean(weighted * unit, -1, keepdims=True))
-        dtok_ref[...] = d_tok.astype(bf16)
-        dgain_ref[...] = jnp.sum(grad * unit, 0, keepdims=True)
-
-
-def attn_back(row, qkv, lse, ctx, d_ctx, vecs, segs, all_a, x, d_mid, gain):
-    slots, rows, cols3, length = qkv.shape
-    heads = lse.shape[2]
-    cols = cols3 // 3
-    width = x.shape[1]
-    own4 = lambda k, row: (k, row[0], 0, 0)
-    slot = lambda k, row: (k, 0, 0)
-    fixed = lambda k, row: (0, 0)
+    slots, heads, _ = vecs.shape
+    length, width = res.shape
+    units = own_b.shape[1]
+    cols = width // 4
+    n_all = pairs.shape[0]
+    anywhere = pl.BlockSpec(memory_space=pl.ANY)
+
+    def full(shape):
+        zeros = (0,) * len(shape)
+        return pl.BlockSpec(shape, lambda i, at, row: zeros)
+
+    def slot(i):
+        return jnp.maximum(i - slots - 1, 0)
+
+    row_shape = (length, width)
     return pl.pallas_call(
-        functools.partial(attn_back_kernel, heads, cols // heads),
+        functools.partial(row_back_kernel, len(pieces), with_loss, heads, cols // heads),
         grid_spec=pltpu.PrefetchScalarGridSpec(
-            num_scalar_prefetch=1,
-            grid=(slots,),
-            in_specs=[
-                pl.BlockSpec((1, 1, cols3, length), own4),
-                pl.BlockSpec((1, 1, heads, length), own4),
-                pl.BlockSpec((1, 1, cols, length), own4),
-                pl.BlockSpec((1, cols, length), slot),
-                pl.BlockSpec((1, heads, 4 * TILE), slot),
-                pl.BlockSpec((1, 1, length), lambda k, row: (row[0], 0, 0)),
-                pl.BlockSpec((1, cols3, width), slot),
-                pl.BlockSpec((length, width), lambda k, row: (row[0], 0)),
-                pl.BlockSpec((length, width), fixed),
-                pl.BlockSpec((1, width), fixed),
-            ],
+            num_scalar_prefetch=2,
+            grid=(2 * slots + 1,),
+            in_specs=[full(piece.shape) for piece in pieces]
+            + [full(project.shape), full((n_all, 1)), full((1, n_all))]
+            + [full((1, width))] * 3
+            + [
+                pl.BlockSpec((1, 1, length), lambda i, at, row: (row[0], 0, 0)),
+                full(lse.shape),
+                full(vecs.shape),
+            ]
+            + [anywhere] * 11,
             out_specs=[
-                pl.BlockSpec((1, cols3, length), slot),
-                pl.BlockSpec((1, heads, 8, 6 * TILE), lambda k, row: (k, 0, 0, 0)),
-                pl.BlockSpec((length, width), fixed),
-                pl.BlockSpec((1, width), fixed),
+                full((here, width)),
+                full((block, width)),
+                full((1, width)),
+                full((1, width)),
+                full(row_shape),
+                pl.BlockSpec((1, 3 * cols, length), lambda i, at, row: (slot(i), 0, 0)),
+                pl.BlockSpec((1, heads, 8, 6 * TILE), lambda i, at, row: (slot(i), 0, 0, 0)),
+                full(row_shape),
+                full((1, width)),
             ],
             scratch_shapes=[
+                pltpu.VMEM((n_all if with_loss else 8, width), f32),
+                pltpu.VMEM((width, width), f32),
+                pltpu.VMEM((slots, width, units), bf16),
+                pltpu.VMEM((slots, units, width), bf16),
+                pltpu.VMEM((slots, cols, width), bf16),
+                pltpu.VMEM((slots, 3 * cols, width), bf16),
+                pltpu.VMEM(row_shape, bf16),
+                pltpu.VMEM(row_shape, bf16),
+                pltpu.VMEM(row_shape, bf16),
+                pltpu.VMEM(row_shape, bf16),
+                pltpu.VMEM((slots, 3 * cols, length), bf16),
+                pltpu.VMEM((slots, cols, length), bf16),
+                pltpu.VMEM(row_shape, f32),
+                pltpu.VMEM(row_shape, bf16),
+                pltpu.VMEM(row_shape, f32),
+                pltpu.VMEM((slots, cols, length), bf16),
                 pltpu.VMEM((heads, TILE, 4 * TILE), f32),
-                pltpu.VMEM((length, width), f32),
+                pltpu.SemaphoreType.DMA((slots,)),
+                pltpu.SemaphoreType.DMA((slots,)),
+                pltpu.SemaphoreType.DMA((8,)),
             ],
         ),
         out_shape=[
-            jax.ShapeDtypeStruct((slots, cols3, length), bf16),
+            jax.ShapeDtypeStruct((here, width), f32),
+            jax.ShapeDtypeStruct((block, width), f32),
+            jax.ShapeDtypeStruct((1, width), f32),
+            jax.ShapeDtypeStruct((1, width), f32),
+            jax.ShapeDtypeStruct(row_shape, bf16),
+            jax.ShapeDtypeStruct((slots, 3 * cols, length), bf16),
             jax.ShapeDtypeStruct((slots, heads, 8, 6 * TILE), f32),
-            jax.ShapeDtypeStruct((length, width), bf16),
+            jax.ShapeDtypeStruct(row_shape, bf16),
             jax.ShapeDtypeStruct((1, width), f32),
         ],
         compiler_params=pltpu.CompilerParams(vmem_limit_bytes=VMEM),
-        cost_estimate=cost(1.5 * 10**10, 2**24),
-        name="attn_back",
-    )(row, qkv, lse, ctx, d_ctx, vecs, segs, all_a, x, d_mid, gain)
+        cost_estimate=cost(3 * 10**10, 2**24),
+        name="row_back",
+    )(
+        at,
+        row,
+        *pieces,
+        project,
+        pairs[:, None],
+        pairs[None, :],
+        *gains,
+        segs,
+        lse,
+        vecs,
+        res,
+        mid,
+        a2,
+        x,
+        own_b,
+        own_c,
+        far_b,
+        far_c,
+        sorted_a,
+        qkv,
+        ctx,
+    )
 
 
 def split_blocks(core, rel_ref, block, pad, extra, values, keep_ref, give_ref, lead):
@@ -1198,14 +1202,18 @@
 
     x = tokens.astype(f32)
     a1 = (x * inv_rms(x) * one).astype(bf16)
-    state = attention(after(a1, far_a), pack_a, vec_own, segs, n_tp)
+    state = attention(
+        "attn_own", after(a1, far_a), vec_own, segs, place, order, 0, 0, rows, [pack_a], None
+    )
     far_a = from_chips(far_a)
     far_b, far_c = others_of(after(order, (state, far_a)), all_bc, 2)
     groups = np.arange(n_dp).reshape(-1, share).tolist()
     far_c = lax.all_gather(far_c, "dp", axis=0, axis_index_groups=groups)
     far_a = from_cores(after(far_a, far_b))
     far_b = from_chips(after(far_b, far_a))
-    qkv, lse, ctx, sorted_a = attention(a1, pack_a, vecs, segs, n_tp, place, far_a, state)
+    qkv, lse, ctx, sorted_a = attention(
+        "attn_far", a1, vecs[1:], segs, place, order, 1, 0, rows, far_a, state
+    )
     far_b = from_cores(after(far_b, lse))
     mid, a2, part = ffn_own(tokens, ctx, sorted_a, two, w_hidden, w_down)
     layer_out, res, pooled, sorted_b, sorted_c = ffn_first(
@@ -1224,28 +1232,44 @@
         pooled = lax.all_gather(pooled, "tp", axis=0, tiled=True)
         pooled_all = [lax.all_gather(pooled, "dp", axis=0, tiled=True)]
         at = dp[None].astype(jnp.int32)
-    d_pool, grad_project, d_gain_end = loss_head(
-        at, pooled_all, w_project, pair_order // 2, end, here, block
-    )
-    grad_gain_final = lax.dynamic_slice_in_dim(d_gain_end[0], dp * block, block, 0)
-    d_mid, d_attn, d_ctx, d_gain_two = ffn_back(
+    pairs = pair_order // 2
+    if not split:
+        everything = pooled_all[0]
+        d_proj, d_pool, d_gain_end = loss_math(
+            everything, w_project, pairs[:, None], pairs[None, :], end
+        )
+        own_cols = lax.dynamic_slice_in_dim(everything, dp * block, block, 1)
+        grad_project = dg(own_cols, d_proj, TN)
+        pooled_all = [lax.dynamic_slice_in_dim(d_pool, dp * here, here, 0)]
+    made = row_back(
+        at,
         row,
+        pooled_all,
+        split,
+        w_project,
+        pairs,
+        (end, two, one),
+        segs,
+        lse,
+        vecs,
         res,
         mid,
         a2,
-        segs,
-        d_pool,
-        end,
-        two,
-        sorted_a,
+        tokens,
         w_hidden,
         w_down,
         sorted_b,
         sorted_c,
-    )
-    d_qkv, folded, d_tok, d_gain_one = attn_back(
-        row, qkv, lse, ctx, d_ctx, vecs, segs, sorted_a, tokens, d_mid, one
-    )
+        sorted_a,
+        qkv,
+        ctx,
+        here,
+        block,
+    )
+    d_pool, d_gain_two, d_attn, d_qkv, folded, d_tok, d_gain_one = made[0], *made[3:]
+    if split:
+        grad_project, d_gain_end = made[1], made[2]
+    grad_gain_final = lax.dynamic_slice_in_dim(d_gain_end[0], dp * block, block, 0)
     d_tokens = lax.all_gather(d_tok, "tp", axis=0, tiled=True).astype(f32)
 
     d_rel = jnp.einsum(

time: 293 us -> 285 us (0.973)
  the two profiles are of different devices: /device:TPU:0 before, /device:TPU:11 now
where the time goes in v2:
time: 285 us; the launch traced here: 280 us
  Pallas kernels  149 us (52%)
  waiting for transfers between devices  43.2 us (15%)
  starting transfers between devices  38.9 us (14%)
  other arithmetic  20.8 us (7%)
  between operations  14.9 us (5%)
  local copies, waits for them, and re-layouts  11.2 us (4%)
    pallas_call x2, Pallas kernels, attention(): pl.pallas_call(functools.partial(attn_kernel, heads, hd, n, low, keeps),...  44 us
    pallas_call x1, Pallas kernels, ffn_tail(): pl.pallas_call(functools.partial(ffn_tail_kernel, block), grid_spec=pltpu...  33.2 us
    pallas_call x1, Pallas kernels, row_back(): pl.pallas_call(functools.partial(row_back_kernel, len(pieces), with_loss,...  31.8 us
    ppermute x9, waiting for transfers between devices, over_tp(): return lax.ppermute(value, 'tp', levels[k])  27.6 us
    ppermute x23, starting transfers between devices, over_dp(): return lax.ppermute(value, 'dp', mates[m])  24.2 us
    pallas_call x1, Pallas kernels, ffn_own(): pl.pallas_call(ffn_own_kernel, grid=(rows,), in_specs=[by_row, pl.BlockSp...  13.5 us
    ppermute x23, waiting for transfers between devices, over_dp(): return lax.ppermute(value, 'dp', mates[m])  12.7 us
    pallas_call x1, Pallas kernels, ffn_first(): pl.pallas_call(functools.partial(ffn_first_kernel, n), grid_spec=pltpu.Pr...  11.5 us
  transfers between devices with their start and end apart: 36, of which 16 were waited for; matrix products, arithmetic and copies ran while one was open for 9% of the time, Pallas kernels for 33%

profile of v2, /device:TPU:11, one launch (start us, length us, event | category | flops | bytes accessed | tf_op | source)
XLA Modules:
  0.0 280.0 jit_solution(4679377811660855548)
XLA Ops:
  9.9 1.4 pack_weights.1
  11.5 2.3 collective-permute-start.1
  15.7 2.6 fusion
  18.4 4.5 %fusion.2.a1_ref = bf16[2048,768]{1,0:T(8,128)(2,1)} fusion(bf16[2048,768]{1,0:T(8,128)(2,1)} %refs_16_.1, f32[768]{0:T(1024)S(1)} %copy-done.21, f32[2048]{0:T(1024)S(1)} %add_rsqrt_fusion), kind=kLoop, calls=%fused_computation.4 | loop fusion | flops 6291456 | bytes 6302720 | tf_op jit(solution)/shard_map/convert_element_type | solution.py:1204
  23.1 5.5 %collective-permute-done.2.refs_2_ = bf16[112,768]{1,0:T(8,128)(2,1)S(1)} collective-permute-done((bf16[112,768]{1,0:T(8,128)(2,1)S(1)}, bf16[112,768]{1,0:T(8,128)(2,1)S(1)}, u32[]{:S(2)}, u32[]{:S(2)}) %collective-permute-start.2) | collective-permute-done | bytes 172064 | tf_op jit(solution)/shard_map/ppermute | solution.py:1163
  29.2 1.9 stack.1
  33.8 11.7 %attn_own.1 = (bf16[4,576,512]{2,1,0:T(8,128)(2,1)}, f32[4,3,512]{2,1,0:T(4,128)S(1)}, bf16[4,4,192,512]{3,2,1,0:T(8,128)(2,1)}, bf16[4,768,768]{2,1,0:T(8,128)(2,1)}) custom-call(s32[8]{0:T(128)S(1)} %xor_multiply_fusion.place_ref, s32[4]{0:T(128)S(1)} %iota_xor_fusion.order_ref, bf16[2048,768]{1,0:T(8,128)(2,1)} %fusion.2.a1_ref, ...), custom_call_target="tpu_custom_call" | custom-call | flops 10000000000 | bytes 1048576 | tf_op jit(solution)/shard_map/attn_own/pallas_call | solution.py:361
  45.6 2.9 %all-gather.8.cloned.1.call-done = bf16[768,768]{1,0:T(8,128)(2,1)} async-done(((bf16[192,768]{1,0:T(8,128)(2,1)}), bf16[768,768]{1,0:T(8,128)(2,1)}) %all-gather.8.cloned.1.call-update) | async-done | bytes 1179664 | tf_op jit(solution)/shard_map/all_gather | solution.py:1193
  48.5 3.0 %others_of.1 = (bf16[3,96,768]{2,1,0:T(8,128)(2,1)}, bf16[3,96,768]{2,1,0:T(8,128)(2,1)}) custom-call(s32[4]{0:T(128)} %copy-done.2, bf16[4,192,768]{2,1,0:T(8,128)(2,1)} %bitcast.75), custom_call_target="tpu_custom_call" | custom-call | bytes 2359296 | tf_op jit(solution)/shard_map/others_of/pallas_call | solution.py:223
  52.0 6.5 %collective-permute-start.6 = (bf16[3,96,768]{2,1,0:T(8,128)(2,1)S(1)}, bf16[3,96,768]{2,1,0:T(8,128)(2,1)S(1)}, u32[]{:S(2)}, u32[]{:S(2)}) collective-permute-start(bf16[3,96,768]{2,1,0:T(8,128)(2,1)S(1)} %copy-done.5), channel_id=1, source_target_pairs={{0,4},{4,0},{8,12},{12,8},{16,20},{20,16},{24,28},{28,24},{1,5},{5... | collective-permute-start | bytes 1327112 | tf_op jit(solution)/shard_map/ppermute | solution.py:1160
  64.6 32.3 %attn_far.1 = (bf16[4,576,512]{2,1,0:T(8,128)(2,1)}, f32[4,3,512]{2,1,0:T(4,128)S(1)}, bf16[4,4,192,512]{3,2,1,0:T(8,128)(2,1)}, bf16[4,768,768]{2,1,0:T(8,128)(2,1)}) custom-call(s32[8]{0:T(128)S(1)} %xor_multiply_fusion.place_ref, s32[4]{0:T(128)S(1)} %copy-done.3, ...), custom_call_target="tpu_custom_call", output_to_operand_aliasing={{0}: (13, {}), {1}: (14, {}), {2}: (15, {}), {3}: (16, {})} | custom-call | flops 30000001024 | bytes 1048576 | tf_op jit(solution)/shard_map/attn_far/pallas_call | solution.py:361
  97.0 1.3 collective-permute-start.13
  98.9 13.5 %ffn_own.1 = (bf16[2048,768]{1,0:T(8,128)(2,1)}, bf16[2048,768]{1,0:T(8,128)(2,1)}, bf16[2048,768]{1,0:T(8,128)(2,1)}) custom-call(bf16[2048,768]{1,0:T(8,128)(2,1)} %refs_16_.1, bf16[4,4,192,512]{3,2,1,0:T(8,128)(2,1)} %get-tuple-element.77.ctx_ref.refs_23_, bf16[4,768,768]{2,1,0:T(8,128)(2,1)} %get-tuple-element.78.wo_ref.refs_21_, ...), custom_call_target="tpu_custom_call" | custom-call | flops 7247757312 | bytes 16777216 | tf_op jit(solution)/shard_map/ffn_own/pallas_call | solution.py:423
  113.2 11.5 %ffn_first.1 = (bf16[2048,768]{1,0:T(8,128)(2,1)}, bf16[512,768]{1,0:T(8,128)(2,1)}, f32[8,768]{1,0:T(8,128)S(1)}, bf16[3,768,768]{2,1,0:T(8,128)(2,1)}, bf16[3,768,768]{2,1,0:T(8,128)(2,1)}) custom-call(s32[8]{0:T(128)S(1)} %xor_multiply_fusion.place_ref, s32[4]{0:T(128)S(1)} %copy-done.3, bf16[2048,768]{1,0:T(8,128)(2,1)} %get-tuple-element.79.a2_ref.refs_15_, ...), custom_call_target="tpu_custom_call" | custom-call | flops 3623878656 | bytes 16777216 | tf_op jit(solution)/shard_map/ffn_first/pallas_call | solution.py:515
  124.8 4.3 %collective-permute-start.18 = (bf16[8,768]{1,0:T(8,128)(2,1)S(1)}, bf16[8,768]{1,0:T(8,128)(2,1)S(1)}, u32[]{:S(2)}, u32[]{:S(2)}) collective-permute-start(bf16[8,768]{1,0:T(8,128)(2,1)S(1)} %get-tuple-element.166), channel_id=1, source_target_pairs={{0,2},{1,3},{2,0},{3,1},{4,6},{5,7},{6,4},{7,5},{8,10},{9,11},{10,... | collective-permute-start | bytes 36872 | tf_op jit(solution)/shard_map/ppermute | solution.py:1163
  130.3 1.3 collective-permute-done.19
  131.6 2.1 collective-permute-start.20
  138.9 2.9 %collective-permute-done.23.refs_3_ = bf16[64,768]{1,0:T(8,128)(2,1)S(1)} collective-permute-done((bf16[64,768]{1,0:T(8,128)(2,1)S(1)}, bf16[64,768]{1,0:T(8,128)(2,1)S(1)}, u32[]{:S(2)}, u32[]{:S(2)}) %collective-permute-start.23) | collective-permute-done | bytes 98336 | tf_op jit(solution)/shard_map/ppermute | solution.py:1160
  141.8 31.8 %row_back.1 = (f32[32,768]{1,0:T(8,128)S(1)}, f32[96,768]{1,0:T(8,128)}, f32[1,768]{1,0:T(1,128)S(1)}, f32[1,768]{1,0:T(1,128)S(1)}, bf16[512,768]{1,0:T(8,128)(...) custom-call(s32[33]{0:T(128)S(1)} %pad_add_fusion.1.at_ref, ...), custom_call_target="tpu_custom_call" | custom-call | flops 30000001024 | bytes 16777216 | tf_op jit(solution)/shard_map/row_back/pallas_call | solution.py:836
  176.5 9.0 %attn_weights.1 = (bf16[4,4,112,768]{3,2,1,0:T(8,128)(2,1)}, bf16[4,4,112,768]{3,2,1,0:T(8,128)(2,1)}) custom-call(s32[6]{0:T(128)S(1)} %pad_add_fusion.place_ref, bf16[2048,768]{1,0:T(8,128)(2,1)} %fusion.2.a1_ref, bf16[512,768]{1,0:T(8,128)(2,1)S(1)} %get-tuple-element.94.dattn_ref, bf16[4,576,512]{2,1,0:T(8,128)(2,1)} %get-tuple-element.95.dqkv_ref, ...), custom_call_target="tpu_custom_call" | custom-call | flops 1000000 | bytes 1000000 | tf_op jit(solution)/shard_map/attn_weights/pallas_call | solution.py:980
  186.7 4.9 %collective-permute-done.24 = bf16[4,4,112,768]{3,2,1,0:T(8,128)(2,1)S(1)} collective-permute-done((bf16[4,4,112,768]{3,2,1,0:T(8,128)(2,1)}, bf16[4,4,112,768]{3,2,1,0:T(8,128)(2,1)S(1)}, u32[]{:S(2)}, u32[]{:S(2)}) %collective-permute-start.24) | collective-permute-done | bytes 2752544 | tf_op jit(solution)/shard_map/ppermute | solution.py:1160
  191.6 2.1 fusion.14
  196.4 33.2 %ffn_tail.1 = (bf16[2048,768]{1,0:T(8,128)(2,1)}, bf16[4,2,96,768]{3,2,1,0:T(8,128)(2,1)}, bf16[4,2,96,768]{3,2,1,0:T(8,128)(2,1)}) custom-call(s32[6]{0:T(128)S(1)} %pad_add_fusion.place_ref, s32[4]{0:T(128)S(1)} %copy-done.3, bf16[2048,768]{1,0:T(8,128)(2,1)} %get-tuple-element.79.a2_ref.refs_15_, ...), custom_call_target="tpu_custom_call", output_to_operand_aliasing={{0}: (13, {})} | custom-call | flops 20000000000 | bytes 16777216 | tf_op jit(solution)/shard_map/ffn_tail/pallas_call | solution.py:1095
  229.7 1.3 collective-permute-start.31
  231.0 2.9 %fusion.17 = (bf16[4,112,768]{2,1,0:T(8,128)(2,1)S(1)}, f32[4,112,768]{2,1,0:T(8,128)}) fusion(bf16[4,112,768]{2,1,0:T(8,128)(2,1)S(1)} %collective-permute-done.27, bf16[4,112,768]{2,1,0:T(8,128)(2,1)S(1)} %collective-permute-done.26, bf16[4,112,768]{2,1,0:T(8,128)(2,1)S(1)} %collective-permute-done.25, ...), kind=kLoop, calls=%fused_computation.65 | loop fusion | flops 4128768 | bytes 5505024 | tf_op jit(solution)/shard_map/convert.2
  233.9 1.8 collective-permute-start.28
  237.0 1.3 add_convert_fusion
  238.3 4.3 %all-to-all-start = ((bf16[4,2,96,768]{3,2,1,0:T(8,128)(2,1)}), bf16[4,2,96,768]{3,2,1,0:T(8,128)(2,1)S(1)}, u32[]{:S(2)}, u32[]{:S(2)}) async-start(bf16[4,2,96,768]{3,2,1,0:T(8,128)(2,1)} %add_convert_fusion), calls=%async_computation | async-start | bytes 2359296 | tf_op jit(solution)/shard_map/all_to_all | solution.py:1329
  243.2 6.8 %collective-permute-done.28 = bf16[112,768]{1,0:T(8,128)(2,1)S(1)} collective-permute-done((bf16[112,768]{1,0:T(8,128)(2,1)S(1)}, bf16[112,768]{1,0:T(8,128)(2,1)S(1)}, u32[]{:S(2)}, u32[]{:S(2)}) %collective-permute-start.28) | collective-permute-done | bytes 172064 | tf_op jit(solution)/shard_map/ppermute | solution.py:1163
  250.0 1.3 collective-permute-done.29
  251.3 11.8 %collective-permute-done.30 = bf16[112,768]{1,0:T(8,128)(2,1)S(1)} collective-permute-done((bf16[112,768]{1,0:T(8,128)(2,1)S(1)}, bf16[112,768]{1,0:T(8,128)(2,1)S(1)}, u32[]{:S(2)}, u32[]{:S(2)}) %collective-permute-start.30) | collective-permute-done | bytes 172064 | tf_op jit(solution)/shard_map/ppermute | solution.py:1163
  267.0 5.1 %convert_element_type.158 = f32[2048,768]{1,0:T(8,128)} convert(bf16[2048,768]{1,0:T(8,128)(2,1)} %all-gather.6.cloned.1.call-done) | non-fusion elementwise | flops 1572864 | bytes 9437184 | tf_op jit(solution)/shard_map/convert_element_type | solution.py:1273
  (175 shorter events, 36.0 us)
Async XLA Ops:
  7.2 41.3 %all-gather.8.cloned.1.call-start = ((), (), s32[]{:S(2)}) async-start(), calls=%async_computation.2 | async-start | bytes 1474560 | tf_op jit(solution)/shard_map/all_gather | solution.py:1193
  11.3 11.8 %collective-permute-start = (bf16[112,768]{1,0:T(8,128)(2,1)S(1)}, bf16[112,768]{1,0:T(8,128)(2,1)S(1)}, u32[]{:S(2)}, u32[]{:S(2)}) collective-permute-start(bf16[112,768]{1,0:T(8,128)(2,1)S(1)} %get-tuple-element.62), channel_id=1, source_target_pairs={{0,1},{1,0},{2,3},{3,2},{4,5},{5,4},{6,7},{7,6},{8,9},{9,8},{10,11... | collective-permute-start | bytes 516104 | tf_op jit(solution)/shard_map/ppermute | solution.py:1163
  11.5 11.6 %collective-permute-start.1 = (bf16[112,768]{1,0:T(8,128)(2,1)S(1)}, bf16[112,768]{1,0:T(8,128)(2,1)S(1)}, u32[]{:S(2)}, u32[]{:S(2)}) collective-permute-start(bf16[112,768]{1,0:T(8,128)(2,1)S(1)} %get-tuple-element.62), channel_id=1, source_target_pairs={{0,2},{1,3},{2,0},{3,1},{4,6},{5,7},{6,4},{7,5},{8,10},{9,11},{10,... | collective-permute-start | bytes 516104 | tf_op jit(solution)/shard_map/ppermute | solution.py:1163
  13.8 14.8 %collective-permute-start.2 = (bf16[112,768]{1,0:T(8,128)(2,1)S(1)}, bf16[112,768]{1,0:T(8,128)(2,1)S(1)}, u32[]{:S(2)}, u32[]{:S(2)}) collective-permute-start(bf16[112,768]{1,0:T(8,128)(2,1)S(1)} %get-tuple-element.62), channel_id=1, source_target_pairs={{0,3},{1,2},{2,1},{3,0},{4,7},{5,6},{6,5},{7,4},{8,11},{9,10},{10,... | collective-permute-start | bytes 516104 | tf_op jit(solution)/shard_map/ppermute | solution.py:1163
  15.6 97.6 %all-gather.10.cloned.1.call-start = ((), (), s32[]{:S(2)}) async-start(), calls=%async_computation.3 | async-start | bytes 3981312 | tf_op jit(solution)/shard_map/all_gather | solution.py:1211
  31.1 14.4 %collective-permute-start.3 = (bf16[3,96,768]{2,1,0:T(8,128)(2,1)}, bf16[3,96,768]{2,1,0:T(8,128)(2,1)S(1)}, u32[]{:S(2)}, u32[]{:S(2)}) collective-permute-start(bf16[3,96,768]{2,1,0:T(8,128)(2,1)} %get-tuple-element.73.rest_0_), channel_id=1, source_target_pairs={{0,8},{4,12},{8,0},{12,4},{16,24},{20,28},{24,16},{28,20},{1,9},{5... | collective-permute-start | bytes 1327112 | tf_op jit(solution)/shard_map/ppermute | solution.py:1160
  31.4 14.2 %collective-permute-start.4 = (bf16[3,96,768]{2,1,0:T(8,128)(2,1)}, bf16[3,96,768]{2,1,0:T(8,128)(2,1)S(1)}, u32[]{:S(2)}, u32[]{:S(2)}) collective-permute-start(bf16[3,96,768]{2,1,0:T(8,128)(2,1)} %get-tuple-element.73.rest_0_), channel_id=1, source_target_pairs={{0,16},{4,20},{8,24},{12,28},{16,0},{20,4},{24,8},{28,12},{1,17},{... | collective-permute-start | bytes 1327112 | tf_op jit(solution)/shard_map/ppermute | solution.py:1160
  32.6 13.0 %collective-permute-start.5 = (bf16[3,96,768]{2,1,0:T(8,128)(2,1)}, bf16[3,96,768]{2,1,0:T(8,128)(2,1)}, u32[]{:S(2)}, u32[]{:S(2)}) collective-permute-start(bf16[3,96,768]{2,1,0:T(8,128)(2,1)} %get-tuple-element.73.rest_0_), channel_id=1, source_target_pairs={{0,24},{4,28},{8,16},{12,20},{16,8},{20,12},{24,0},{28,4},{1,25},{... | collective-permute-start | bytes 1327112 | tf_op jit(solution)/shard_map/ppermute | solution.py:1160
  51.5 215.5 %all-gather.6.cloned.1.call-start = ((), (), s32[]{:S(2)}) async-start(), calls=%async_computation.1 | async-start | bytes 3932160 | tf_op jit(solution)/shard_map/all_gather | solution.py:1273
  52.0 7.9 %collective-permute-start.6 = (bf16[3,96,768]{2,1,0:T(8,128)(2,1)S(1)}, bf16[3,96,768]{2,1,0:T(8,128)(2,1)S(1)}, u32[]{:S(2)}, u32[]{:S(2)}) collective-permute-start(bf16[3,96,768]{2,1,0:T(8,128)(2,1)S(1)} %copy-done.5), channel_id=1, source_target_pairs={{0,4},{4,0},{8,12},{12,8},{16,20},{20,16},{24,28},{28,24},{1,5},{5... | collective-permute-start | bytes 1327112 | tf_op jit(solution)/shard_map/ppermute | solution.py:1160
  58.6 3.2 %collective-permute-start.8 = (bf16[3,96,768]{2,1,0:T(8,128)(2,1)S(1)}, bf16[3,96,768]{2,1,0:T(8,128)(2,1)S(1)}, u32[]{:S(2)}, u32[]{:S(2)}) collective-permute-start(bf16[3,96,768]{2,1,0:T(8,128)(2,1)S(1)} %collective-permute-done.4.rest_4_), channel_id=1, source_target_pairs={{0,4},{4,0},{8,12},{12,8},{16,20},{20,16},{24,28},{28,24},{1,5},{5... | collective-permute-start | bytes 1327112 | tf_op jit(solution)/shard_map/ppermute | solution.py:1160
  61.9 35.0 %collective-permute-start.10 = (bf16[3,96,768]{2,1,0:T(8,128)(2,1)}, bf16[3,96,768]{2,1,0:T(8,128)(2,1)S(1)}, u32[]{:S(2)}, u32[]{:S(2)}) collective-permute-start(bf16[3,96,768]{2,1,0:T(8,128)(2,1)} %get-tuple-element.84.rest_0_), channel_id=1, source_target_pairs={{0,8},{4,12},{8,0},{12,4},{16,24},{20,28},{24,16},{28,20},{1,9},{5... | collective-permute-start | bytes 1327112 | tf_op jit(solution)/shard_map/ppermute | solution.py:1160
  62.4 34.5 %collective-permute-start.11 = (bf16[3,96,768]{2,1,0:T(8,128)(2,1)}, bf16[3,96,768]{2,1,0:T(8,128)(2,1)S(1)}, u32[]{:S(2)}, u32[]{:S(2)}) collective-permute-start(bf16[3,96,768]{2,1,0:T(8,128)(2,1)} %get-tuple-element.84.rest_0_), channel_id=1, source_target_pairs={{0,16},{4,20},{8,24},{12,28},{16,0},{20,4},{24,8},{28,12},{1,17},{... | collective-permute-start | bytes 1327112 | tf_op jit(solution)/shard_map/ppermute | solution.py:1160
  63.4 33.5 %collective-permute-start.12 = (bf16[3,96,768]{2,1,0:T(8,128)(2,1)}, bf16[3,96,768]{2,1,0:T(8,128)(2,1)S(1)}, u32[]{:S(2)}, u32[]{:S(2)}) collective-permute-start(bf16[3,96,768]{2,1,0:T(8,128)(2,1)} %get-tuple-element.84.rest_0_), channel_id=1, source_target_pairs={{0,24},{4,28},{8,16},{12,20},{16,8},{20,12},{24,0},{28,4},{1,25},{... | collective-permute-start | bytes 1327112 | tf_op jit(solution)/shard_map/ppermute | solution.py:1160
  97.0 15.4 %collective-permute-start.13 = (bf16[3,96,768]{2,1,0:T(8,128)(2,1)S(1)}, bf16[3,96,768]{2,1,0:T(8,128)(2,1)S(1)}, u32[]{:S(2)}, u32[]{:S(2)}) collective-permute-start(bf16[3,96,768]{2,1,0:T(8,128)(2,1)S(1)} %copy-done), channel_id=1, source_target_pairs={{0,4},{4,0},{8,12},{12,8},{16,20},{20,16},{24,28},{28,24},{1,5},{5... | collective-permute-start | bytes 1327112 | tf_op jit(solution)/shard_map/ppermute | solution.py:1160
  98.3 14.1 %collective-permute-start.14 = (bf16[3,96,768]{2,1,0:T(8,128)(2,1)S(1)}, bf16[3,96,768]{2,1,0:T(8,128)(2,1)S(1)}, u32[]{:S(2)}, u32[]{:S(2)}) collective-permute-start(bf16[3,96,768]{2,1,0:T(8,128)(2,1)S(1)} %collective-permute-done.10.rest_2_), channel_id=1, source_target_pairs={{0,4},{4,0},{8,12},{12,8},{16,20},{20,16},{24,28},{28,24},{1,5},{5... | collective-permute-start | bytes 1327112 | tf_op jit(solution)/shard_map/ppermute | solution.py:1160
  98.4 14.0 %collective-permute-start.15 = (bf16[3,96,768]{2,1,0:T(8,128)(2,1)S(1)}, bf16[3,96,768]{2,1,0:T(8,128)(2,1)S(1)}, u32[]{:S(2)}, u32[]{:S(2)}) collective-permute-start(bf16[3,96,768]{2,1,0:T(8,128)(2,1)S(1)} %collective-permute-done.11.rest_4_), channel_id=1, source_target_pairs={{0,4},{4,0},{8,12},{12,8},{16,20},{20,16},{24,28},{28,24},{1,5},{5... | collective-permute-start | bytes 1327112 | tf_op jit(solution)/shard_map/ppermute | solution.py:1160
  98.8 14.4 %collective-permute-start.16 = (bf16[3,96,768]{2,1,0:T(8,128)(2,1)S(1)}, bf16[3,96,768]{2,1,0:T(8,128)(2,1)}, u32[]{:S(2)}, u32[]{:S(2)}) collective-permute-start(bf16[3,96,768]{2,1,0:T(8,128)(2,1)S(1)} %collective-permute-done.12.rest_6_), channel_id=1, source_target_pairs={{0,4},{4,0},{8,12},{12,8},{16,20},{20,16},{24,28},{28,24},{1,5},{5... | collective-permute-start | bytes 1327112 | tf_op jit(solution)/shard_map/ppermute | solution.py:1160
  124.7 4.7 %collective-permute-start.17 = (bf16[8,768]{1,0:T(8,128)(2,1)S(1)}, bf16[8,768]{1,0:T(8,128)(2,1)S(1)}, u32[]{:S(2)}, u32[]{:S(2)}) collective-permute-start(bf16[8,768]{1,0:T(8,128)(2,1)S(1)} %get-tuple-element.166), channel_id=1, source_target_pairs={{0,1},{1,0},{2,3},{3,2},{4,5},{5,4},{6,7},{7,6},{8,9},{9,8},{10,11... | collective-permute-start | bytes 36872 | tf_op jit(solution)/shard_map/ppermute | solution.py:1163
  124.8 5.5 %collective-permute-start.18 = (bf16[8,768]{1,0:T(8,128)(2,1)S(1)}, bf16[8,768]{1,0:T(8,128)(2,1)S(1)}, u32[]{:S(2)}, u32[]{:S(2)}) collective-permute-start(bf16[8,768]{1,0:T(8,128)(2,1)S(1)} %get-tuple-element.166), channel_id=1, source_target_pairs={{0,2},{1,3},{2,0},{3,1},{4,6},{5,7},{6,4},{7,5},{8,10},{9,11},{10,... | collective-permute-start | bytes 36872 | tf_op jit(solution)/shard_map/ppermute | solution.py:1163
  134.6 4.0 %collective-permute-start.21 = (bf16[64,768]{1,0:T(8,128)(2,1)S(1)}, bf16[64,768]{1,0:T(8,128)(2,1)S(1)}, u32[]{:S(2)}, u32[]{:S(2)}) collective-permute-start(bf16[64,768]{1,0:T(8,128)(2,1)S(1)} %constant_dynamic-update-slice_fusion.refs_0_), channel_id=1, source_target_pairs={{0,8},{4,12},{8,0},{12,4},{16,24},{20,28},{24,16},{28,20},{1,9},{5... | collective-permute-start | bytes 294920 | tf_op jit(solution)/shard_map/ppermute | solution.py:1160
  135.2 3.8 %collective-permute-start.22 = (bf16[64,768]{1,0:T(8,128)(2,1)S(1)}, bf16[64,768]{1,0:T(8,128)(2,1)S(1)}, u32[]{:S(2)}, u32[]{:S(2)}) collective-permute-start(bf16[64,768]{1,0:T(8,128)(2,1)S(1)} %constant_dynamic-update-slice_fusion.refs_0_), channel_id=1, source_target_pairs={{0,16},{4,20},{8,24},{12,28},{16,0},{20,4},{24,8},{28,12},{1,17},{... | collective-permute-start | bytes 294920 | tf_op jit(solution)/shard_map/ppermute | solution.py:1160
  136.2 5.7 %collective-permute-start.23 = (bf16[64,768]{1,0:T(8,128)(2,1)S(1)}, bf16[64,768]{1,0:T(8,128)(2,1)S(1)}, u32[]{:S(2)}, u32[]{:S(2)}) collective-permute-start(bf16[64,768]{1,0:T(8,128)(2,1)S(1)} %constant_dynamic-update-slice_fusion.refs_0_), channel_id=1, source_target_pairs={{0,24},{4,28},{8,16},{12,20},{16,8},{20,12},{24,0},{28,4},{1,25},{... | collective-permute-start | bytes 294920 | tf_op jit(solution)/shard_map/ppermute | solution.py:1160
  185.6 6.0 %collective-permute-start.24 = (bf16[4,4,112,768]{3,2,1,0:T(8,128)(2,1)}, bf16[4,4,112,768]{3,2,1,0:T(8,128)(2,1)S(1)}, u32[]{:S(2)}, u32[]{:S(2)}) collective-permute-start(bf16[4,4,112,768]{3,2,1,0:T(8,128)(2,1)} %get-tuple-element.100), channel_id=1, source_target_pairs={{0,4},{4,0},{8,12},{12,8},{16,20},{20,16},{24,28},{28,24},{1,5},{5... | collective-permute-start | bytes 8257544 | tf_op jit(solution)/shard_map/ppermute | solution.py:1160
  193.7 36.0 %collective-permute-start.25 = (bf16[4,112,768]{2,1,0:T(8,128)(2,1)S(1)}, bf16[4,112,768]{2,1,0:T(8,128)(2,1)S(1)}, u32[]{:S(2)}, u32[]{:S(2)}) collective-permute-start(bf16[4,112,768]{2,1,0:T(8,128)(2,1)S(1)} %get-tuple-element.167), channel_id=1, source_target_pairs={{0,8},{4,12},{8,0},{12,4},{16,24},{20,28},{24,16},{28,20},{1,9},{5... | collective-permute-start | bytes 2064392 | tf_op jit(solution)/shard_map/ppermute | solution.py:1160
  194.7 34.9 %collective-permute-start.26 = (bf16[4,112,768]{2,1,0:T(8,128)(2,1)S(1)}, bf16[4,112,768]{2,1,0:T(8,128)(2,1)S(1)}, u32[]{:S(2)}, u32[]{:S(2)}) collective-permute-start(bf16[4,112,768]{2,1,0:T(8,128)(2,1)S(1)} %get-tuple-element.168), channel_id=1, source_target_pairs={{0,16},{4,20},{8,24},{12,28},{16,0},{20,4},{24,8},{28,12},{1,17},{... | collective-permute-start | bytes 2064392 | tf_op jit(solution)/shard_map/ppermute | solution.py:1160
  195.6 34.0 %collective-permute-start.27 = (bf16[4,112,768]{2,1,0:T(8,128)(2,1)S(1)}, bf16[4,112,768]{2,1,0:T(8,128)(2,1)S(1)}, u32[]{:S(2)}, u32[]{:S(2)}) collective-permute-start(bf16[4,112,768]{2,1,0:T(8,128)(2,1)S(1)} %get-tuple-element.169), channel_id=1, source_target_pairs={{0,24},{4,28},{8,16},{12,20},{16,8},{20,12},{24,0},{28,4},{1,25},{... | collective-permute-start | bytes 2064392 | tf_op jit(solution)/shard_map/ppermute | solution.py:1160
  229.7 7.3 %collective-permute-start.31 = (bf16[4,2,96,768]{3,2,1,0:T(8,128)(2,1)}, bf16[4,2,96,768]{3,2,1,0:T(8,128)(2,1)S(1)}, u32[]{:S(2)}, u32[]{:S(2)}) collective-permute-start(bf16[4,2,96,768]{3,2,1,0:T(8,128)(2,1)} %get-tuple-element.108), channel_id=1, source_target_pairs={{0,4},{4,0},{8,12},{12,8},{16,20},{20,16},{24,28},{28,24},{1,5},{5... | collective-permute-start | bytes 3538952 | tf_op jit(solution)/shard_map/ppermute | solution.py:1160
  233.9 16.1 %collective-permute-start.28 = (bf16[112,768]{1,0:T(8,128)(2,1)S(1)}, bf16[112,768]{1,0:T(8,128)(2,1)S(1)}, u32[]{:S(2)}, u32[]{:S(2)}) collective-permute-start(bf16[112,768]{1,0:T(8,128)(2,1)S(1)} %get-tuple-element.170), channel_id=1, source_target_pairs={{0,1},{1,0},{2,3},{3,2},{4,5},{5,4},{6,7},{7,6},{8,9},{9,8},{10,11... | collective-permute-start | bytes 516104 | tf_op jit(solution)/shard_map/ppermute | solution.py:1163
  235.7 15.6 %collective-permute-start.29 = (bf16[112,768]{1,0:T(8,128)(2,1)S(1)}, bf16[112,768]{1,0:T(8,128)(2,1)S(1)}, u32[]{:S(2)}, u32[]{:S(2)}) collective-permute-start(bf16[112,768]{1,0:T(8,128)(2,1)S(1)} %get-tuple-element.172), channel_id=1, source_target_pairs={{0,2},{1,3},{2,0},{3,1},{4,6},{5,7},{6,4},{7,5},{8,10},{9,11},{10,... | collective-permute-start | bytes 516104 | tf_op jit(solution)/shard_map/ppermute | solution.py:1163
  235.7 27.4 %collective-permute-start.30 = (bf16[112,768]{1,0:T(8,128)(2,1)S(1)}, bf16[112,768]{1,0:T(8,128)(2,1)S(1)}, u32[]{:S(2)}, u32[]{:S(2)}) collective-permute-start(bf16[112,768]{1,0:T(8,128)(2,1)S(1)} %get-tuple-element.171), channel_id=1, source_target_pairs={{0,3},{1,2},{2,1},{3,0},{4,7},{5,6},{6,5},{7,4},{8,11},{9,10},{10,... | collective-permute-start | bytes 516104 | tf_op jit(solution)/shard_map/ppermute | solution.py:1163
  238.3 33.7 %all-to-all-start = ((bf16[4,2,96,768]{3,2,1,0:T(8,128)(2,1)}), bf16[4,2,96,768]{3,2,1,0:T(8,128)(2,1)S(1)}, u32[]{:S(2)}, u32[]{:S(2)}) async-start(bf16[4,2,96,768]{3,2,1,0:T(8,128)(2,1)} %add_convert_fusion), calls=%async_computation | async-start | bytes 2359296 | tf_op jit(solution)/shard_map/all_to_all | solution.py:1329
  (33 other events, 246.8 us)
Sparse Core Ops, SparseCore 0:
  15.8 32.6 all-gather.7
  51.6 53.1 all-gather.9
  186.8 72.1 all-gather.5

commit v3 on v2

--- a/solution.py
+++ b/solution.py
@@ -1122,7 +1122,7 @@
         + [jax.ShapeDtypeStruct(shape, bf16)] * n,
         input_output_aliases={13: 0},
         compiler_params=pltpu.CompilerParams(vmem_limit_bytes=VMEM),
-        cost_estimate=cost(2 * 10**10, 2**24),
+        cost_estimate=cost(10**6, 10**6),
         name="ffn_tail",
     )(place, order, a2, mid, part, res, segs, d_pool, gain, own_b, own_c, far_b, far_c, out)
 
@@ -1270,7 +1270,7 @@
     if split:
         grad_project, d_gain_end = made[1], made[2]
     grad_gain_final = lax.dynamic_slice_in_dim(d_gain_end[0], dp * block, block, 0)
-    d_tokens = lax.all_gather(d_tok, "tp", axis=0, tiled=True).astype(f32)
+    d_tokens = lax.all_gather(d_tok, "tp", axis=0, tiled=True)
 
     d_rel = jnp.einsum(
         "khn,nb->kbh",
@@ -1325,7 +1325,7 @@
         chips = [[c + core for c in range(0, n_dp, 2)] for core in range(2)]
         give_f = over_dp(after(parts_f[1], got_a), 1)
         pair_f = parts_f[0].astype(f32) + give_f.astype(f32)
-        own_a = rounded(total(got_a))
+        own_a = rounded(total(after(got_a, (d_tokens, pair_f))))
         swapped = lax.all_to_all(
             pair_f.astype(bf16), "dp", 0, 0, axis_index_groups=chips, tiled=True
         )
@@ -1350,7 +1350,7 @@
         gain_one, gain_two = lax.dynamic_slice_in_dim(gains, dp * block, block, 1)
     return (
         layer_out,
-        d_tokens,
+        d_tokens.astype(f32),
         grad_a[:block, :cols],
         grad_a[:block, cols : 2 * cols],
         grad_a[:block, 2 * cols : 3 * cols],

time: 285 us -> 280 us (0.982)
  the two profiles are of different devices: /device:TPU:11 before, /device:TPU:0 now
where the time goes in v3:
time: 280 us; the launch traced here: 275 us
  Pallas kernels  149 us (53%)
  starting transfers between devices  39.1 us (14%)
  waiting for transfers between devices  34.1 us (12%)
  other arithmetic  21.4 us (8%)
  between operations  14.9 us (5%)
  local copies, waits for them, and re-layouts  14.2 us (5%)
    pallas_call x2, Pallas kernels, attention(): pl.pallas_call(functools.partial(attn_kernel, heads, hd, n, low, keeps),...  44 us
    pallas_call x1, Pallas kernels, ffn_tail(): pl.pallas_call(functools.partial(ffn_tail_kernel, block), grid_spec=pltpu...  33.3 us
    pallas_call x1, Pallas kernels, row_back(): pl.pallas_call(functools.partial(row_back_kernel, len(pieces), with_loss,...  31.8 us
    ppermute x9, starting transfers between devices, over_tp(): return lax.ppermute(value, 'tp', levels[k])  19 us
    ppermute x23, waiting for transfers between devices, over_dp(): return lax.ppermute(value, 'dp', mates[m])  18.3 us
    ppermute x23, starting transfers between devices, over_dp(): return lax.ppermute(value, 'dp', mates[m])  16.2 us
    pallas_call x1, Pallas kernels, ffn_own(): pl.pallas_call(ffn_own_kernel, grid=(rows,), in_specs=[by_row, pl.BlockSp...  13.5 us
    pallas_call x1, Pallas kernels, ffn_first(): pl.pallas_call(functools.partial(ffn_first_kernel, n), grid_spec=pltpu.Pr...  11.5 us
  transfers between devices with their start and end apart: 36, of which 15 were waited for; matrix products, arithmetic and copies ran while one was open for 10% of the time, Pallas kernels for 37%

profile of v3, /device:TPU:0, one launch (start us, length us, event | category | flops | bytes accessed | tf_op | source)
XLA Modules:
  0.0 274.8 jit_solution(18247160375347842638)
XLA Ops:
  11.3 3.0 %collective-permute-start = (bf16[112,768]{1,0:T(8,128)(2,1)S(1)}, bf16[112,768]{1,0:T(8,128)(2,1)S(1)}, u32[]{:S(2)}, u32[]{:S(2)}) collective-permute-start(bf16[112,768]{1,0:T(8,128)(2,1)S(1)} %get-tuple-element.66), channel_id=1, source_target_pairs={{0,1},{1,0},{2,3},{3,2},{4,5},{5,4},{6,7},{7,6},{8,9},{9,8},{10,11... | collective-permute-start | bytes 516104 | tf_op jit(solution)/shard_map/ppermute | solution.py:1163
  14.3 2.6 collective-permute-start.1
  18.7 2.6 fusion
  21.4 4.5 %fusion.2.a1_ref = bf16[2048,768]{1,0:T(8,128)(2,1)} fusion(bf16[2048,768]{1,0:T(8,128)(2,1)} %refs_16_.1, f32[768]{0:T(1024)S(1)} %copy-done.23, f32[2048]{0:T(1024)S(1)} %add_rsqrt_fusion), kind=kLoop, calls=%fused_computation.4 | loop fusion | flops 6291456 | bytes 6302720 | tf_op jit(solution)/shard_map/convert_element_type | solution.py:1204
  26.0 3.9 %collective-permute-done.1.refs_1_ = bf16[112,768]{1,0:T(8,128)(2,1)S(1)} collective-permute-done((bf16[112,768]{1,0:T(8,128)(2,1)S(1)}, bf16[112,768]{1,0:T(8,128)(2,1)S(1)}, u32[]{:S(2)}, u32[]{:S(2)}) %collective-permute-start.1) | collective-permute-done | bytes 172064 | tf_op jit(solution)/shard_map/ppermute | solution.py:1163
  31.2 1.9 stack.1
  33.1 1.5 collective-permute-start.3
  34.6 1.5 collective-permute-start.4
  36.6 11.7 %attn_own.1 = (bf16[4,576,512]{2,1,0:T(8,128)(2,1)}, f32[4,3,512]{2,1,0:T(4,128)S(1)}, bf16[4,4,192,512]{3,2,1,0:T(8,128)(2,1)}, bf16[4,768,768]{2,1,0:T(8,128)(2,1)}) custom-call(s32[8]{0:T(128)S(1)} %xor_multiply_fusion.place_ref, s32[4]{0:T(128)S(1)} %iota_xor_fusion.order_ref, bf16[2048,768]{1,0:T(8,128)(2,1)} %fusion.2.a1_ref, ...), custom_call_target="tpu_custom_call" | custom-call | flops 10000000000 | bytes 1048576 | tf_op jit(solution)/shard_map/attn_own/pallas_call | solution.py:361
  48.4 4.5 %collective-permute-done.4.rest_4_ = bf16[3,96,768]{2,1,0:T(8,128)(2,1)} collective-permute-done((bf16[3,96,768]{2,1,0:T(8,128)(2,1)}, bf16[3,96,768]{2,1,0:T(8,128)(2,1)}, u32[]{:S(2)}, u32[]{:S(2)}) %collective-permute-start.4) | collective-permute-done | bytes 442400 | tf_op jit(solution)/shard_map/ppermute | solution.py:1160
  52.9 3.0 %others_of.1 = (bf16[3,96,768]{2,1,0:T(8,128)(2,1)}, bf16[3,96,768]{2,1,0:T(8,128)(2,1)}) custom-call(s32[4]{0:T(128)} %copy-done.3, bf16[4,192,768]{2,1,0:T(8,128)(2,1)} %bitcast.72), custom_call_target="tpu_custom_call" | custom-call | bytes 2359296 | tf_op jit(solution)/shard_map/others_of/pallas_call | solution.py:223
  62.5 1.4 collective-permute-start.12
  63.9 32.3 %attn_far.1 = (bf16[4,576,512]{2,1,0:T(8,128)(2,1)}, f32[4,3,512]{2,1,0:T(4,128)S(1)}, bf16[4,4,192,512]{3,2,1,0:T(8,128)(2,1)}, bf16[4,768,768]{2,1,0:T(8,128)(2,1)}) custom-call(s32[8]{0:T(128)S(1)} %xor_multiply_fusion.place_ref, s32[4]{0:T(128)S(1)} %copy-done.4, ...), custom_call_target="tpu_custom_call", output_to_operand_aliasing={{0}: (13, {}), {1}: (14, {}), {2}: (15, {}), {3}: (16, {})} | custom-call | flops 30000001024 | bytes 1048576 | tf_op jit(solution)/shard_map/attn_far/pallas_call | solution.py:361
  97.4 13.5 %ffn_own.1 = (bf16[2048,768]{1,0:T(8,128)(2,1)}, bf16[2048,768]{1,0:T(8,128)(2,1)}, bf16[2048,768]{1,0:T(8,128)(2,1)}) custom-call(bf16[2048,768]{1,0:T(8,128)(2,1)} %refs_16_.1, bf16[4,4,192,512]{3,2,1,0:T(8,128)(2,1)} %get-tuple-element.81.ctx_ref.refs_23_, bf16[4,768,768]{2,1,0:T(8,128)(2,1)} %get-tuple-element.82.wo_ref.refs_21_, ...), custom_call_target="tpu_custom_call" | custom-call | flops 7247757312 | bytes 16777216 | tf_op jit(solution)/shard_map/ffn_own/pallas_call | solution.py:423
  111.8 11.5 %ffn_first.1 = (bf16[2048,768]{1,0:T(8,128)(2,1)}, bf16[512,768]{1,0:T(8,128)(2,1)}, f32[8,768]{1,0:T(8,128)S(1)}, bf16[3,768,768]{2,1,0:T(8,128)(2,1)}, bf16[3,768,768]{2,1,0:T(8,128)(2,1)}) custom-call(s32[8]{0:T(128)S(1)} %xor_multiply_fusion.place_ref, s32[4]{0:T(128)S(1)} %copy-done.4, bf16[2048,768]{1,0:T(8,128)(2,1)} %get-tuple-element.83.a2_ref.refs_15_, ...), custom_call_target="tpu_custom_call" | custom-call | flops 3623878656 | bytes 16777216 | tf_op jit(solution)/shard_map/ffn_first/pallas_call | solution.py:515
  123.3 4.6 %collective-permute-start.17 = (bf16[8,768]{1,0:T(8,128)(2,1)S(1)}, bf16[8,768]{1,0:T(8,128)(2,1)S(1)}, u32[]{:S(2)}, u32[]{:S(2)}) collective-permute-start(bf16[8,768]{1,0:T(8,128)(2,1)S(1)} %get-tuple-element.174), channel_id=1, source_target_pairs={{0,1},{1,0},{2,3},{3,2},{4,5},{5,4},{6,7},{7,6},{8,9},{9,8},{10,11... | collective-permute-start | bytes 36872 | tf_op jit(solution)/shard_map/ppermute | solution.py:1163
  127.9 3.0 %collective-permute-start.18 = (bf16[8,768]{1,0:T(8,128)(2,1)S(1)}, bf16[8,768]{1,0:T(8,128)(2,1)S(1)}, u32[]{:S(2)}, u32[]{:S(2)}) collective-permute-start(bf16[8,768]{1,0:T(8,128)(2,1)S(1)} %get-tuple-element.174), channel_id=1, source_target_pairs={{0,2},{1,3},{2,0},{3,1},{4,6},{5,7},{6,4},{7,5},{8,10},{9,11},{10,... | collective-permute-start | bytes 36872 | tf_op jit(solution)/shard_map/ppermute | solution.py:1163
  132.6 3.8 %collective-permute-done.19 = bf16[8,768]{1,0:T(8,128)(2,1)S(1)} collective-permute-done((bf16[8,768]{1,0:T(8,128)(2,1)S(1)}, bf16[8,768]{1,0:T(8,128)(2,1)S(1)}, u32[]{:S(2)}, u32[]{:S(2)}) %collective-permute-start.19) | collective-permute-done | bytes 12320 | tf_op jit(solution)/shard_map/ppermute | solution.py:1163
  138.8 1.6 collective-permute-start.22
  142.5 2.1 collective-permute-done.22.refs_2_
  145.9 31.8 %row_back.1 = (f32[32,768]{1,0:T(8,128)S(1)}, f32[96,768]{1,0:T(8,128)}, f32[1,768]{1,0:T(1,128)S(1)}, f32[1,768]{1,0:T(1,128)S(1)}, bf16[512,768]{1,0:T(8,128)(...) custom-call(s32[33]{0:T(128)S(1)} %pad_add_fusion.1.at_ref, ...), custom_call_target="tpu_custom_call" | custom-call | flops 30000001024 | bytes 16777216 | tf_op jit(solution)/shard_map/row_back/pallas_call | solution.py:836
  180.6 9.0 %attn_weights.1 = (bf16[4,4,112,768]{3,2,1,0:T(8,128)(2,1)}, bf16[4,4,112,768]{3,2,1,0:T(8,128)(2,1)}) custom-call(s32[6]{0:T(128)S(1)} %pad_add_fusion.place_ref, bf16[2048,768]{1,0:T(8,128)(2,1)} %fusion.2.a1_ref, bf16[512,768]{1,0:T(8,128)(2,1)S(1)} %get-tuple-element.98.dattn_ref, bf16[4,576,512]{2,1,0:T(8,128)(2,1)} %get-tuple-element.99.dqkv_ref, ...), custom_call_target="tpu_custom_call" | custom-call | flops 1000000 | bytes 1000000 | tf_op jit(solution)/shard_map/attn_weights/pallas_call | solution.py:980
  189.6 5.3 %collective-permute-done.24 = bf16[4,4,112,768]{3,2,1,0:T(8,128)(2,1)S(1)} collective-permute-done((bf16[4,4,112,768]{3,2,1,0:T(8,128)(2,1)}, bf16[4,4,112,768]{3,2,1,0:T(8,128)(2,1)S(1)}, u32[]{:S(2)}, u32[]{:S(2)}) %collective-permute-start.24) | collective-permute-done | bytes 2752544 | tf_op jit(solution)/shard_map/ppermute | solution.py:1160
  194.9 2.7 fusion.17
  199.4 1.8 collective-permute-start.27
  201.2 33.3 %ffn_tail.1 = (bf16[2048,768]{1,0:T(8,128)(2,1)}, bf16[4,2,96,768]{3,2,1,0:T(8,128)(2,1)}, bf16[4,2,96,768]{3,2,1,0:T(8,128)(2,1)}) custom-call(s32[6]{0:T(128)S(1)} %pad_add_fusion.place_ref, s32[4]{0:T(128)S(1)} %copy-done.4, bf16[2048,768]{1,0:T(8,128)(2,1)} %get-tuple-element.83.a2_ref.refs_15_, ...), custom_call_target="tpu_custom_call", output_to_operand_aliasing={{0}: (13, {})} | custom-call | flops 1000000 | bytes 1000000 | tf_op jit(solution)/shard_map/ffn_tail/pallas_call | solution.py:1095
  236.2 3.3 %all-gather.6.cloned.1.call-done = bf16[2048,768]{1,0:T(8,128)(2,1)} async-done(((bf16[512,768]{1,0:T(8,128)(2,1)}), bf16[2048,768]{1,0:T(8,128)(2,1)}) %all-gather.6.cloned.1.call-update) | async-done | bytes 3145744 | tf_op jit(solution)/shard_map/all_gather | solution.py:1273
  239.5 2.9 %fusion.18 = (bf16[4,112,768]{2,1,0:T(8,128)(2,1)S(1)}, f32[4,112,768]{2,1,0:T(8,128)}) fusion(bf16[4,112,768]{2,1,0:T(8,128)(2,1)} %copy-done.11, bf16[4,112,768]{2,1,0:T(8,128)(2,1)} %copy-done.10, f32[4,112,768]{2,1,0:T(8,128)S(1)} %get-tuple-element.113, bf16[4,112,768]{2,1,0:T(8,128)(2,1)S(1)} %collective-permute-done.25), kind=kLoop, calls=%fused_computation.66 | loop fusion | flops 2752512 | bytes 5505024 | tf_op jit(solution)/shard_map/convert.2
  244.4 3.1 %collective-permute-start.31 = (bf16[112,768]{1,0:T(8,128)(2,1)S(1)}, bf16[112,768]{1,0:T(8,128)(2,1)S(1)}, u32[]{:S(2)}, u32[]{:S(2)}) collective-permute-start(bf16[112,768]{1,0:T(8,128)(2,1)S(1)} %get-tuple-element.180), channel_id=1, source_target_pairs={{0,3},{1,2},{2,1},{3,0},{4,7},{5,6},{6,5},{7,4},{8,11},{9,10},{10,... | collective-permute-start | bytes 516104 | tf_op jit(solution)/shard_map/ppermute | solution.py:1163
  248.8 3.7 %all-to-all-start = ((bf16[4,2,96,768]{3,2,1,0:T(8,128)(2,1)}), bf16[4,2,96,768]{3,2,1,0:T(8,128)(2,1)S(1)}, u32[]{:S(2)}, u32[]{:S(2)}) async-start(bf16[4,2,96,768]{3,2,1,0:T(8,128)(2,1)} %fusion.14), calls=%async_computation | async-start | bytes 2359296 | tf_op jit(solution)/shard_map/all_to_all | solution.py:1329
  253.1 5.1 %convert_element_type.158 = f32[2048,768]{1,0:T(8,128)} convert(bf16[2048,768]{1,0:T(8,128)(2,1)} %all-gather.6.cloned.1.call-done) | non-fusion elementwise | flops 1572864 | bytes 9437184 | tf_op jit(solution)/shard_map/convert_element_type | solution.py:1353
  262.5 4.3 %all-to-all-done = bf16[4,2,96,768]{3,2,1,0:T(8,128)(2,1)S(1)} async-done(((bf16[4,2,96,768]{3,2,1,0:T(8,128)(2,1)}), bf16[4,2,96,768]{3,2,1,0:T(8,128)(2,1)S(1)}, u32[]{:S(2)}, u32[]{:S(2)}) %all-to-all-start) | async-done | bytes 1179680 | tf_op jit(solution)/shard_map/all_to_all | solution.py:1329
  (177 shorter events, 39.2 us)
Async XLA Ops:
  7.2 45.7 %all-gather.8.cloned.1.call-start = ((), (), s32[]{:S(2)}) async-start(), calls=%async_computation.2 | async-start | bytes 1474560 | tf_op jit(solution)/shard_map/all_gather | solution.py:1193
  11.3 14.7 %collective-permute-start = (bf16[112,768]{1,0:T(8,128)(2,1)S(1)}, bf16[112,768]{1,0:T(8,128)(2,1)S(1)}, u32[]{:S(2)}, u32[]{:S(2)}) collective-permute-start(bf16[112,768]{1,0:T(8,128)(2,1)S(1)} %get-tuple-element.66), channel_id=1, source_target_pairs={{0,1},{1,0},{2,3},{3,2},{4,5},{5,4},{6,7},{7,6},{8,9},{9,8},{10,11... | collective-permute-start | bytes 516104 | tf_op jit(solution)/shard_map/ppermute | solution.py:1163
  14.3 15.6 %collective-permute-start.1 = (bf16[112,768]{1,0:T(8,128)(2,1)S(1)}, bf16[112,768]{1,0:T(8,128)(2,1)S(1)}, u32[]{:S(2)}, u32[]{:S(2)}) collective-permute-start(bf16[112,768]{1,0:T(8,128)(2,1)S(1)} %get-tuple-element.66), channel_id=1, source_target_pairs={{0,2},{1,3},{2,0},{3,1},{4,6},{5,7},{6,4},{7,5},{8,10},{9,11},{10,... | collective-permute-start | bytes 516104 | tf_op jit(solution)/shard_map/ppermute | solution.py:1163
  16.9 13.0 %collective-permute-start.2 = (bf16[112,768]{1,0:T(8,128)(2,1)S(1)}, bf16[112,768]{1,0:T(8,128)(2,1)S(1)}, u32[]{:S(2)}, u32[]{:S(2)}) collective-permute-start(bf16[112,768]{1,0:T(8,128)(2,1)S(1)} %get-tuple-element.66), channel_id=1, source_target_pairs={{0,3},{1,2},{2,1},{3,0},{4,7},{5,6},{6,5},{7,4},{8,11},{9,10},{10,... | collective-permute-start | bytes 516104 | tf_op jit(solution)/shard_map/ppermute | solution.py:1163
  18.6 93.2 %all-gather.10.cloned.1.call-start = ((), (), s32[]{:S(2)}) async-start(), calls=%async_computation.3 | async-start | bytes 3981312 | tf_op jit(solution)/shard_map/all_gather | solution.py:1211
  33.1 15.3 %collective-permute-start.3 = (bf16[3,96,768]{2,1,0:T(8,128)(2,1)}, bf16[3,96,768]{2,1,0:T(8,128)(2,1)S(1)}, u32[]{:S(2)}, u32[]{:S(2)}) collective-permute-start(bf16[3,96,768]{2,1,0:T(8,128)(2,1)} %get-tuple-element.77.rest_0_), channel_id=1, source_target_pairs={{0,8},{4,12},{8,0},{12,4},{16,24},{20,28},{24,16},{28,20},{1,9},{5... | collective-permute-start | bytes 1327112 | tf_op jit(solution)/shard_map/ppermute | solution.py:1160
  34.6 18.3 %collective-permute-start.4 = (bf16[3,96,768]{2,1,0:T(8,128)(2,1)}, bf16[3,96,768]{2,1,0:T(8,128)(2,1)}, u32[]{:S(2)}, u32[]{:S(2)}) collective-permute-start(bf16[3,96,768]{2,1,0:T(8,128)(2,1)} %get-tuple-element.77.rest_0_), channel_id=1, source_target_pairs={{0,16},{4,20},{8,24},{12,28},{16,0},{20,4},{24,8},{28,12},{1,17},{... | collective-permute-start | bytes 1327112 | tf_op jit(solution)/shard_map/ppermute | solution.py:1160
  36.1 16.8 %collective-permute-start.5 = (bf16[3,96,768]{2,1,0:T(8,128)(2,1)}, bf16[3,96,768]{2,1,0:T(8,128)(2,1)}, u32[]{:S(2)}, u32[]{:S(2)}) collective-permute-start(bf16[3,96,768]{2,1,0:T(8,128)(2,1)} %get-tuple-element.77.rest_0_), channel_id=1, source_target_pairs={{0,24},{4,28},{8,16},{12,20},{16,8},{20,12},{24,0},{28,4},{1,25},{... | collective-permute-start | bytes 1327112 | tf_op jit(solution)/shard_map/ppermute | solution.py:1160
  55.9 183.6 %all-gather.6.cloned.1.call-start = ((), (), s32[]{:S(2)}) async-start(), calls=%async_computation.1 | async-start | bytes 3932160 | tf_op jit(solution)/shard_map/all_gather | solution.py:1273
  57.1 3.3 %collective-permute-start.9 = (bf16[3,96,768]{2,1,0:T(8,128)(2,1)}, bf16[3,96,768]{2,1,0:T(8,128)(2,1)S(1)}, u32[]{:S(2)}, u32[]{:S(2)}) collective-permute-start(bf16[3,96,768]{2,1,0:T(8,128)(2,1)} %collective-permute-done.5.rest_6_), channel_id=1, source_target_pairs={{0,4},{4,0},{8,12},{12,8},{16,20},{20,16},{24,28},{28,24},{1,5},{5... | collective-permute-start | bytes 1327112 | tf_op jit(solution)/shard_map/ppermute | solution.py:1160
  60.4 35.8 %collective-permute-start.10 = (bf16[3,96,768]{2,1,0:T(8,128)(2,1)}, bf16[3,96,768]{2,1,0:T(8,128)(2,1)S(1)}, u32[]{:S(2)}, u32[]{:S(2)}) collective-permute-start(bf16[3,96,768]{2,1,0:T(8,128)(2,1)} %get-tuple-element.88.rest_0_), channel_id=1, source_target_pairs={{0,8},{4,12},{8,0},{12,4},{16,24},{20,28},{24,16},{28,20},{1,9},{5... | collective-permute-start | bytes 1327112 | tf_op jit(solution)/shard_map/ppermute | solution.py:1160
  61.7 34.6 %collective-permute-start.11 = (bf16[3,96,768]{2,1,0:T(8,128)(2,1)}, bf16[3,96,768]{2,1,0:T(8,128)(2,1)S(1)}, u32[]{:S(2)}, u32[]{:S(2)}) collective-permute-start(bf16[3,96,768]{2,1,0:T(8,128)(2,1)} %get-tuple-element.88.rest_0_), channel_id=1, source_target_pairs={{0,16},{4,20},{8,24},{12,28},{16,0},{20,4},{24,8},{28,12},{1,17},{... | collective-permute-start | bytes 1327112 | tf_op jit(solution)/shard_map/ppermute | solution.py:1160
  62.5 33.8 %collective-permute-start.12 = (bf16[3,96,768]{2,1,0:T(8,128)(2,1)}, bf16[3,96,768]{2,1,0:T(8,128)(2,1)S(1)}, u32[]{:S(2)}, u32[]{:S(2)}) collective-permute-start(bf16[3,96,768]{2,1,0:T(8,128)(2,1)} %get-tuple-element.88.rest_0_), channel_id=1, source_target_pairs={{0,24},{4,28},{8,16},{12,20},{16,8},{20,12},{24,0},{28,4},{1,25},{... | collective-permute-start | bytes 1327112 | tf_op jit(solution)/shard_map/ppermute | solution.py:1160
  96.3 14.6 %collective-permute-start.13 = (bf16[3,96,768]{2,1,0:T(8,128)(2,1)S(1)}, bf16[3,96,768]{2,1,0:T(8,128)(2,1)S(1)}, u32[]{:S(2)}, u32[]{:S(2)}) collective-permute-start(bf16[3,96,768]{2,1,0:T(8,128)(2,1)S(1)} %copy-done.2), channel_id=1, source_target_pairs={{0,4},{4,0},{8,12},{12,8},{16,20},{20,16},{24,28},{28,24},{1,5},{5... | collective-permute-start | bytes 1327112 | tf_op jit(solution)/shard_map/ppermute | solution.py:1160
  96.4 14.6 %collective-permute-start.14 = (bf16[3,96,768]{2,1,0:T(8,128)(2,1)S(1)}, bf16[3,96,768]{2,1,0:T(8,128)(2,1)S(1)}, u32[]{:S(2)}, u32[]{:S(2)}) collective-permute-start(bf16[3,96,768]{2,1,0:T(8,128)(2,1)S(1)} %collective-permute-done.10.rest_2_), channel_id=1, source_target_pairs={{0,4},{4,0},{8,12},{12,8},{16,20},{20,16},{24,28},{28,24},{1,5},{5... | collective-permute-start | bytes 1327112 | tf_op jit(solution)/shard_map/ppermute | solution.py:1160
  96.9 14.1 %collective-permute-start.15 = (bf16[3,96,768]{2,1,0:T(8,128)(2,1)S(1)}, bf16[3,96,768]{2,1,0:T(8,128)(2,1)S(1)}, u32[]{:S(2)}, u32[]{:S(2)}) collective-permute-start(bf16[3,96,768]{2,1,0:T(8,128)(2,1)S(1)} %collective-permute-done.11.rest_4_), channel_id=1, source_target_pairs={{0,4},{4,0},{8,12},{12,8},{16,20},{20,16},{24,28},{28,24},{1,5},{5... | collective-permute-start | bytes 1327112 | tf_op jit(solution)/shard_map/ppermute | solution.py:1160
  97.0 14.8 %collective-permute-start.16 = (bf16[3,96,768]{2,1,0:T(8,128)(2,1)S(1)}, bf16[3,96,768]{2,1,0:T(8,128)(2,1)}, u32[]{:S(2)}, u32[]{:S(2)}) collective-permute-start(bf16[3,96,768]{2,1,0:T(8,128)(2,1)S(1)} %collective-permute-done.12.rest_6_), channel_id=1, source_target_pairs={{0,4},{4,0},{8,12},{12,8},{16,20},{20,16},{24,28},{28,24},{1,5},{5... | collective-permute-start | bytes 1327112 | tf_op jit(solution)/shard_map/ppermute | solution.py:1160
  123.3 9.3 %collective-permute-start.17 = (bf16[8,768]{1,0:T(8,128)(2,1)S(1)}, bf16[8,768]{1,0:T(8,128)(2,1)S(1)}, u32[]{:S(2)}, u32[]{:S(2)}) collective-permute-start(bf16[8,768]{1,0:T(8,128)(2,1)S(1)} %get-tuple-element.174), channel_id=1, source_target_pairs={{0,1},{1,0},{2,3},{3,2},{4,5},{5,4},{6,7},{7,6},{8,9},{9,8},{10,11... | collective-permute-start | bytes 36872 | tf_op jit(solution)/shard_map/ppermute | solution.py:1163
  127.9 4.7 %collective-permute-start.18 = (bf16[8,768]{1,0:T(8,128)(2,1)S(1)}, bf16[8,768]{1,0:T(8,128)(2,1)S(1)}, u32[]{:S(2)}, u32[]{:S(2)}) collective-permute-start(bf16[8,768]{1,0:T(8,128)(2,1)S(1)} %get-tuple-element.174), channel_id=1, source_target_pairs={{0,2},{1,3},{2,0},{3,1},{4,6},{5,7},{6,4},{7,5},{8,10},{9,11},{10,... | collective-permute-start | bytes 36872 | tf_op jit(solution)/shard_map/ppermute | solution.py:1163
  130.9 5.5 %collective-permute-start.19 = (bf16[8,768]{1,0:T(8,128)(2,1)S(1)}, bf16[8,768]{1,0:T(8,128)(2,1)S(1)}, u32[]{:S(2)}, u32[]{:S(2)}) collective-permute-start(bf16[8,768]{1,0:T(8,128)(2,1)S(1)} %get-tuple-element.174), channel_id=1, source_target_pairs={{0,3},{1,2},{2,1},{3,0},{4,7},{5,6},{6,5},{7,4},{8,11},{9,10},{10,... | collective-permute-start | bytes 36872 | tf_op jit(solution)/shard_map/ppermute | solution.py:1163
  137.6 4.9 %collective-permute-start.21 = (bf16[64,768]{1,0:T(8,128)(2,1)S(1)}, bf16[64,768]{1,0:T(8,128)(2,1)S(1)}, u32[]{:S(2)}, u32[]{:S(2)}) collective-permute-start(bf16[64,768]{1,0:T(8,128)(2,1)S(1)} %constant_dynamic-update-slice_fusion.refs_0_), channel_id=1, source_target_pairs={{0,8},{4,12},{8,0},{12,4},{16,24},{20,28},{24,16},{28,20},{1,9},{5... | collective-permute-start | bytes 294920 | tf_op jit(solution)/shard_map/ppermute | solution.py:1160
  138.8 5.8 %collective-permute-start.22 = (bf16[64,768]{1,0:T(8,128)(2,1)S(1)}, bf16[64,768]{1,0:T(8,128)(2,1)S(1)}, u32[]{:S(2)}, u32[]{:S(2)}) collective-permute-start(bf16[64,768]{1,0:T(8,128)(2,1)S(1)} %constant_dynamic-update-slice_fusion.refs_0_), channel_id=1, source_target_pairs={{0,16},{4,20},{8,24},{12,28},{16,0},{20,4},{24,8},{28,12},{1,17},{... | collective-permute-start | bytes 294920 | tf_op jit(solution)/shard_map/ppermute | solution.py:1160
  140.4 5.5 %collective-permute-start.23 = (bf16[64,768]{1,0:T(8,128)(2,1)S(1)}, bf16[64,768]{1,0:T(8,128)(2,1)S(1)}, u32[]{:S(2)}, u32[]{:S(2)}) collective-permute-start(bf16[64,768]{1,0:T(8,128)(2,1)S(1)} %constant_dynamic-update-slice_fusion.refs_0_), channel_id=1, source_target_pairs={{0,24},{4,28},{8,16},{12,20},{16,8},{20,12},{24,0},{28,4},{1,25},{... | collective-permute-start | bytes 294920 | tf_op jit(solution)/shard_map/ppermute | solution.py:1160
  189.6 5.3 %collective-permute-start.24 = (bf16[4,4,112,768]{3,2,1,0:T(8,128)(2,1)}, bf16[4,4,112,768]{3,2,1,0:T(8,128)(2,1)S(1)}, u32[]{:S(2)}, u32[]{:S(2)}) collective-permute-start(bf16[4,4,112,768]{3,2,1,0:T(8,128)(2,1)} %get-tuple-element.104), channel_id=1, source_target_pairs={{0,4},{4,0},{8,12},{12,8},{16,20},{20,16},{24,28},{28,24},{1,5},{5... | collective-permute-start | bytes 8257544 | tf_op jit(solution)/shard_map/ppermute | solution.py:1160
  197.6 36.8 %collective-permute-start.25 = (bf16[4,112,768]{2,1,0:T(8,128)(2,1)S(1)}, bf16[4,112,768]{2,1,0:T(8,128)(2,1)S(1)}, u32[]{:S(2)}, u32[]{:S(2)}) collective-permute-start(bf16[4,112,768]{2,1,0:T(8,128)(2,1)S(1)} %get-tuple-element.176), channel_id=1, source_target_pairs={{0,8},{4,12},{8,0},{12,4},{16,24},{20,28},{24,16},{28,20},{1,9},{5... | collective-permute-start | bytes 2064392 | tf_op jit(solution)/shard_map/ppermute | solution.py:1160
  198.5 36.0 %collective-permute-start.26 = (bf16[4,112,768]{2,1,0:T(8,128)(2,1)S(1)}, bf16[4,112,768]{2,1,0:T(8,128)(2,1)S(1)}, u32[]{:S(2)}, u32[]{:S(2)}) collective-permute-start(bf16[4,112,768]{2,1,0:T(8,128)(2,1)S(1)} %get-tuple-element.177), channel_id=1, source_target_pairs={{0,16},{4,20},{8,24},{12,28},{16,0},{20,4},{24,8},{28,12},{1,17},{... | collective-permute-start | bytes 2064392 | tf_op jit(solution)/shard_map/ppermute | solution.py:1160
  199.4 35.1 %collective-permute-start.27 = (bf16[4,112,768]{2,1,0:T(8,128)(2,1)S(1)}, bf16[4,112,768]{2,1,0:T(8,128)(2,1)S(1)}, u32[]{:S(2)}, u32[]{:S(2)}) collective-permute-start(bf16[4,112,768]{2,1,0:T(8,128)(2,1)S(1)} %get-tuple-element.175), channel_id=1, source_target_pairs={{0,24},{4,28},{8,16},{12,20},{16,8},{20,12},{24,0},{28,4},{1,25},{... | collective-permute-start | bytes 2064392 | tf_op jit(solution)/shard_map/ppermute | solution.py:1160
  236.2 11.3 %collective-permute-start.28 = (bf16[4,2,96,768]{3,2,1,0:T(8,128)(2,1)}, bf16[4,2,96,768]{3,2,1,0:T(8,128)(2,1)S(1)}, u32[]{:S(2)}, u32[]{:S(2)}) collective-permute-start(bf16[4,2,96,768]{3,2,1,0:T(8,128)(2,1)} %get-tuple-element.112), channel_id=1, source_target_pairs={{0,4},{4,0},{8,12},{12,8},{16,20},{20,16},{24,28},{28,24},{1,5},{5... | collective-permute-start | bytes 3538952 | tf_op jit(solution)/shard_map/ppermute | solution.py:1160
  243.1 15.1 %collective-permute-start.29 = (bf16[112,768]{1,0:T(8,128)(2,1)}, bf16[112,768]{1,0:T(8,128)(2,1)S(1)}, u32[]{:S(2)}, u32[]{:S(2)}) collective-permute-start(bf16[112,768]{1,0:T(8,128)(2,1)} %get-tuple-element.179), channel_id=1, source_target_pairs={{0,1},{1,0},{2,3},{3,2},{4,5},{5,4},{6,7},{7,6},{8,9},{9,8},{10,11... | collective-permute-start | bytes 516104 | tf_op jit(solution)/shard_map/ppermute | solution.py:1163
  243.1 15.5 %collective-permute-start.30 = (bf16[112,768]{1,0:T(8,128)(2,1)S(1)}, bf16[112,768]{1,0:T(8,128)(2,1)S(1)}, u32[]{:S(2)}, u32[]{:S(2)}) collective-permute-start(bf16[112,768]{1,0:T(8,128)(2,1)S(1)} %get-tuple-element.181), channel_id=1, source_target_pairs={{0,2},{1,3},{2,0},{3,1},{4,6},{5,7},{6,4},{7,5},{8,10},{9,11},{10,... | collective-permute-start | bytes 516104 | tf_op jit(solution)/shard_map/ppermute | solution.py:1163
  244.4 14.3 %collective-permute-start.31 = (bf16[112,768]{1,0:T(8,128)(2,1)S(1)}, bf16[112,768]{1,0:T(8,128)(2,1)S(1)}, u32[]{:S(2)}, u32[]{:S(2)}) collective-permute-start(bf16[112,768]{1,0:T(8,128)(2,1)S(1)} %get-tuple-element.180), channel_id=1, source_target_pairs={{0,3},{1,2},{2,1},{3,0},{4,7},{5,6},{6,5},{7,4},{8,11},{9,10},{10,... | collective-permute-start | bytes 516104 | tf_op jit(solution)/shard_map/ppermute | solution.py:1163
  248.8 17.9 %all-to-all-start = ((bf16[4,2,96,768]{3,2,1,0:T(8,128)(2,1)}), bf16[4,2,96,768]{3,2,1,0:T(8,128)(2,1)S(1)}, u32[]{:S(2)}, u32[]{:S(2)}) async-start(bf16[4,2,96,768]{3,2,1,0:T(8,128)(2,1)} %fusion.14), calls=%async_computation | async-start | bytes 2359296 | tf_op jit(solution)/shard_map/all_to_all | solution.py:1329
  (34 other events, 227.8 us)
Sparse Core Ops, SparseCore 0:
  18.7 32.7 all-gather.7
  56.0 50.0 all-gather.9
  178.2 61.2 all-gather.5

commit v4 on v3

--- a/solution.py
+++ b/solution.py
@@ -12,6 +12,7 @@
 MAX_DIST = 128
 SEG_ROW = 8
 TILE = 128
+LONGEST = 256
 VMEM = 52 * 2**20
 
 epsilon = 1e-06
@@ -68,18 +69,15 @@
 
 
 def bring(place_ref, piece_refs, into, sems):
-    width = into.shape[1]
-    slices = width // len(piece_refs)
+    slices = into.shape[1] // len(piece_refs)
     copies = []
-    for m, piece in enumerate(piece_refs):
-        start = pl.multiple_of(place_ref[m], 16) if slices % 16 == 0 else place_ref[m]
-        if len(piece.shape) == 2:
-            piece, to = piece.at[pl.ds(0, slices)], into.at[0, pl.ds(start, slices)]
-        else:
-            to = into.at[:, pl.ds(start, slices), :]
-        copy = pltpu.make_async_copy(piece, to, sems.at[m])
-        copy.start()
-        copies.append(copy)
+    for k in range(into.shape[0]):
+        here = []
+        for m, piece in enumerate(piece_refs):
+            start = pl.multiple_of(place_ref[m], 16) if slices % 16 == 0 else place_ref[m]
+            to = into.at[k, pl.ds(start, slices), :]
+            here.append(pltpu.make_async_copy(piece.at[k], to, sems.at[k, m]))
+        copies.append(here)
     return copies
 
 
@@ -98,6 +96,10 @@
         return tile + bias_s[first + h, :, TILE : 2 * TILE]
     lane = 2 * TILE + 1 if offset > 1 else 2 * TILE - 1
     return tile + vec_ref[0, h : h + 1, lane : lane + 1]
+
+
+def apart(i, j):
+    return (abs(i - j) - 1) * TILE + 1 >= LONGEST
 
 
 def masks(seg):
@@ -248,20 +250,21 @@
         columns = []
         tops = []
         for i in range(blocks):
+            at = slice(i * TILE, (i + 1) * TILE)
             tiles = [
-                with_bias(
-                    scores[j * TILE : (j + 1) * TILE, i * TILE : (i + 1) * TILE],
-                    j - i,
-                    h,
-                    bias_s,
-                    vec_ref,
-                    first,
+                None
+                if apart(i, j)
+                else with_bias(
+                    scores[j * TILE : (j + 1) * TILE, at], j - i, h, bias_s, vec_ref, first
                 )
                 for j in range(blocks)
             ]
-            top = jnp.max(functools.reduce(jnp.maximum, tiles), 0, keepdims=True)
+            live = [tile for tile in tiles if tile is not None]
+            top = jnp.max(functools.reduce(jnp.maximum, live), 0, keepdims=True)
             tops.append(top)
-            columns.append(jnp.concatenate([jnp.exp(t - top).astype(bf16) for t in tiles], 0))
+            none = jnp.zeros((TILE, TILE), bf16)
+            exps = [none if t is None else jnp.exp(t - top).astype(bf16) for t in tiles]
+            columns.append(jnp.concatenate(exps, 0))
         mixed = dg(v_t, jnp.concatenate(columns, 1), NN)
         total = mixed[hd : hd + 1]
         lse_s[h : h + 1, :] = jnp.concatenate(tops, 1) + jnp.log(total)
@@ -283,17 +286,28 @@
         spread_bias(vec_ref, bias_s, heads, first)
 
     if keeps:
-        count = w_s.shape[0]
-        source = w_s if n else sources[0]
-        into = sorted_ref.at[pl.ds(low, count)] if n else sorted_ref.at[low]
-        keep = pltpu.make_async_copy(source, into, out_sem)
+        count = w_s.shape[0] if n else 1
+        copies = bring(place_ref, sources, w_s, sems) if n else [[]]
+        keep = [
+            pltpu.make_async_copy(
+                w_s.at[k] if n else sources[0], sorted_ref.at[low + k], out_sem.at[k]
+            )
+            for k in range(count)
+        ]
 
         @pl.when((s == 0) & (r == 0))
         def _():
-            if n:
-                for copy in bring(place_ref, sources, w_s, sems):
+            for here in copies:
+                for copy in here:
+                    copy.start()
+
+        for k in range(count):
+
+            @pl.when((s == k) & (r == 0))
+            def _():
+                for copy in copies[k]:
                     copy.wait()
-            keep.start()
+                keep[k].start()
 
         weights = w_s[s, : 3 * heads * hd] if n else sources[0][: 3 * heads * hd]
     else:
@@ -310,7 +324,8 @@
 
         @pl.when((s == pl.num_programs(1) - 1) & (r == pl.num_programs(0) - 1))
         def _():
-            keep.wait()
+            for copy in keep:
+                copy.wait()
 
 
 def attention(name, a1, vecs, segs, place, order, low, first_row, n_rows, weights, chain):
@@ -351,8 +366,8 @@
     if keeps:
         scratch += [
             pltpu.VMEM((count, width, width) if n else (1, 16, TILE), bf16),
-            pltpu.SemaphoreType.DMA((max(n, 1),)),
-            pltpu.SemaphoreType.DMA(()),
+            pltpu.SemaphoreType.DMA((count, max(n, 1))),
+            pltpu.SemaphoreType.DMA((count,)),
         ]
         linked = [] if chain is None else list(chain)
     else:
@@ -757,6 +772,10 @@
                 probs = []
                 grads = []
                 for j in range(blocks):
+                    if apart(i, j):
+                        probs.append(jnp.zeros((TILE, TILE), bf16))
+                        grads.append(jnp.zeros((TILE, TILE), bf16))
+                        continue
                     to = slice(j * TILE, (j + 1) * TILE)
                     tile = with_bias(scores[to, at], j - i, h, bias_s, vec_ref.at[pl.ds(slot, 1)])
                     prob = jnp.exp(tile - lse[:, at])
@@ -1016,18 +1035,29 @@
     gain_ref,
     own_b_ref,
     own_c_ref,
-    b_ref,
-    c_ref,
+    b_any,
+    c_any,
     _out,
     out_ref,
     *rest,
 ):
-    outs, (res_s, up_s, down_s) = rest[:-3], rest[-3:]
+    outs, (b_ref, c_ref, sems, res_s, up_s, down_s) = rest[:-6], rest[-6:]
     r = pl.program_id(0)
     others = b_ref.shape[0]
+    copies = [
+        pltpu.make_async_copy(b_any, b_ref, sems.at[0]),
+        pltpu.make_async_copy(c_any, c_ref, sems.at[1]),
+    ]
+
+    @pl.when(r == 1)
+    def _():
+        for copy in copies:
+            copy.wait()
 
     @pl.when(r == 0)
     def _():
+        for copy in copies:
+            copy.start()
         res_s[...] = own_ref[...]
         up_s[...] = jnp.zeros_like(up_s)
         down_s[...] = jnp.zeros_like(down_s)
@@ -1107,12 +1137,13 @@
                 fixed((1, width)),
                 fixed((width, units)),
                 fixed((units, width)),
-                fixed((others, width, units)),
-                fixed((others, units, width)),
-                pl.BlockSpec(memory_space=pl.ANY),
-            ],
+            ]
+            + [pl.BlockSpec(memory_space=pl.ANY)] * 3,
             out_specs=[later] + [pl.BlockSpec(shape, lambda r, p, o: zeros)] * n,
             scratch_shapes=[
+                pltpu.VMEM((others, width, units), bf16),
+                pltpu.VMEM((others, units, width), bf16),
+                pltpu.SemaphoreType.DMA((2,)),
                 pltpu.VMEM((length, width), bf16),
                 pltpu.VMEM((width, units), f32),
                 pltpu.VMEM((width, units), f32),

time: 280 us -> 280 us (level)
  transfers between devices with their start and end apart: 36 -> 36, of which waited for: 15 -> 15; matrix products, arithmetic and copies ran while one was open for 10% -> 10% of each run, Pallas kernels for 37% -> 36%
where the time goes in v4:
time: 280 us; the launch traced here: 275 us
  Pallas kernels  147 us (52%)
  starting transfers between devices  38.9 us (14%)
  waiting for transfers between devices  36.7 us (13%)
  other arithmetic  21.4 us (8%)
  between operations  14.9 us (5%)
  local copies, waits for them, and re-layouts  14.2 us (5%)
    pallas_call x2, Pallas kernels, attention(): pl.pallas_call(functools.partial(attn_kernel, heads, hd, n, low, keeps),...  43.7 us
    pallas_call x1, Pallas kernels, row_back(): pl.pallas_call(functools.partial(row_back_kernel, len(pieces), with_loss,...  31.8 us
    pallas_call x1, Pallas kernels, ffn_tail(): pl.pallas_call(functools.partial(ffn_tail_kernel, block), grid_spec=pltpu...  31.1 us
    ppermute x9, starting transfers between devices, over_tp(): return lax.ppermute(value, 'tp', levels[k])  18.7 us
    ppermute x23, waiting for transfers between devices, over_dp(): return lax.ppermute(value, 'dp', mates[m])  18.6 us
    ppermute x23, starting transfers between devices, over_dp(): return lax.ppermute(value, 'dp', mates[m])  16.2 us
    pallas_call x1, Pallas kernels, ffn_own(): pl.pallas_call(ffn_own_kernel, grid=(rows,), in_specs=[by_row, pl.BlockSp...  13.5 us
    pallas_call x1, Pallas kernels, ffn_first(): pl.pallas_call(functools.partial(ffn_first_kernel, n), grid_spec=pltpu.Pr...  11.5 us
  transfers between devices with their start and end apart: 36, of which 15 were waited for; matrix products, arithmetic and copies ran while one was open for 10% of the time, Pallas kernels for 36%

profile of v4, /device:TPU:0, one launch (start us, length us, event | category | flops | bytes accessed | tf_op | source)
XLA Modules:
  0.0 274.7 jit_solution(17255728820462265252)
XLA Ops:
  11.3 3.0 %collective-permute-start = (bf16[112,768]{1,0:T(8,128)(2,1)S(1)}, bf16[112,768]{1,0:T(8,128)(2,1)S(1)}, u32[]{:S(2)}, u32[]{:S(2)}) collective-permute-start(bf16[112,768]{1,0:T(8,128)(2,1)S(1)} %get-tuple-element.66), channel_id=1, source_target_pairs={{0,1},{1,0},{2,3},{3,2},{4,5},{5,4},{6,7},{7,6},{8,9},{9,8},{10,11... | collective-permute-start | bytes 516104 | tf_op jit(solution)/shard_map/ppermute | solution.py:1194
  14.3 2.6 collective-permute-start.1
  18.7 2.6 fusion
  21.4 4.5 %fusion.2.a1_ref = bf16[2048,768]{1,0:T(8,128)(2,1)} fusion(bf16[2048,768]{1,0:T(8,128)(2,1)} %refs_16_.1, f32[768]{0:T(1024)S(1)} %copy-done.23, f32[2048]{0:T(1024)S(1)} %add_rsqrt_fusion), kind=kLoop, calls=%fused_computation.4 | loop fusion | flops 6291456 | bytes 6302720 | tf_op jit(solution)/shard_map/convert_element_type | solution.py:1235
  26.0 3.9 %collective-permute-done.1.refs_1_ = bf16[112,768]{1,0:T(8,128)(2,1)S(1)} collective-permute-done((bf16[112,768]{1,0:T(8,128)(2,1)S(1)}, bf16[112,768]{1,0:T(8,128)(2,1)S(1)}, u32[]{:S(2)}, u32[]{:S(2)}) %collective-permute-start.1) | collective-permute-done | bytes 172064 | tf_op jit(solution)/shard_map/ppermute | solution.py:1194
  31.2 1.9 stack.1
  33.1 1.5 collective-permute-start.3
  34.6 1.5 collective-permute-start.4
  36.6 11.3 %attn_own.1 = (bf16[4,576,512]{2,1,0:T(8,128)(2,1)}, f32[4,3,512]{2,1,0:T(4,128)S(1)}, bf16[4,4,192,512]{3,2,1,0:T(8,128)(2,1)}, bf16[4,768,768]{2,1,0:T(8,128)(2,1)}) custom-call(s32[8]{0:T(128)S(1)} %xor_multiply_fusion.place_ref, s32[4]{0:T(128)S(1)} %iota_xor_fusion.order_ref, bf16[2048,768]{1,0:T(8,128)(2,1)} %fusion.2.a1_ref, ...), custom_call_target="tpu_custom_call" | custom-call | flops 10000000000 | bytes 1048576 | tf_op jit(solution)/shard_map/attn_own/pallas_call | solution.py:376
  48.1 4.9 %collective-permute-done.4.rest_4_ = bf16[3,96,768]{2,1,0:T(8,128)(2,1)} collective-permute-done((bf16[3,96,768]{2,1,0:T(8,128)(2,1)}, bf16[3,96,768]{2,1,0:T(8,128)(2,1)}, u32[]{:S(2)}, u32[]{:S(2)}) %collective-permute-start.4) | collective-permute-done | bytes 442400 | tf_op jit(solution)/shard_map/ppermute | solution.py:1191
  52.9 3.0 %others_of.1 = (bf16[3,96,768]{2,1,0:T(8,128)(2,1)}, bf16[3,96,768]{2,1,0:T(8,128)(2,1)}) custom-call(s32[4]{0:T(128)} %copy-done.3, bf16[4,192,768]{2,1,0:T(8,128)(2,1)} %bitcast.72), custom_call_target="tpu_custom_call" | custom-call | bytes 2359296 | tf_op jit(solution)/shard_map/others_of/pallas_call | solution.py:225
  62.5 1.4 collective-permute-start.12
  63.9 32.4 %attn_far.1 = (bf16[4,576,512]{2,1,0:T(8,128)(2,1)}, f32[4,3,512]{2,1,0:T(4,128)S(1)}, bf16[4,4,192,512]{3,2,1,0:T(8,128)(2,1)}, bf16[4,768,768]{2,1,0:T(8,128)(2,1)}) custom-call(s32[8]{0:T(128)S(1)} %xor_multiply_fusion.place_ref, s32[4]{0:T(128)S(1)} %copy-done.4, ...), custom_call_target="tpu_custom_call", output_to_operand_aliasing={{0}: (13, {}), {1}: (14, {}), {2}: (15, {}), {3}: (16, {})} | custom-call | flops 30000001024 | bytes 1048576 | tf_op jit(solution)/shard_map/attn_far/pallas_call | solution.py:376
  97.5 13.5 %ffn_own.1 = (bf16[2048,768]{1,0:T(8,128)(2,1)}, bf16[2048,768]{1,0:T(8,128)(2,1)}, bf16[2048,768]{1,0:T(8,128)(2,1)}) custom-call(bf16[2048,768]{1,0:T(8,128)(2,1)} %refs_16_.1, bf16[4,4,192,512]{3,2,1,0:T(8,128)(2,1)} %get-tuple-element.81.ctx_ref.refs_23_, bf16[4,768,768]{2,1,0:T(8,128)(2,1)} %get-tuple-element.82.wo_ref.refs_21_, ...), custom_call_target="tpu_custom_call" | custom-call | flops 7247757312 | bytes 16777216 | tf_op jit(solution)/shard_map/ffn_own/pallas_call | solution.py:438
  111.9 11.5 %ffn_first.1 = (bf16[2048,768]{1,0:T(8,128)(2,1)}, bf16[512,768]{1,0:T(8,128)(2,1)}, f32[8,768]{1,0:T(8,128)S(1)}, bf16[3,768,768]{2,1,0:T(8,128)(2,1)}, bf16[3,768,768]{2,1,0:T(8,128)(2,1)}) custom-call(s32[8]{0:T(128)S(1)} %xor_multiply_fusion.place_ref, s32[4]{0:T(128)S(1)} %copy-done.4, bf16[2048,768]{1,0:T(8,128)(2,1)} %get-tuple-element.83.a2_ref.refs_15_, ...), custom_call_target="tpu_custom_call" | custom-call | flops 3623878656 | bytes 16777216 | tf_op jit(solution)/shard_map/ffn_first/pallas_call | solution.py:530
  123.4 4.4 %collective-permute-start.17 = (bf16[8,768]{1,0:T(8,128)(2,1)S(1)}, bf16[8,768]{1,0:T(8,128)(2,1)S(1)}, u32[]{:S(2)}, u32[]{:S(2)}) collective-permute-start(bf16[8,768]{1,0:T(8,128)(2,1)S(1)} %get-tuple-element.174), channel_id=1, source_target_pairs={{0,1},{1,0},{2,3},{3,2},{4,5},{5,4},{6,7},{7,6},{8,9},{9,8},{10,11... | collective-permute-start | bytes 36872 | tf_op jit(solution)/shard_map/ppermute | solution.py:1194
  127.8 2.9 %collective-permute-start.18 = (bf16[8,768]{1,0:T(8,128)(2,1)S(1)}, bf16[8,768]{1,0:T(8,128)(2,1)S(1)}, u32[]{:S(2)}, u32[]{:S(2)}) collective-permute-start(bf16[8,768]{1,0:T(8,128)(2,1)S(1)} %get-tuple-element.174), channel_id=1, source_target_pairs={{0,2},{1,3},{2,0},{3,1},{4,6},{5,7},{6,4},{7,5},{8,10},{9,11},{10,... | collective-permute-start | bytes 36872 | tf_op jit(solution)/shard_map/ppermute | solution.py:1194
  132.4 3.8 %collective-permute-done.19 = bf16[8,768]{1,0:T(8,128)(2,1)S(1)} collective-permute-done((bf16[8,768]{1,0:T(8,128)(2,1)S(1)}, bf16[8,768]{1,0:T(8,128)(2,1)S(1)}, u32[]{:S(2)}, u32[]{:S(2)}) %collective-permute-start.19) | collective-permute-done | bytes 12320 | tf_op jit(solution)/shard_map/ppermute | solution.py:1194
  138.7 1.5 collective-permute-start.22
  142.3 2.1 collective-permute-done.22.refs_2_
  145.7 31.8 %row_back.1 = (f32[32,768]{1,0:T(8,128)S(1)}, f32[96,768]{1,0:T(8,128)}, f32[1,768]{1,0:T(1,128)S(1)}, f32[1,768]{1,0:T(1,128)S(1)}, bf16[512,768]{1,0:T(8,128)(...) custom-call(s32[33]{0:T(128)S(1)} %pad_add_fusion.1.at_ref, ...), custom_call_target="tpu_custom_call" | custom-call | flops 30000001024 | bytes 16777216 | tf_op jit(solution)/shard_map/row_back/pallas_call | solution.py:855
  180.4 9.0 %attn_weights.1 = (bf16[4,4,112,768]{3,2,1,0:T(8,128)(2,1)}, bf16[4,4,112,768]{3,2,1,0:T(8,128)(2,1)}) custom-call(s32[6]{0:T(128)S(1)} %pad_add_fusion.place_ref, bf16[2048,768]{1,0:T(8,128)(2,1)} %fusion.2.a1_ref, bf16[512,768]{1,0:T(8,128)(2,1)S(1)} %get-tuple-element.98.dattn_ref, bf16[4,576,512]{2,1,0:T(8,128)(2,1)} %get-tuple-element.99.dqkv_ref, ...), custom_call_target="tpu_custom_call" | custom-call | flops 1000000 | bytes 1000000 | tf_op jit(solution)/shard_map/attn_weights/pallas_call | solution.py:999
  189.4 5.3 %collective-permute-done.24 = bf16[4,4,112,768]{3,2,1,0:T(8,128)(2,1)S(1)} collective-permute-done((bf16[4,4,112,768]{3,2,1,0:T(8,128)(2,1)}, bf16[4,4,112,768]{3,2,1,0:T(8,128)(2,1)S(1)}, u32[]{:S(2)}, u32[]{:S(2)}) %collective-permute-start.24) | collective-permute-done | bytes 2752544 | tf_op jit(solution)/shard_map/ppermute | solution.py:1191
  194.7 2.7 fusion.17
  199.4 1.6 collective-permute-start.27
  200.9 31.1 %ffn_tail.1 = (bf16[2048,768]{1,0:T(8,128)(2,1)}, bf16[4,2,96,768]{3,2,1,0:T(8,128)(2,1)}, bf16[4,2,96,768]{3,2,1,0:T(8,128)(2,1)}) custom-call(s32[6]{0:T(128)S(1)} %pad_add_fusion.place_ref, s32[4]{0:T(128)S(1)} %copy-done.4, bf16[2048,768]{1,0:T(8,128)(2,1)} %get-tuple-element.83.a2_ref.refs_15_, ...), custom_call_target="tpu_custom_call", output_to_operand_aliasing={{0}: (13, {})} | custom-call | flops 1000000 | bytes 1000000 | tf_op jit(solution)/shard_map/ffn_tail/pallas_call | solution.py:1125
  233.9 5.6 %all-gather.6.cloned.1.call-done = bf16[2048,768]{1,0:T(8,128)(2,1)} async-done(((bf16[512,768]{1,0:T(8,128)(2,1)}), bf16[2048,768]{1,0:T(8,128)(2,1)}) %all-gather.6.cloned.1.call-update) | async-done | bytes 3145744 | tf_op jit(solution)/shard_map/all_gather | solution.py:1304
  239.5 2.9 %fusion.18 = (bf16[4,112,768]{2,1,0:T(8,128)(2,1)S(1)}, f32[4,112,768]{2,1,0:T(8,128)}) fusion(bf16[4,112,768]{2,1,0:T(8,128)(2,1)} %copy-done.11, bf16[4,112,768]{2,1,0:T(8,128)(2,1)} %copy-done.10, f32[4,112,768]{2,1,0:T(8,128)S(1)} %get-tuple-element.113, bf16[4,112,768]{2,1,0:T(8,128)(2,1)S(1)} %collective-permute-done.25), kind=kLoop, calls=%fused_computation.66 | loop fusion | flops 2752512 | bytes 5505024 | tf_op jit(solution)/shard_map/convert.2
  244.3 3.1 %collective-permute-start.31 = (bf16[112,768]{1,0:T(8,128)(2,1)S(1)}, bf16[112,768]{1,0:T(8,128)(2,1)S(1)}, u32[]{:S(2)}, u32[]{:S(2)}) collective-permute-start(bf16[112,768]{1,0:T(8,128)(2,1)S(1)} %get-tuple-element.180), channel_id=1, source_target_pairs={{0,3},{1,2},{2,1},{3,0},{4,7},{5,6},{6,5},{7,4},{8,11},{9,10},{10,... | collective-permute-start | bytes 516104 | tf_op jit(solution)/shard_map/ppermute | solution.py:1194
  248.8 3.7 %all-to-all-start = ((bf16[4,2,96,768]{3,2,1,0:T(8,128)(2,1)}), bf16[4,2,96,768]{3,2,1,0:T(8,128)(2,1)S(1)}, u32[]{:S(2)}, u32[]{:S(2)}) async-start(bf16[4,2,96,768]{3,2,1,0:T(8,128)(2,1)} %fusion.14), calls=%async_computation | async-start | bytes 2359296 | tf_op jit(solution)/shard_map/all_to_all | solution.py:1360
  253.0 5.1 %convert_element_type.158 = f32[2048,768]{1,0:T(8,128)} convert(bf16[2048,768]{1,0:T(8,128)(2,1)} %all-gather.6.cloned.1.call-done) | non-fusion elementwise | flops 1572864 | bytes 9437184 | tf_op jit(solution)/shard_map/convert_element_type | solution.py:1384
  262.5 4.3 %all-to-all-done = bf16[4,2,96,768]{3,2,1,0:T(8,128)(2,1)S(1)} async-done(((bf16[4,2,96,768]{3,2,1,0:T(8,128)(2,1)}), bf16[4,2,96,768]{3,2,1,0:T(8,128)(2,1)S(1)}, u32[]{:S(2)}, u32[]{:S(2)}) %all-to-all-start) | async-done | bytes 1179680 | tf_op jit(solution)/shard_map/all_to_all | solution.py:1360
  (177 shorter events, 39.5 us)
Async XLA Ops:
  7.2 45.7 %all-gather.8.cloned.1.call-start = ((), (), s32[]{:S(2)}) async-start(), calls=%async_computation.2 | async-start | bytes 1474560 | tf_op jit(solution)/shard_map/all_gather | solution.py:1224
  11.3 14.7 %collective-permute-start = (bf16[112,768]{1,0:T(8,128)(2,1)S(1)}, bf16[112,768]{1,0:T(8,128)(2,1)S(1)}, u32[]{:S(2)}, u32[]{:S(2)}) collective-permute-start(bf16[112,768]{1,0:T(8,128)(2,1)S(1)} %get-tuple-element.66), channel_id=1, source_target_pairs={{0,1},{1,0},{2,3},{3,2},{4,5},{5,4},{6,7},{7,6},{8,9},{9,8},{10,11... | collective-permute-start | bytes 516104 | tf_op jit(solution)/shard_map/ppermute | solution.py:1194
  14.3 15.6 %collective-permute-start.1 = (bf16[112,768]{1,0:T(8,128)(2,1)S(1)}, bf16[112,768]{1,0:T(8,128)(2,1)S(1)}, u32[]{:S(2)}, u32[]{:S(2)}) collective-permute-start(bf16[112,768]{1,0:T(8,128)(2,1)S(1)} %get-tuple-element.66), channel_id=1, source_target_pairs={{0,2},{1,3},{2,0},{3,1},{4,6},{5,7},{6,4},{7,5},{8,10},{9,11},{10,... | collective-permute-start | bytes 516104 | tf_op jit(solution)/shard_map/ppermute | solution.py:1194
  16.9 13.0 %collective-permute-start.2 = (bf16[112,768]{1,0:T(8,128)(2,1)S(1)}, bf16[112,768]{1,0:T(8,128)(2,1)S(1)}, u32[]{:S(2)}, u32[]{:S(2)}) collective-permute-start(bf16[112,768]{1,0:T(8,128)(2,1)S(1)} %get-tuple-element.66), channel_id=1, source_target_pairs={{0,3},{1,2},{2,1},{3,0},{4,7},{5,6},{6,5},{7,4},{8,11},{9,10},{10,... | collective-permute-start | bytes 516104 | tf_op jit(solution)/shard_map/ppermute | solution.py:1194
  18.6 93.3 %all-gather.10.cloned.1.call-start = ((), (), s32[]{:S(2)}) async-start(), calls=%async_computation.3 | async-start | bytes 3981312 | tf_op jit(solution)/shard_map/all_gather | solution.py:1242
  33.1 14.9 %collective-permute-start.3 = (bf16[3,96,768]{2,1,0:T(8,128)(2,1)}, bf16[3,96,768]{2,1,0:T(8,128)(2,1)S(1)}, u32[]{:S(2)}, u32[]{:S(2)}) collective-permute-start(bf16[3,96,768]{2,1,0:T(8,128)(2,1)} %get-tuple-element.77.rest_0_), channel_id=1, source_target_pairs={{0,8},{4,12},{8,0},{12,4},{16,24},{20,28},{24,16},{28,20},{1,9},{5... | collective-permute-start | bytes 1327112 | tf_op jit(solution)/shard_map/ppermute | solution.py:1191
  34.6 18.3 %collective-permute-start.4 = (bf16[3,96,768]{2,1,0:T(8,128)(2,1)}, bf16[3,96,768]{2,1,0:T(8,128)(2,1)}, u32[]{:S(2)}, u32[]{:S(2)}) collective-permute-start(bf16[3,96,768]{2,1,0:T(8,128)(2,1)} %get-tuple-element.77.rest_0_), channel_id=1, source_target_pairs={{0,16},{4,20},{8,24},{12,28},{16,0},{20,4},{24,8},{28,12},{1,17},{... | collective-permute-start | bytes 1327112 | tf_op jit(solution)/shard_map/ppermute | solution.py:1191
  36.1 16.8 %collective-permute-start.5 = (bf16[3,96,768]{2,1,0:T(8,128)(2,1)}, bf16[3,96,768]{2,1,0:T(8,128)(2,1)}, u32[]{:S(2)}, u32[]{:S(2)}) collective-permute-start(bf16[3,96,768]{2,1,0:T(8,128)(2,1)} %get-tuple-element.77.rest_0_), channel_id=1, source_target_pairs={{0,24},{4,28},{8,16},{12,20},{16,8},{20,12},{24,0},{28,4},{1,25},{... | collective-permute-start | bytes 1327112 | tf_op jit(solution)/shard_map/ppermute | solution.py:1191
  55.9 183.6 %all-gather.6.cloned.1.call-start = ((), (), s32[]{:S(2)}) async-start(), calls=%async_computation.1 | async-start | bytes 3932160 | tf_op jit(solution)/shard_map/all_gather | solution.py:1304
  57.1 3.3 %collective-permute-start.9 = (bf16[3,96,768]{2,1,0:T(8,128)(2,1)}, bf16[3,96,768]{2,1,0:T(8,128)(2,1)S(1)}, u32[]{:S(2)}, u32[]{:S(2)}) collective-permute-start(bf16[3,96,768]{2,1,0:T(8,128)(2,1)} %collective-permute-done.5.rest_6_), channel_id=1, source_target_pairs={{0,4},{4,0},{8,12},{12,8},{16,20},{20,16},{24,28},{28,24},{1,5},{5... | collective-permute-start | bytes 1327112 | tf_op jit(solution)/shard_map/ppermute | solution.py:1191
  60.4 35.9 %collective-permute-start.10 = (bf16[3,96,768]{2,1,0:T(8,128)(2,1)}, bf16[3,96,768]{2,1,0:T(8,128)(2,1)S(1)}, u32[]{:S(2)}, u32[]{:S(2)}) collective-permute-start(bf16[3,96,768]{2,1,0:T(8,128)(2,1)} %get-tuple-element.88.rest_0_), channel_id=1, source_target_pairs={{0,8},{4,12},{8,0},{12,4},{16,24},{20,28},{24,16},{28,20},{1,9},{5... | collective-permute-start | bytes 1327112 | tf_op jit(solution)/shard_map/ppermute | solution.py:1191
  61.7 34.7 %collective-permute-start.11 = (bf16[3,96,768]{2,1,0:T(8,128)(2,1)}, bf16[3,96,768]{2,1,0:T(8,128)(2,1)S(1)}, u32[]{:S(2)}, u32[]{:S(2)}) collective-permute-start(bf16[3,96,768]{2,1,0:T(8,128)(2,1)} %get-tuple-element.88.rest_0_), channel_id=1, source_target_pairs={{0,16},{4,20},{8,24},{12,28},{16,0},{20,4},{24,8},{28,12},{1,17},{... | collective-permute-start | bytes 1327112 | tf_op jit(solution)/shard_map/ppermute | solution.py:1191
  62.5 33.9 %collective-permute-start.12 = (bf16[3,96,768]{2,1,0:T(8,128)(2,1)}, bf16[3,96,768]{2,1,0:T(8,128)(2,1)S(1)}, u32[]{:S(2)}, u32[]{:S(2)}) collective-permute-start(bf16[3,96,768]{2,1,0:T(8,128)(2,1)} %get-tuple-element.88.rest_0_), channel_id=1, source_target_pairs={{0,24},{4,28},{8,16},{12,20},{16,8},{20,12},{24,0},{28,4},{1,25},{... | collective-permute-start | bytes 1327112 | tf_op jit(solution)/shard_map/ppermute | solution.py:1191
  96.4 14.6 %collective-permute-start.13 = (bf16[3,96,768]{2,1,0:T(8,128)(2,1)S(1)}, bf16[3,96,768]{2,1,0:T(8,128)(2,1)S(1)}, u32[]{:S(2)}, u32[]{:S(2)}) collective-permute-start(bf16[3,96,768]{2,1,0:T(8,128)(2,1)S(1)} %copy-done.2), channel_id=1, source_target_pairs={{0,4},{4,0},{8,12},{12,8},{16,20},{20,16},{24,28},{28,24},{1,5},{5... | collective-permute-start | bytes 1327112 | tf_op jit(solution)/shard_map/ppermute | solution.py:1191
  96.5 14.6 %collective-permute-start.14 = (bf16[3,96,768]{2,1,0:T(8,128)(2,1)S(1)}, bf16[3,96,768]{2,1,0:T(8,128)(2,1)S(1)}, u32[]{:S(2)}, u32[]{:S(2)}) collective-permute-start(bf16[3,96,768]{2,1,0:T(8,128)(2,1)S(1)} %collective-permute-done.10.rest_2_), channel_id=1, source_target_pairs={{0,4},{4,0},{8,12},{12,8},{16,20},{20,16},{24,28},{28,24},{1,5},{5... | collective-permute-start | bytes 1327112 | tf_op jit(solution)/shard_map/ppermute | solution.py:1191
  97.0 14.1 %collective-permute-start.15 = (bf16[3,96,768]{2,1,0:T(8,128)(2,1)S(1)}, bf16[3,96,768]{2,1,0:T(8,128)(2,1)S(1)}, u32[]{:S(2)}, u32[]{:S(2)}) collective-permute-start(bf16[3,96,768]{2,1,0:T(8,128)(2,1)S(1)} %collective-permute-done.11.rest_4_), channel_id=1, source_target_pairs={{0,4},{4,0},{8,12},{12,8},{16,20},{20,16},{24,28},{28,24},{1,5},{5... | collective-permute-start | bytes 1327112 | tf_op jit(solution)/shard_map/ppermute | solution.py:1191
  97.1 14.8 %collective-permute-start.16 = (bf16[3,96,768]{2,1,0:T(8,128)(2,1)S(1)}, bf16[3,96,768]{2,1,0:T(8,128)(2,1)}, u32[]{:S(2)}, u32[]{:S(2)}) collective-permute-start(bf16[3,96,768]{2,1,0:T(8,128)(2,1)S(1)} %collective-permute-done.12.rest_6_), channel_id=1, source_target_pairs={{0,4},{4,0},{8,12},{12,8},{16,20},{20,16},{24,28},{28,24},{1,5},{5... | collective-permute-start | bytes 1327112 | tf_op jit(solution)/shard_map/ppermute | solution.py:1191
  123.4 9.0 %collective-permute-start.17 = (bf16[8,768]{1,0:T(8,128)(2,1)S(1)}, bf16[8,768]{1,0:T(8,128)(2,1)S(1)}, u32[]{:S(2)}, u32[]{:S(2)}) collective-permute-start(bf16[8,768]{1,0:T(8,128)(2,1)S(1)} %get-tuple-element.174), channel_id=1, source_target_pairs={{0,1},{1,0},{2,3},{3,2},{4,5},{5,4},{6,7},{7,6},{8,9},{9,8},{10,11... | collective-permute-start | bytes 36872 | tf_op jit(solution)/shard_map/ppermute | solution.py:1194
  127.8 4.6 %collective-permute-start.18 = (bf16[8,768]{1,0:T(8,128)(2,1)S(1)}, bf16[8,768]{1,0:T(8,128)(2,1)S(1)}, u32[]{:S(2)}, u32[]{:S(2)}) collective-permute-start(bf16[8,768]{1,0:T(8,128)(2,1)S(1)} %get-tuple-element.174), channel_id=1, source_target_pairs={{0,2},{1,3},{2,0},{3,1},{4,6},{5,7},{6,4},{7,5},{8,10},{9,11},{10,... | collective-permute-start | bytes 36872 | tf_op jit(solution)/shard_map/ppermute | solution.py:1194
  130.7 5.5 %collective-permute-start.19 = (bf16[8,768]{1,0:T(8,128)(2,1)S(1)}, bf16[8,768]{1,0:T(8,128)(2,1)S(1)}, u32[]{:S(2)}, u32[]{:S(2)}) collective-permute-start(bf16[8,768]{1,0:T(8,128)(2,1)S(1)} %get-tuple-element.174), channel_id=1, source_target_pairs={{0,3},{1,2},{2,1},{3,0},{4,7},{5,6},{6,5},{7,4},{8,11},{9,10},{10,... | collective-permute-start | bytes 36872 | tf_op jit(solution)/shard_map/ppermute | solution.py:1194
  137.5 4.9 %collective-permute-start.21 = (bf16[64,768]{1,0:T(8,128)(2,1)S(1)}, bf16[64,768]{1,0:T(8,128)(2,1)S(1)}, u32[]{:S(2)}, u32[]{:S(2)}) collective-permute-start(bf16[64,768]{1,0:T(8,128)(2,1)S(1)} %constant_dynamic-update-slice_fusion.refs_0_), channel_id=1, source_target_pairs={{0,8},{4,12},{8,0},{12,4},{16,24},{20,28},{24,16},{28,20},{1,9},{5... | collective-permute-start | bytes 294920 | tf_op jit(solution)/shard_map/ppermute | solution.py:1191
  138.7 5.8 %collective-permute-start.22 = (bf16[64,768]{1,0:T(8,128)(2,1)S(1)}, bf16[64,768]{1,0:T(8,128)(2,1)S(1)}, u32[]{:S(2)}, u32[]{:S(2)}) collective-permute-start(bf16[64,768]{1,0:T(8,128)(2,1)S(1)} %constant_dynamic-update-slice_fusion.refs_0_), channel_id=1, source_target_pairs={{0,16},{4,20},{8,24},{12,28},{16,0},{20,4},{24,8},{28,12},{1,17},{... | collective-permute-start | bytes 294920 | tf_op jit(solution)/shard_map/ppermute | solution.py:1191
  140.2 5.5 %collective-permute-start.23 = (bf16[64,768]{1,0:T(8,128)(2,1)S(1)}, bf16[64,768]{1,0:T(8,128)(2,1)S(1)}, u32[]{:S(2)}, u32[]{:S(2)}) collective-permute-start(bf16[64,768]{1,0:T(8,128)(2,1)S(1)} %constant_dynamic-update-slice_fusion.refs_0_), channel_id=1, source_target_pairs={{0,24},{4,28},{8,16},{12,20},{16,8},{20,12},{24,0},{28,4},{1,25},{... | collective-permute-start | bytes 294920 | tf_op jit(solution)/shard_map/ppermute | solution.py:1191
  189.4 5.3 %collective-permute-start.24 = (bf16[4,4,112,768]{3,2,1,0:T(8,128)(2,1)}, bf16[4,4,112,768]{3,2,1,0:T(8,128)(2,1)S(1)}, u32[]{:S(2)}, u32[]{:S(2)}) collective-permute-start(bf16[4,4,112,768]{3,2,1,0:T(8,128)(2,1)} %get-tuple-element.104), channel_id=1, source_target_pairs={{0,4},{4,0},{8,12},{12,8},{16,20},{20,16},{24,28},{28,24},{1,5},{5... | collective-permute-start | bytes 8257544 | tf_op jit(solution)/shard_map/ppermute | solution.py:1191
  197.4 34.7 %collective-permute-start.25 = (bf16[4,112,768]{2,1,0:T(8,128)(2,1)S(1)}, bf16[4,112,768]{2,1,0:T(8,128)(2,1)S(1)}, u32[]{:S(2)}, u32[]{:S(2)}) collective-permute-start(bf16[4,112,768]{2,1,0:T(8,128)(2,1)S(1)} %get-tuple-element.176), channel_id=1, source_target_pairs={{0,8},{4,12},{8,0},{12,4},{16,24},{20,28},{24,16},{28,20},{1,9},{5... | collective-permute-start | bytes 2064392 | tf_op jit(solution)/shard_map/ppermute | solution.py:1191
  198.3 33.8 %collective-permute-start.26 = (bf16[4,112,768]{2,1,0:T(8,128)(2,1)S(1)}, bf16[4,112,768]{2,1,0:T(8,128)(2,1)S(1)}, u32[]{:S(2)}, u32[]{:S(2)}) collective-permute-start(bf16[4,112,768]{2,1,0:T(8,128)(2,1)S(1)} %get-tuple-element.177), channel_id=1, source_target_pairs={{0,16},{4,20},{8,24},{12,28},{16,0},{20,4},{24,8},{28,12},{1,17},{... | collective-permute-start | bytes 2064392 | tf_op jit(solution)/shard_map/ppermute | solution.py:1191
  199.4 32.8 %collective-permute-start.27 = (bf16[4,112,768]{2,1,0:T(8,128)(2,1)S(1)}, bf16[4,112,768]{2,1,0:T(8,128)(2,1)S(1)}, u32[]{:S(2)}, u32[]{:S(2)}) collective-permute-start(bf16[4,112,768]{2,1,0:T(8,128)(2,1)S(1)} %get-tuple-element.175), channel_id=1, source_target_pairs={{0,24},{4,28},{8,16},{12,20},{16,8},{20,12},{24,0},{28,4},{1,25},{... | collective-permute-start | bytes 2064392 | tf_op jit(solution)/shard_map/ppermute | solution.py:1191
  233.9 13.6 %collective-permute-start.28 = (bf16[4,2,96,768]{3,2,1,0:T(8,128)(2,1)}, bf16[4,2,96,768]{3,2,1,0:T(8,128)(2,1)S(1)}, u32[]{:S(2)}, u32[]{:S(2)}) collective-permute-start(bf16[4,2,96,768]{3,2,1,0:T(8,128)(2,1)} %get-tuple-element.112), channel_id=1, source_target_pairs={{0,4},{4,0},{8,12},{12,8},{16,20},{20,16},{24,28},{28,24},{1,5},{5... | collective-permute-start | bytes 3538952 | tf_op jit(solution)/shard_map/ppermute | solution.py:1191
  243.1 15.1 %collective-permute-start.29 = (bf16[112,768]{1,0:T(8,128)(2,1)}, bf16[112,768]{1,0:T(8,128)(2,1)S(1)}, u32[]{:S(2)}, u32[]{:S(2)}) collective-permute-start(bf16[112,768]{1,0:T(8,128)(2,1)} %get-tuple-element.179), channel_id=1, source_target_pairs={{0,1},{1,0},{2,3},{3,2},{4,5},{5,4},{6,7},{7,6},{8,9},{9,8},{10,11... | collective-permute-start | bytes 516104 | tf_op jit(solution)/shard_map/ppermute | solution.py:1194
  243.1 15.5 %collective-permute-start.30 = (bf16[112,768]{1,0:T(8,128)(2,1)S(1)}, bf16[112,768]{1,0:T(8,128)(2,1)S(1)}, u32[]{:S(2)}, u32[]{:S(2)}) collective-permute-start(bf16[112,768]{1,0:T(8,128)(2,1)S(1)} %get-tuple-element.181), channel_id=1, source_target_pairs={{0,2},{1,3},{2,0},{3,1},{4,6},{5,7},{6,4},{7,5},{8,10},{9,11},{10,... | collective-permute-start | bytes 516104 | tf_op jit(solution)/shard_map/ppermute | solution.py:1194
  244.3 14.3 %collective-permute-start.31 = (bf16[112,768]{1,0:T(8,128)(2,1)S(1)}, bf16[112,768]{1,0:T(8,128)(2,1)S(1)}, u32[]{:S(2)}, u32[]{:S(2)}) collective-permute-start(bf16[112,768]{1,0:T(8,128)(2,1)S(1)} %get-tuple-element.180), channel_id=1, source_target_pairs={{0,3},{1,2},{2,1},{3,0},{4,7},{5,6},{6,5},{7,4},{8,11},{9,10},{10,... | collective-permute-start | bytes 516104 | tf_op jit(solution)/shard_map/ppermute | solution.py:1194
  248.8 17.9 %all-to-all-start = ((bf16[4,2,96,768]{3,2,1,0:T(8,128)(2,1)}), bf16[4,2,96,768]{3,2,1,0:T(8,128)(2,1)S(1)}, u32[]{:S(2)}, u32[]{:S(2)}) async-start(bf16[4,2,96,768]{3,2,1,0:T(8,128)(2,1)} %fusion.14), calls=%async_computation | async-start | bytes 2359296 | tf_op jit(solution)/shard_map/all_to_all | solution.py:1360
  (34 other events, 230.1 us)
Sparse Core Ops, SparseCore 0:
  18.7 32.7 all-gather.7
  56.0 50.0 all-gather.9
  178.0 61.4 all-gather.5

commit v5 on v4

--- a/solution.py
+++ b/solution.py
@@ -206,6 +206,7 @@
     return pl.pallas_call(
         stack_kernel,
         out_shape=[jax.ShapeDtypeStruct(shape, bf16) for shape in shapes],
+        compiler_params=pltpu.CompilerParams(vmem_limit_bytes=VMEM),
         cost_estimate=cost(0, 12 * arrays[0].size),
         name="stack",
     )(*arrays)
@@ -231,6 +232,7 @@
             out_specs=[pl.BlockSpec(shape, lambda i, p: (0, 0, 0))] * count,
         ),
         out_shape=[jax.ShapeDtypeStruct(shape, bf16)] * count,
+        compiler_params=pltpu.CompilerParams(vmem_limit_bytes=VMEM),
         cost_estimate=cost(0, 4 * everything.size),
         name="others_of",
     )(order, everything)

time: 280 us -> 276 us (0.986)
    unnamed x69 -> x55, local copies, waits for them, and re-layouts: 8.72 us -> 7.3 us
  transfers between devices with their start and end apart: 36 -> 36, of which waited for: 15 -> 15; matrix products, arithmetic and copies ran while one was open for 10% -> 11% of each run, Pallas kernels for 36% -> 36%
where the time goes in v5:
time: 276 us; the launch traced here: 272 us
  Pallas kernels  145 us (53%)
  waiting for transfers between devices  38.1 us (14%)
  starting transfers between devices  37.7 us (14%)
  other arithmetic  21.5 us (8%)
  between operations  14.8 us (5%)
  local copies, waits for them, and re-layouts  12.8 us (5%)
    pallas_call x2, Pallas kernels, attention(): pl.pallas_call(functools.partial(attn_kernel, heads, hd, n, low, keeps),...  43.8 us
    pallas_call x1, Pallas kernels, row_back(): pl.pallas_call(functools.partial(row_back_kernel, len(pieces), with_loss,...  31.8 us
    pallas_call x1, Pallas kernels, ffn_tail(): pl.pallas_call(functools.partial(ffn_tail_kernel, block), grid_spec=pltpu...  31.1 us
    ppermute x23, waiting for transfers between devices, over_dp(): return lax.ppermute(value, 'dp', mates[m])  18.9 us
    ppermute x9, starting transfers between devices, over_tp(): return lax.ppermute(value, 'tp', levels[k])  17.5 us
    ppermute x23, starting transfers between devices, over_dp(): return lax.ppermute(value, 'dp', mates[m])  16.3 us
    pallas_call x1, Pallas kernels, ffn_own(): pl.pallas_call(ffn_own_kernel, grid=(rows,), in_specs=[by_row, pl.BlockSp...  13.5 us
    pallas_call x1, Pallas kernels, ffn_first(): pl.pallas_call(functools.partial(ffn_first_kernel, n), grid_spec=pltpu.Pr...  11.5 us
  transfers between devices with their start and end apart: 36, of which 15 were waited for; matrix products, arithmetic and copies ran while one was open for 11% of the time, Pallas kernels for 36%

profile of v5, /device:TPU:0, one launch (start us, length us, event | category | flops | bytes accessed | tf_op | source)
XLA Modules:
  0.0 271.5 jit_solution(12291379575259002757)
XLA Ops:
  11.3 3.0 %collective-permute-start = (bf16[112,768]{1,0:T(8,128)(2,1)S(1)}, bf16[112,768]{1,0:T(8,128)(2,1)S(1)}, u32[]{:S(2)}, u32[]{:S(2)}) collective-permute-start(bf16[112,768]{1,0:T(8,128)(2,1)S(1)} %get-tuple-element.66), channel_id=1, source_target_pairs={{0,1},{1,0},{2,3},{3,2},{4,5},{5,4},{6,7},{7,6},{8,9},{9,8},{10,11... | collective-permute-start | bytes 516104 | tf_op jit(solution)/shard_map/ppermute | solution.py:1196
  14.3 2.6 collective-permute-start.1
  18.7 2.6 fusion
  21.4 4.5 %fusion.2.a1_ref = bf16[2048,768]{1,0:T(8,128)(2,1)} fusion(bf16[2048,768]{1,0:T(8,128)(2,1)} %refs_16_.1, f32[768]{0:T(1024)S(1)} %copy-done.15, f32[2048]{0:T(1024)S(1)} %add_rsqrt_fusion), kind=kLoop, calls=%fused_computation.4 | loop fusion | flops 6291456 | bytes 6302720 | tf_op jit(solution)/shard_map/convert_element_type | solution.py:1237
  26.1 3.8 %collective-permute-done.1.refs_1_ = bf16[112,768]{1,0:T(8,128)(2,1)S(1)} collective-permute-done((bf16[112,768]{1,0:T(8,128)(2,1)S(1)}, bf16[112,768]{1,0:T(8,128)(2,1)S(1)}, u32[]{:S(2)}, u32[]{:S(2)}) %collective-permute-start.1) | collective-permute-done | bytes 172064 | tf_op jit(solution)/shard_map/ppermute | solution.py:1196
  29.9 1.6 collective-permute-start.3
  31.5 1.5 collective-permute-start.4
  33.5 11.3 %attn_own.1 = (bf16[4,576,512]{2,1,0:T(8,128)(2,1)}, f32[4,3,512]{2,1,0:T(4,128)S(1)}, bf16[4,4,192,512]{3,2,1,0:T(8,128)(2,1)}, bf16[4,768,768]{2,1,0:T(8,128)(2,1)}) custom-call(s32[8]{0:T(128)S(1)} %xor_multiply_fusion.place_ref, s32[4]{0:T(128)S(1)} %iota_xor_fusion.order_ref, bf16[2048,768]{1,0:T(8,128)(2,1)} %fusion.2.a1_ref, ...), custom_call_target="tpu_custom_call" | custom-call | flops 10000000000 | bytes 1048576 | tf_op jit(solution)/shard_map/attn_own/pallas_call | solution.py:378
  44.9 5.2 %collective-permute-done.4.rest_4_ = bf16[3,96,768]{2,1,0:T(8,128)(2,1)S(1)} collective-permute-done((bf16[3,96,768]{2,1,0:T(8,128)(2,1)S(1)}, bf16[3,96,768]{2,1,0:T(8,128)(2,1)S(1)}, u32[]{:S(2)}, u32[]{:S(2)}) %collective-permute-start.4) | collective-permute-done | bytes 442400 | tf_op jit(solution)/shard_map/ppermute | solution.py:1193
  51.5 2.7 others_of.1
  58.5 1.6 collective-permute-start.10
  60.1 1.5 collective-permute-start.11
  62.1 32.4 %attn_far.1 = (bf16[4,576,512]{2,1,0:T(8,128)(2,1)}, f32[4,3,512]{2,1,0:T(4,128)S(1)}, bf16[4,4,192,512]{3,2,1,0:T(8,128)(2,1)}, bf16[4,768,768]{2,1,0:T(8,128)(2,1)}) custom-call(s32[8]{0:T(128)S(1)} %xor_multiply_fusion.place_ref, s32[4]{0:T(128)S(1)} %iota_xor_fusion.order_ref, ...), custom_call_target="tpu_custom_call", output_to_operand_aliasing={{0}: (13, {}), {1}: (14, {}), {2}: (15, {}), {3}: (16, {})} | custom-call | flops 30000001024 | bytes 1048576 | tf_op jit(solution)/shard_map/attn_far/pallas_call | solution.py:378
  95.6 13.5 %ffn_own.1 = (bf16[2048,768]{1,0:T(8,128)(2,1)}, bf16[2048,768]{1,0:T(8,128)(2,1)}, bf16[2048,768]{1,0:T(8,128)(2,1)}) custom-call(bf16[2048,768]{1,0:T(8,128)(2,1)} %refs_16_.1, bf16[4,4,192,512]{3,2,1,0:T(8,128)(2,1)} %get-tuple-element.81.ctx_ref.refs_23_, bf16[4,768,768]{2,1,0:T(8,128)(2,1)} %get-tuple-element.82.wo_ref.refs_21_, ...), custom_call_target="tpu_custom_call" | custom-call | flops 7247757312 | bytes 16777216 | tf_op jit(solution)/shard_map/ffn_own/pallas_call | solution.py:440
  110.0 11.5 %ffn_first.1 = (bf16[2048,768]{1,0:T(8,128)(2,1)}, bf16[512,768]{1,0:T(8,128)(2,1)}, f32[8,768]{1,0:T(8,128)S(1)}, bf16[3,768,768]{2,1,0:T(8,128)(2,1)}, bf16[3,768,768]{2,1,0:T(8,128)(2,1)}) custom-call(s32[8]{0:T(128)S(1)} %xor_multiply_fusion.place_ref, s32[4]{0:T(128)S(1)} %iota_xor_fusion.order_ref, ...), custom_call_target="tpu_custom_call" | custom-call | flops 3623878656 | bytes 16777216 | tf_op jit(solution)/shard_map/ffn_first/pallas_call | solution.py:532
  121.5 3.1 %collective-permute-start.17 = (bf16[8,768]{1,0:T(8,128)(2,1)S(1)}, bf16[8,768]{1,0:T(8,128)(2,1)S(1)}, u32[]{:S(2)}, u32[]{:S(2)}) collective-permute-start(bf16[8,768]{1,0:T(8,128)(2,1)S(1)} %get-tuple-element.174), channel_id=1, source_target_pairs={{0,1},{1,0},{2,3},{3,2},{4,5},{5,4},{6,7},{7,6},{8,9},{9,8},{10,11... | collective-permute-start | bytes 36872 | tf_op jit(solution)/shard_map/ppermute | solution.py:1196
  124.6 3.0 %collective-permute-start.18 = (bf16[8,768]{1,0:T(8,128)(2,1)S(1)}, bf16[8,768]{1,0:T(8,128)(2,1)S(1)}, u32[]{:S(2)}, u32[]{:S(2)}) collective-permute-start(bf16[8,768]{1,0:T(8,128)(2,1)S(1)} %get-tuple-element.174), channel_id=1, source_target_pairs={{0,2},{1,3},{2,0},{3,1},{4,6},{5,7},{6,4},{7,5},{8,10},{9,11},{10,... | collective-permute-start | bytes 36872 | tf_op jit(solution)/shard_map/ppermute | solution.py:1196
  129.3 3.8 %collective-permute-done.19 = bf16[8,768]{1,0:T(8,128)(2,1)S(1)} collective-permute-done((bf16[8,768]{1,0:T(8,128)(2,1)S(1)}, bf16[8,768]{1,0:T(8,128)(2,1)S(1)}, u32[]{:S(2)}, u32[]{:S(2)}) %collective-permute-start.19) | collective-permute-done | bytes 12320 | tf_op jit(solution)/shard_map/ppermute | solution.py:1196
  135.5 1.6 collective-permute-start.22
  139.1 2.2 collective-permute-done.22.refs_2_
  142.7 31.8 %row_back.1 = (f32[32,768]{1,0:T(8,128)S(1)}, f32[96,768]{1,0:T(8,128)}, f32[1,768]{1,0:T(1,128)S(1)}, f32[1,768]{1,0:T(1,128)S(1)}, bf16[512,768]{1,0:T(8,128)(...) custom-call(s32[33]{0:T(128)S(1)} %pad_add_fusion.1.at_ref, ...), custom_call_target="tpu_custom_call" | custom-call | flops 30000001024 | bytes 16777216 | tf_op jit(solution)/shard_map/row_back/pallas_call | solution.py:857
  177.3 9.1 %attn_weights.1 = (bf16[4,4,112,768]{3,2,1,0:T(8,128)(2,1)}, bf16[4,4,112,768]{3,2,1,0:T(8,128)(2,1)}) custom-call(s32[6]{0:T(128)S(1)} %pad_add_fusion.place_ref, bf16[2048,768]{1,0:T(8,128)(2,1)} %fusion.2.a1_ref, bf16[512,768]{1,0:T(8,128)(2,1)S(1)} %get-tuple-element.98.dattn_ref, bf16[4,576,512]{2,1,0:T(8,128)(2,1)} %get-tuple-element.99.dqkv_ref, ...), custom_call_target="tpu_custom_call" | custom-call | flops 1000000 | bytes 1000000 | tf_op jit(solution)/shard_map/attn_weights/pallas_call | solution.py:1001
  186.4 5.3 %collective-permute-done.24 = bf16[4,4,112,768]{3,2,1,0:T(8,128)(2,1)S(1)} collective-permute-done((bf16[4,4,112,768]{3,2,1,0:T(8,128)(2,1)}, bf16[4,4,112,768]{3,2,1,0:T(8,128)(2,1)S(1)}, u32[]{:S(2)}, u32[]{:S(2)}) %collective-permute-start.24) | collective-permute-done | bytes 2752544 | tf_op jit(solution)/shard_map/ppermute | solution.py:1193
  191.7 2.7 fusion.17
  196.2 1.8 collective-permute-start.27
  198.0 31.1 %ffn_tail.1 = (bf16[2048,768]{1,0:T(8,128)(2,1)}, bf16[4,2,96,768]{3,2,1,0:T(8,128)(2,1)}, bf16[4,2,96,768]{3,2,1,0:T(8,128)(2,1)}) custom-call(s32[6]{0:T(128)S(1)} %pad_add_fusion.place_ref, s32[4]{0:T(128)S(1)} %iota_xor_fusion.order_ref, bf16[2048,768]{1,0:T(8,128)(2,1)} %get-tuple-element.83.a2_ref.refs_15_, ...), custom_call_target="tpu_custom_call", output_to_operand_aliasing={{0}: (13, {})} | custom-call | flops 1000000 | bytes 1000000 | tf_op jit(solution)/shard_map/ffn_tail/pallas_call | solution.py:1127
  230.9 5.4 %all-gather.6.cloned.1.call-done = bf16[2048,768]{1,0:T(8,128)(2,1)} async-done(((bf16[512,768]{1,0:T(8,128)(2,1)}), bf16[2048,768]{1,0:T(8,128)(2,1)}) %all-gather.6.cloned.1.call-update) | async-done | bytes 3145744 | tf_op jit(solution)/shard_map/all_gather | solution.py:1306
  236.3 2.9 %fusion.18 = (bf16[4,112,768]{2,1,0:T(8,128)(2,1)S(1)}, f32[4,112,768]{2,1,0:T(8,128)}) fusion(bf16[4,112,768]{2,1,0:T(8,128)(2,1)} %copy-done.7, bf16[4,112,768]{2,1,0:T(8,128)(2,1)} %copy-done.6, f32[4,112,768]{2,1,0:T(8,128)S(1)} %get-tuple-element.113, bf16[4,112,768]{2,1,0:T(8,128)(2,1)S(1)} %collective-permute-done.25), kind=kLoop, calls=%fused_computation.66 | loop fusion | flops 2752512 | bytes 5505024 | tf_op jit(solution)/shard_map/convert.2
  241.1 3.1 %collective-permute-start.31 = (bf16[112,768]{1,0:T(8,128)(2,1)S(1)}, bf16[112,768]{1,0:T(8,128)(2,1)S(1)}, u32[]{:S(2)}, u32[]{:S(2)}) collective-permute-start(bf16[112,768]{1,0:T(8,128)(2,1)S(1)} %get-tuple-element.180), channel_id=1, source_target_pairs={{0,3},{1,2},{2,1},{3,0},{4,7},{5,6},{6,5},{7,4},{8,11},{9,10},{10,... | collective-permute-start | bytes 516104 | tf_op jit(solution)/shard_map/ppermute | solution.py:1196
  245.6 3.7 %all-to-all-start = ((bf16[4,2,96,768]{3,2,1,0:T(8,128)(2,1)}), bf16[4,2,96,768]{3,2,1,0:T(8,128)(2,1)S(1)}, u32[]{:S(2)}, u32[]{:S(2)}) async-start(bf16[4,2,96,768]{3,2,1,0:T(8,128)(2,1)} %fusion.14), calls=%async_computation | async-start | bytes 2359296 | tf_op jit(solution)/shard_map/all_to_all | solution.py:1362
  249.8 5.1 %convert_element_type.158 = f32[2048,768]{1,0:T(8,128)} convert(bf16[2048,768]{1,0:T(8,128)(2,1)} %all-gather.6.cloned.1.call-done) | non-fusion elementwise | flops 1572864 | bytes 9437184 | tf_op jit(solution)/shard_map/convert_element_type | solution.py:1386
  259.3 4.3 %all-to-all-done = bf16[4,2,96,768]{3,2,1,0:T(8,128)(2,1)S(1)} async-done(((bf16[4,2,96,768]{3,2,1,0:T(8,128)(2,1)}), bf16[4,2,96,768]{3,2,1,0:T(8,128)(2,1)S(1)}, u32[]{:S(2)}, u32[]{:S(2)}) %all-to-all-start) | async-done | bytes 1179680 | tf_op jit(solution)/shard_map/all_to_all | solution.py:1362
  (163 shorter events, 37.4 us)
Async XLA Ops:
  7.2 44.3 %all-gather.8.cloned.1.call-start = ((), (), s32[]{:S(2)}) async-start(), calls=%async_computation.2 | async-start | bytes 1474560 | tf_op jit(solution)/shard_map/all_gather | solution.py:1226
  11.3 14.7 %collective-permute-start = (bf16[112,768]{1,0:T(8,128)(2,1)S(1)}, bf16[112,768]{1,0:T(8,128)(2,1)S(1)}, u32[]{:S(2)}, u32[]{:S(2)}) collective-permute-start(bf16[112,768]{1,0:T(8,128)(2,1)S(1)} %get-tuple-element.66), channel_id=1, source_target_pairs={{0,1},{1,0},{2,3},{3,2},{4,5},{5,4},{6,7},{7,6},{8,9},{9,8},{10,11... | collective-permute-start | bytes 516104 | tf_op jit(solution)/shard_map/ppermute | solution.py:1196
  14.3 15.6 %collective-permute-start.1 = (bf16[112,768]{1,0:T(8,128)(2,1)S(1)}, bf16[112,768]{1,0:T(8,128)(2,1)S(1)}, u32[]{:S(2)}, u32[]{:S(2)}) collective-permute-start(bf16[112,768]{1,0:T(8,128)(2,1)S(1)} %get-tuple-element.66), channel_id=1, source_target_pairs={{0,2},{1,3},{2,0},{3,1},{4,6},{5,7},{6,4},{7,5},{8,10},{9,11},{10,... | collective-permute-start | bytes 516104 | tf_op jit(solution)/shard_map/ppermute | solution.py:1196
  16.9 13.0 %collective-permute-start.2 = (bf16[112,768]{1,0:T(8,128)(2,1)S(1)}, bf16[112,768]{1,0:T(8,128)(2,1)S(1)}, u32[]{:S(2)}, u32[]{:S(2)}) collective-permute-start(bf16[112,768]{1,0:T(8,128)(2,1)S(1)} %get-tuple-element.66), channel_id=1, source_target_pairs={{0,3},{1,2},{2,1},{3,0},{4,7},{5,6},{6,5},{7,4},{8,11},{9,10},{10,... | collective-permute-start | bytes 516104 | tf_op jit(solution)/shard_map/ppermute | solution.py:1196
  18.6 91.4 %all-gather.10.cloned.1.call-start = ((), (), s32[]{:S(2)}) async-start(), calls=%async_computation.3 | async-start | bytes 3981312 | tf_op jit(solution)/shard_map/all_gather | solution.py:1244
  29.9 15.0 %collective-permute-start.3 = (bf16[3,96,768]{2,1,0:T(8,128)(2,1)S(1)}, bf16[3,96,768]{2,1,0:T(8,128)(2,1)S(1)}, u32[]{:S(2)}, u32[]{:S(2)}) collective-permute-start(bf16[3,96,768]{2,1,0:T(8,128)(2,1)S(1)} %get-tuple-element.77.rest_0_), channel_id=1, source_target_pairs={{0,8},{4,12},{8,0},{12,4},{16,24},{20,28},{24,16},{28,20},{1,9},{5... | collective-permute-start | bytes 1327112 | tf_op jit(solution)/shard_map/ppermute | solution.py:1193
  31.5 18.6 %collective-permute-start.4 = (bf16[3,96,768]{2,1,0:T(8,128)(2,1)S(1)}, bf16[3,96,768]{2,1,0:T(8,128)(2,1)S(1)}, u32[]{:S(2)}, u32[]{:S(2)}) collective-permute-start(bf16[3,96,768]{2,1,0:T(8,128)(2,1)S(1)} %get-tuple-element.77.rest_0_), channel_id=1, source_target_pairs={{0,16},{4,20},{8,24},{12,28},{16,0},{20,4},{24,8},{28,12},{1,17},{... | collective-permute-start | bytes 1327112 | tf_op jit(solution)/shard_map/ppermute | solution.py:1193
  33.0 17.1 %collective-permute-start.5 = (bf16[3,96,768]{2,1,0:T(8,128)(2,1)S(1)}, bf16[3,96,768]{2,1,0:T(8,128)(2,1)}, u32[]{:S(2)}, u32[]{:S(2)}) collective-permute-start(bf16[3,96,768]{2,1,0:T(8,128)(2,1)S(1)} %get-tuple-element.77.rest_0_), channel_id=1, source_target_pairs={{0,24},{4,28},{8,16},{12,20},{16,8},{20,12},{24,0},{28,4},{1,25},{... | collective-permute-start | bytes 1327112 | tf_op jit(solution)/shard_map/ppermute | solution.py:1193
  54.2 182.1 %all-gather.6.cloned.1.call-start = ((), (), s32[]{:S(2)}) async-start(), calls=%async_computation.1 | async-start | bytes 3932160 | tf_op jit(solution)/shard_map/all_gather | solution.py:1306
  55.3 3.2 %collective-permute-start.8 = (bf16[3,96,768]{2,1,0:T(8,128)(2,1)S(1)}, bf16[3,96,768]{2,1,0:T(8,128)(2,1)S(1)}, u32[]{:S(2)}, u32[]{:S(2)}) collective-permute-start(bf16[3,96,768]{2,1,0:T(8,128)(2,1)S(1)} %collective-permute-done.4.rest_4_), channel_id=1, source_target_pairs={{0,4},{4,0},{8,12},{12,8},{16,20},{20,16},{24,28},{28,24},{1,5},{5... | collective-permute-start | bytes 1327112 | tf_op jit(solution)/shard_map/ppermute | solution.py:1193
  58.5 36.0 %collective-permute-start.10 = (bf16[3,96,768]{2,1,0:T(8,128)(2,1)S(1)}, bf16[3,96,768]{2,1,0:T(8,128)(2,1)S(1)}, u32[]{:S(2)}, u32[]{:S(2)}) collective-permute-start(bf16[3,96,768]{2,1,0:T(8,128)(2,1)S(1)} %get-tuple-element.88.rest_0_), channel_id=1, source_target_pairs={{0,8},{4,12},{8,0},{12,4},{16,24},{20,28},{24,16},{28,20},{1,9},{5... | collective-permute-start | bytes 1327112 | tf_op jit(solution)/shard_map/ppermute | solution.py:1193
  60.1 34.5 %collective-permute-start.11 = (bf16[3,96,768]{2,1,0:T(8,128)(2,1)S(1)}, bf16[3,96,768]{2,1,0:T(8,128)(2,1)S(1)}, u32[]{:S(2)}, u32[]{:S(2)}) collective-permute-start(bf16[3,96,768]{2,1,0:T(8,128)(2,1)S(1)} %get-tuple-element.88.rest_0_), channel_id=1, source_target_pairs={{0,16},{4,20},{8,24},{12,28},{16,0},{20,4},{24,8},{28,12},{1,17},{... | collective-permute-start | bytes 1327112 | tf_op jit(solution)/shard_map/ppermute | solution.py:1193
  61.6 33.0 %collective-permute-start.12 = (bf16[3,96,768]{2,1,0:T(8,128)(2,1)S(1)}, bf16[3,96,768]{2,1,0:T(8,128)(2,1)S(1)}, u32[]{:S(2)}, u32[]{:S(2)}) collective-permute-start(bf16[3,96,768]{2,1,0:T(8,128)(2,1)S(1)} %get-tuple-element.88.rest_0_), channel_id=1, source_target_pairs={{0,24},{4,28},{8,16},{12,20},{16,8},{20,12},{24,0},{28,4},{1,25},{... | collective-permute-start | bytes 1327112 | tf_op jit(solution)/shard_map/ppermute | solution.py:1193
  94.6 14.6 %collective-permute-start.13 = (bf16[3,96,768]{2,1,0:T(8,128)(2,1)S(1)}, bf16[3,96,768]{2,1,0:T(8,128)(2,1)S(1)}, u32[]{:S(2)}, u32[]{:S(2)}) collective-permute-start(bf16[3,96,768]{2,1,0:T(8,128)(2,1)S(1)} %get-tuple-element.88.rest_0_), channel_id=1, source_target_pairs={{0,4},{4,0},{8,12},{12,8},{16,20},{20,16},{24,28},{28,24},{1,5},{5... | collective-permute-start | bytes 1327112 | tf_op jit(solution)/shard_map/ppermute | solution.py:1193
  94.6 14.6 %collective-permute-start.14 = (bf16[3,96,768]{2,1,0:T(8,128)(2,1)S(1)}, bf16[3,96,768]{2,1,0:T(8,128)(2,1)S(1)}, u32[]{:S(2)}, u32[]{:S(2)}) collective-permute-start(bf16[3,96,768]{2,1,0:T(8,128)(2,1)S(1)} %collective-permute-done.10.rest_2_), channel_id=1, source_target_pairs={{0,4},{4,0},{8,12},{12,8},{16,20},{20,16},{24,28},{28,24},{1,5},{5... | collective-permute-start | bytes 1327112 | tf_op jit(solution)/shard_map/ppermute | solution.py:1193
  95.1 14.1 %collective-permute-start.15 = (bf16[3,96,768]{2,1,0:T(8,128)(2,1)S(1)}, bf16[3,96,768]{2,1,0:T(8,128)(2,1)S(1)}, u32[]{:S(2)}, u32[]{:S(2)}) collective-permute-start(bf16[3,96,768]{2,1,0:T(8,128)(2,1)S(1)} %collective-permute-done.11.rest_4_), channel_id=1, source_target_pairs={{0,4},{4,0},{8,12},{12,8},{16,20},{20,16},{24,28},{28,24},{1,5},{5... | collective-permute-start | bytes 1327112 | tf_op jit(solution)/shard_map/ppermute | solution.py:1193
  95.2 14.8 %collective-permute-start.16 = (bf16[3,96,768]{2,1,0:T(8,128)(2,1)S(1)}, bf16[3,96,768]{2,1,0:T(8,128)(2,1)}, u32[]{:S(2)}, u32[]{:S(2)}) collective-permute-start(bf16[3,96,768]{2,1,0:T(8,128)(2,1)S(1)} %collective-permute-done.12.rest_6_), channel_id=1, source_target_pairs={{0,4},{4,0},{8,12},{12,8},{16,20},{20,16},{24,28},{28,24},{1,5},{5... | collective-permute-start | bytes 1327112 | tf_op jit(solution)/shard_map/ppermute | solution.py:1193
  121.5 7.8 %collective-permute-start.17 = (bf16[8,768]{1,0:T(8,128)(2,1)S(1)}, bf16[8,768]{1,0:T(8,128)(2,1)S(1)}, u32[]{:S(2)}, u32[]{:S(2)}) collective-permute-start(bf16[8,768]{1,0:T(8,128)(2,1)S(1)} %get-tuple-element.174), channel_id=1, source_target_pairs={{0,1},{1,0},{2,3},{3,2},{4,5},{5,4},{6,7},{7,6},{8,9},{9,8},{10,11... | collective-permute-start | bytes 36872 | tf_op jit(solution)/shard_map/ppermute | solution.py:1196
  124.6 4.7 %collective-permute-start.18 = (bf16[8,768]{1,0:T(8,128)(2,1)S(1)}, bf16[8,768]{1,0:T(8,128)(2,1)S(1)}, u32[]{:S(2)}, u32[]{:S(2)}) collective-permute-start(bf16[8,768]{1,0:T(8,128)(2,1)S(1)} %get-tuple-element.174), channel_id=1, source_target_pairs={{0,2},{1,3},{2,0},{3,1},{4,6},{5,7},{6,4},{7,5},{8,10},{9,11},{10,... | collective-permute-start | bytes 36872 | tf_op jit(solution)/shard_map/ppermute | solution.py:1196
  127.6 5.5 %collective-permute-start.19 = (bf16[8,768]{1,0:T(8,128)(2,1)S(1)}, bf16[8,768]{1,0:T(8,128)(2,1)S(1)}, u32[]{:S(2)}, u32[]{:S(2)}) collective-permute-start(bf16[8,768]{1,0:T(8,128)(2,1)S(1)} %get-tuple-element.174), channel_id=1, source_target_pairs={{0,3},{1,2},{2,1},{3,0},{4,7},{5,6},{6,5},{7,4},{8,11},{9,10},{10,... | collective-permute-start | bytes 36872 | tf_op jit(solution)/shard_map/ppermute | solution.py:1196
  134.3 4.9 %collective-permute-start.21 = (bf16[64,768]{1,0:T(8,128)(2,1)S(1)}, bf16[64,768]{1,0:T(8,128)(2,1)S(1)}, u32[]{:S(2)}, u32[]{:S(2)}) collective-permute-start(bf16[64,768]{1,0:T(8,128)(2,1)S(1)} %constant_dynamic-update-slice_fusion.refs_0_), channel_id=1, source_target_pairs={{0,8},{4,12},{8,0},{12,4},{16,24},{20,28},{24,16},{28,20},{1,9},{5... | collective-permute-start | bytes 294920 | tf_op jit(solution)/shard_map/ppermute | solution.py:1193
  135.5 5.8 %collective-permute-start.22 = (bf16[64,768]{1,0:T(8,128)(2,1)S(1)}, bf16[64,768]{1,0:T(8,128)(2,1)S(1)}, u32[]{:S(2)}, u32[]{:S(2)}) collective-permute-start(bf16[64,768]{1,0:T(8,128)(2,1)S(1)} %constant_dynamic-update-slice_fusion.refs_0_), channel_id=1, source_target_pairs={{0,16},{4,20},{8,24},{12,28},{16,0},{20,4},{24,8},{28,12},{1,17},{... | collective-permute-start | bytes 294920 | tf_op jit(solution)/shard_map/ppermute | solution.py:1193
  137.1 5.5 %collective-permute-start.23 = (bf16[64,768]{1,0:T(8,128)(2,1)S(1)}, bf16[64,768]{1,0:T(8,128)(2,1)S(1)}, u32[]{:S(2)}, u32[]{:S(2)}) collective-permute-start(bf16[64,768]{1,0:T(8,128)(2,1)S(1)} %constant_dynamic-update-slice_fusion.refs_0_), channel_id=1, source_target_pairs={{0,24},{4,28},{8,16},{12,20},{16,8},{20,12},{24,0},{28,4},{1,25},{... | collective-permute-start | bytes 294920 | tf_op jit(solution)/shard_map/ppermute | solution.py:1193
  186.4 5.3 %collective-permute-start.24 = (bf16[4,4,112,768]{3,2,1,0:T(8,128)(2,1)}, bf16[4,4,112,768]{3,2,1,0:T(8,128)(2,1)S(1)}, u32[]{:S(2)}, u32[]{:S(2)}) collective-permute-start(bf16[4,4,112,768]{3,2,1,0:T(8,128)(2,1)} %get-tuple-element.104), channel_id=1, source_target_pairs={{0,4},{4,0},{8,12},{12,8},{16,20},{20,16},{24,28},{28,24},{1,5},{5... | collective-permute-start | bytes 8257544 | tf_op jit(solution)/shard_map/ppermute | solution.py:1193
  194.4 34.7 %collective-permute-start.25 = (bf16[4,112,768]{2,1,0:T(8,128)(2,1)S(1)}, bf16[4,112,768]{2,1,0:T(8,128)(2,1)S(1)}, u32[]{:S(2)}, u32[]{:S(2)}) collective-permute-start(bf16[4,112,768]{2,1,0:T(8,128)(2,1)S(1)} %get-tuple-element.176), channel_id=1, source_target_pairs={{0,8},{4,12},{8,0},{12,4},{16,24},{20,28},{24,16},{28,20},{1,9},{5... | collective-permute-start | bytes 2064392 | tf_op jit(solution)/shard_map/ppermute | solution.py:1193
  195.3 33.8 %collective-permute-start.26 = (bf16[4,112,768]{2,1,0:T(8,128)(2,1)S(1)}, bf16[4,112,768]{2,1,0:T(8,128)(2,1)S(1)}, u32[]{:S(2)}, u32[]{:S(2)}) collective-permute-start(bf16[4,112,768]{2,1,0:T(8,128)(2,1)S(1)} %get-tuple-element.177), channel_id=1, source_target_pairs={{0,16},{4,20},{8,24},{12,28},{16,0},{20,4},{24,8},{28,12},{1,17},{... | collective-permute-start | bytes 2064392 | tf_op jit(solution)/shard_map/ppermute | solution.py:1193
  196.2 33.0 %collective-permute-start.27 = (bf16[4,112,768]{2,1,0:T(8,128)(2,1)S(1)}, bf16[4,112,768]{2,1,0:T(8,128)(2,1)S(1)}, u32[]{:S(2)}, u32[]{:S(2)}) collective-permute-start(bf16[4,112,768]{2,1,0:T(8,128)(2,1)S(1)} %get-tuple-element.175), channel_id=1, source_target_pairs={{0,24},{4,28},{8,16},{12,20},{16,8},{20,12},{24,0},{28,4},{1,25},{... | collective-permute-start | bytes 2064392 | tf_op jit(solution)/shard_map/ppermute | solution.py:1193
  230.9 13.4 %collective-permute-start.28 = (bf16[4,2,96,768]{3,2,1,0:T(8,128)(2,1)}, bf16[4,2,96,768]{3,2,1,0:T(8,128)(2,1)S(1)}, u32[]{:S(2)}, u32[]{:S(2)}) collective-permute-start(bf16[4,2,96,768]{3,2,1,0:T(8,128)(2,1)} %get-tuple-element.112), channel_id=1, source_target_pairs={{0,4},{4,0},{8,12},{12,8},{16,20},{20,16},{24,28},{28,24},{1,5},{5... | collective-permute-start | bytes 3538952 | tf_op jit(solution)/shard_map/ppermute | solution.py:1193
  239.9 15.1 %collective-permute-start.29 = (bf16[112,768]{1,0:T(8,128)(2,1)}, bf16[112,768]{1,0:T(8,128)(2,1)S(1)}, u32[]{:S(2)}, u32[]{:S(2)}) collective-permute-start(bf16[112,768]{1,0:T(8,128)(2,1)} %get-tuple-element.179), channel_id=1, source_target_pairs={{0,1},{1,0},{2,3},{3,2},{4,5},{5,4},{6,7},{7,6},{8,9},{9,8},{10,11... | collective-permute-start | bytes 516104 | tf_op jit(solution)/shard_map/ppermute | solution.py:1196
  239.9 15.5 %collective-permute-start.30 = (bf16[112,768]{1,0:T(8,128)(2,1)S(1)}, bf16[112,768]{1,0:T(8,128)(2,1)S(1)}, u32[]{:S(2)}, u32[]{:S(2)}) collective-permute-start(bf16[112,768]{1,0:T(8,128)(2,1)S(1)} %get-tuple-element.181), channel_id=1, source_target_pairs={{0,2},{1,3},{2,0},{3,1},{4,6},{5,7},{6,4},{7,5},{8,10},{9,11},{10,... | collective-permute-start | bytes 516104 | tf_op jit(solution)/shard_map/ppermute | solution.py:1196
  241.1 14.3 %collective-permute-start.31 = (bf16[112,768]{1,0:T(8,128)(2,1)S(1)}, bf16[112,768]{1,0:T(8,128)(2,1)S(1)}, u32[]{:S(2)}, u32[]{:S(2)}) collective-permute-start(bf16[112,768]{1,0:T(8,128)(2,1)S(1)} %get-tuple-element.180), channel_id=1, source_target_pairs={{0,3},{1,2},{2,1},{3,0},{4,7},{5,6},{6,5},{7,4},{8,11},{9,10},{10,... | collective-permute-start | bytes 516104 | tf_op jit(solution)/shard_map/ppermute | solution.py:1196
  245.6 17.9 %all-to-all-start = ((bf16[4,2,96,768]{3,2,1,0:T(8,128)(2,1)}), bf16[4,2,96,768]{3,2,1,0:T(8,128)(2,1)S(1)}, u32[]{:S(2)}, u32[]{:S(2)}) async-start(bf16[4,2,96,768]{3,2,1,0:T(8,128)(2,1)} %fusion.14), calls=%async_computation | async-start | bytes 2359296 | tf_op jit(solution)/shard_map/all_to_all | solution.py:1362
  (27 other events, 148.6 us)
Sparse Core Ops, SparseCore 0:
  18.7 32.7 all-gather.7
  54.3 49.9 all-gather.9
  174.9 61.2 all-gather.5
